TPU v7x, 512 devices: a whole 4x4x16 slice. The times are simulated.
512 devices in a mesh: blk: 32 (over z, core), bond: 16 (over y, x).
Axes of the slice: x: 4, y: 4, z: 16, core: 2. Of those that a mesh axis runs over, the one named last changes fastest.
Arguments:
- iso: bfloat16 [32, 256, 256, 256], P('blk', None, 'bond'), may hold values from -0.03125 to 0.03125
- edge_left: bfloat16 [32, 256, 256], P('blk'), may hold values from -0.375 to 0.375
- edge_right: bfloat16 [32, 256, 256], P('blk'), may hold values from -0.375 to 0.375
- coupling: float32 [32, 256, 256], P('blk'), may hold values from -0.25 to 0.25
Outputs:
- iso_out: bfloat16 [32, 256, 256, 256], P('blk', None, 'bond')
- top_env: float32 [32, 256, 256], P('blk')
All inputs are finite; a program needn't handle non-finite values.
Results may differ from a plain program's by a relative error of at most 0.00105.
The roundings to bfloat16 on the way count: a program that leaves them out, or rounds other values in their place, can miss the bound.
Values may be sent and summed in bfloat16 or wider, within the bound.
No kernel may reach another device: no remote copies, remote signals or barrier semaphores. Data moves between devices by JAX's collectives and lax.ppermute only.
A program may use at most 64 MiB of HBM per device.

v0:
```python
import jax
import jax.numpy as jnp
from jax import lax
from jax.sharding import PartitionSpec as P

bf16 = jnp.bfloat16
f32 = jnp.float32


def split(x):
    rounded = lax.reduce_precision(x, 8, 7)
    return rounded.astype(bf16), (x - rounded).astype(bf16)


def mm(a, b, dims=((1,), (0,))):
    return lax.dot_general(a, b, (dims, ((), ())), preferred_element_type=f32)


def mm3(a, b, dims=((1,), (0,))):
    ah, al = split(a)
    bh, bl = split(b)
    return mm(ah, bh, dims) + (mm(ah, bl, dims) + mm(al, bh, dims))


NT = ((1,), (1,))
TN = ((0,), (0,))


def sandwich(c, e):
    return mm3(mm3(c, e), c, NT)


def exchange(x, axis, groups=None):
    return lax.all_to_all(x, axis, 0, 0, axis_index_groups=groups, tiled=True)


def permuted(x, axis, route):
    return lax.ppermute(x, axis, [(i, route(i)) for i in range(lax.axis_size(axis))])


def body(iso, edge_left, edge_right, coupling):
    iso = iso[0]
    couple = coupling[0]
    size = iso.shape[0]
    width = lax.axis_size("bond")
    rows = size // width
    s = lax.axis_index("blk")
    j = lax.axis_index("bond")
    z = s // 2
    flat = iso.reshape(-1, size)

    couple_1 = permuted(couple, "blk", lambda i: i ^ 2)
    couple_2 = permuted(couple, "blk", lambda i: i ^ 8)

    operators = jnp.concatenate([edge_left[0], edge_right[0]], axis=0)
    mapped = jnp.einsum("xa,abp->xbp", operators, iso, preferred_element_type=f32)
    hi, lo = split(mapped)

    def contract(part):
        part = part.reshape(2, -1, size)
        return jnp.einsum("rp,krq->kpq", flat, part, preferred_element_type=f32)

    partial = contract(hi) + contract(lo)
    blocks = partial.reshape(2, width, rows, size).transpose(1, 0, 2, 3)
    share = exchange(blocks, "bond").sum(axis=0).astype(bf16)
    gathered = exchange(jnp.broadcast_to(share[None], (width, *share.shape)), "bond")
    gathered = gathered.transpose(1, 0, 2, 3).reshape(2, size, size)

    near = permuted(gathered, "blk", lambda i: i ^ 1)
    odd = s % 2 == 1
    outward = jnp.where(odd, gathered[1], gathered[0])
    far = permuted(outward, "blk", lambda i: (i + 1) % 32 if i % 2 else (i - 1) % 32)
    from_left = jnp.where(odd, near[1], far)
    from_right = jnp.where(odd, far, near[0])
    mix = edge_left[0].astype(f32) + from_left.astype(f32) + from_right.astype(f32)
    mix = mix.astype(bf16)

    env = gathered[0].astype(f32) + gathered[1].astype(f32)
    env_near = near[0].astype(f32) + near[1].astype(f32)
    env = 0.5 * (env + sandwich(couple, env_near))

    moved = jnp.einsum("xa,abp->xbp", mix, iso, preferred_element_type=f32).reshape(-1, size)
    moved_hi, moved_lo = split(moved)
    part_q = mm(flat, moved_hi, TN) + mm(flat, moved_lo, TN)
    cross = mm(moved_hi, moved_lo, TN)
    part_r = mm(moved_hi, moved_hi, TN) + cross + cross.T
    part_n = mm(flat, flat, TN)
    row = lax.broadcasted_iota(jnp.int32, (size, size), 0)
    col = lax.broadcasted_iota(jnp.int32, (size, size), 1)
    part_s = jnp.where(row < col, part_n, part_r)
    diag_n = jnp.sum(jnp.where(row == col, part_n, 0.0), axis=0)
    diag_r = jnp.sum(jnp.where(row == col, part_r, 0.0), axis=0)
    nh, nl = split(diag_n)
    _, rl = split(diag_r)
    extra = jnp.concatenate(
        [jnp.stack([nh, nl, rl]), jnp.zeros((rows - 3, size), bf16)], axis=0
    )

    def slices(env, foreign, me):
        own = lax.dynamic_slice_in_dim(env, j * rows, rows, 0)
        left = lax.dynamic_slice_in_dim(foreign, j * rows, rows, 0)
        crossed = mm3(mm3(left, env), foreign, NT)
        which = lax.broadcasted_iota(jnp.int32, (4, 1, 1), 0) ^ me
        return jnp.where(which == 0, 0.0, jnp.where(which == 3, crossed[None], own[None]))

    quads = [[(zq * 4 + zl) * 2 + c for zl in range(4)] for zq in range(4) for c in range(2)]
    strides = [[(zh * 4 + zl) * 2 + c for zh in range(4)] for zl in range(4) for c in range(2)]

    incoming = exchange(slices(env, couple_1, z % 4), "blk", quads).sum(axis=0)
    fh, fl = split(incoming)
    spread = jnp.broadcast_to(
        jnp.stack([fh, fl, extra])[None], (width, 3, rows, size)
    )
    shares = jnp.stack([part_q, part_s]).astype(bf16).reshape(2, width, rows, size).transpose(1, 0, 2, 3)
    got = exchange(jnp.concatenate([spread, shares], axis=1), "bond")
    force = (got[:, 0].astype(f32) + got[:, 1].astype(f32)).reshape(size, size)
    extras = got[:, 2].astype(f32).sum(axis=0)
    sums = got[:, 3:].astype(f32).sum(axis=0).astype(bf16)
    env = 0.25 * (env + sandwich(couple, force))

    incoming = exchange(slices(env, couple_2, z // 4), "blk", strides).sum(axis=0)
    fh, fl = split(incoming)
    spread = jnp.concatenate([jnp.stack([fh, fl]), sums], axis=0)
    got = exchange(jnp.broadcast_to(spread[None], (width, *spread.shape)), "bond")
    got = got.transpose(1, 0, 2, 3).reshape(4, size, size).astype(f32)
    env = 0.25 * (env + sandwich(couple, got[0] + got[1]))

    full_q, full_s = got[2], got[3]
    lower = jnp.where(row > col, full_s, 0.0)
    upper = jnp.where(row < col, full_s, 0.0)
    full_n = upper + upper.T + jnp.where(row == col, (extras[0] + extras[1])[None, :], 0.0)
    full_r = lower + lower.T + jnp.where(row == col, full_s + extras[2][None, :], 0.0)
    top = lax.reduce_precision(env, 8, 7)
    half = full_q + 0.5 * mm3(full_n, top)
    side = mm3(half, top, TN)
    gram = full_r + side + side.T
    trace = jnp.sum(jnp.where(row == col, gram, 0.0))
    factor = lax.rsqrt(trace + 1e-06)
    g = gram * (factor * factor)
    g2 = mm3(g, g)
    eye = jnp.where(row == col, 1.0, 0.0)
    poly = 2.25 * eye - 2.4375 * g + mm3(g2, 1.6875 * eye - 0.5625 * g + 0.0625 * g2)
    poly = poly * factor
    low = mm3(top, poly)
    ph, pl_ = split(poly)
    lh, ll = split(low)
    out = (mm(moved_hi, ph) + mm(flat, lh)) + (mm(moved_lo, ph) + mm(moved_hi, pl_) + mm(flat, ll))
    return (out.reshape(iso.shape).astype(bf16)[None], env[None])


def solution(mesh):
    placed = (
        P("blk", None, "bond", None),
        P("blk", None, None),
        P("blk", None, None),
        P("blk", None, None),
    )
    return jax.shard_map(
        body,
        mesh=mesh,
        in_specs=placed,
        out_specs=(P("blk", None, "bond", None), P("blk", None, None)),
        check_vma=False,
    )
```

profile of v0, /device:TPU:2, one launch (start us, length us, event | category | flops | bytes accessed | tf_op | source)
XLA Modules:
  0.0 185.5 jit_solution(9628947122284443959)
XLA Ops:
  0.6 1.6 copy-done
  2.2 2.6 %fusion = (bf16[512,16,256]{2,0,1:T(8,128)(2,1)S(1)}, bf16[512,16,256]{2,0,1:T(8,128)(2,1)S(1)}) fusion(bf16[256,16,256]{2,1,0:T(8,128)(2,1)S(1)} %bitcast.220, bf16[256,256]{1,0:T(8,128)(2,1)} %bitcast.249, bf16[256,256]{1,0:T(8,128)(2,1)} %bitcast.245), kind=kOutput, calls=%fused_computation.2 | convolution fusion | flops 1082654720 | bytes 10747904 | tf_op jit(solution)/shard_map/xa,abp->xbp/dot_general | solution.py:56
  4.8 2.4 %copy.91 = bf16[512,16,256]{2,1,0:T(8,128)(2,1)S(1)} copy(bf16[512,16,256]{2,0,1:T(8,128)(2,1)S(1)} %get-tuple-element.5) | data formatting | bytes 8388608 | tf_op jit(solution)/shard_map/convert_element_type | solution.py:12
  7.3 2.4 %copy.93 = bf16[512,16,256]{2,1,0:T(8,128)(2,1)S(1)} copy(bf16[512,16,256]{2,0,1:T(8,128)(2,1)S(1)} %get-tuple-element.4) | data formatting | bytes 8388608 | tf_op jit(solution)/shard_map/convert_element_type | solution.py:12
  11.0 1.3 convolution_add_fusion.1
  13.2 9.3 %all-to-all-start = ((f32[16,2,16,256]{3,2,1,0:T(8,128)}), f32[16,2,16,256]{3,2,1,0:T(8,128)S(1)}, u32[]{:S(2)}, u32[]{:S(2)}) async-start(f32[16,2,16,256]{3,2,1,0:T(8,128)} %bitcast.219), calls=%async_computation | async-start | bytes 1048576 | tf_op jit(solution)/shard_map/all_to_all | solution.py:34
  22.4 2.0 %collective-permute-start.3 = (f32[256,256]{1,0:T(8,128)S(1)}, f32[256,256]{1,0:T(8,128)S(1)}, u32[]{:S(2)}, u32[]{:S(2)}) collective-permute-start(f32[256,256]{1,0:T(8,128)S(1)} %bitcast.228), channel_id=1, source_target_pairs={{0,32},{16,48},{32,0},{48,16},{64,96},{80,112},{96,64},{112,80},{1... | collective-permute-start | bytes 786440 | tf_op jit(solution)/shard_map/ppermute | solution.py:38
  24.6 6.7 %all-to-all-done = f32[16,2,16,256]{3,2,1,0:T(8,128)S(1)} async-done(((f32[16,2,16,256]{3,2,1,0:T(8,128)}), f32[16,2,16,256]{3,2,1,0:T(8,128)S(1)}, u32[]{:S(2)}, u32[]{:S(2)}) %all-to-all-start) | async-done | bytes 524320 | tf_op jit(solution)/shard_map/all_to_all | solution.py:34
  32.0 4.8 %all-to-all-start.1 = ((bf16[16,2,16,256]{3,2,1,0:T(8,128)(2,1)}), bf16[16,2,16,256]{3,2,1,0:T(8,128)(2,1)S(1)}, u32[]{:S(2)}, u32[]{:S(2)}) async-start(bf16[16,2,16,256]{3,2,1,0:T(8,128)(2,1)} %broadcast_in_dim.114), calls=%async_computation.1 | async-start | bytes 524288 | tf_op jit(solution)/shard_map/all_to_all | solution.py:34
  37.1 7.1 %all-to-all-done.1 = bf16[16,2,16,256]{3,2,1,0:T(8,128)(2,1)S(1)} async-done(((bf16[16,2,16,256]{3,2,1,0:T(8,128)(2,1)}), bf16[16,2,16,256]{3,2,1,0:T(8,128)(2,1)S(1)}, u32[]{:S(2)}, u32[]{:S(2)}) %all-to-all-start.1) | async-done | bytes 262176 | tf_op jit(solution)/shard_map/all_to_all | solution.py:34
  44.3 1.9 %collective-permute-start = (bf16[2,256,256]{2,1,0:T(8,128)(2,1)S(1)}, bf16[2,256,256]{2,1,0:T(8,128)(2,1)S(1)}, u32[]{:S(2)}, u32[]{:S(2)}) collective-permute-start(bf16[2,256,256]{2,1,0:T(8,128)(2,1)S(1)} %bitcast.248), channel_id=1, source_target_pairs={{0,16},{16,0},{32,48},{48,32},{64,80},{80,64},{96,112},{112,96},{1... | collective-permute-start | bytes 786440 | tf_op jit(solution)/shard_map/ppermute | solution.py:38
  46.3 11.3 %collective-permute-start.1 = (bf16[256,256]{1,0:T(8,128)(2,1)S(1)}, bf16[256,256]{1,0:T(8,128)(2,1)S(1)}, u32[]{:S(2)}, u32[]{:S(2)}) collective-permute-start(bf16[256,256]{1,0:T(8,128)(2,1)S(1)} %bitcast.250), channel_id=1, source_target_pairs={{0,496},{16,32},{32,16},{48,64},{64,48},{80,96},{96,80},{112,128},... | collective-permute-start | bytes 393224 | tf_op jit(solution)/shard_map/ppermute | solution.py:38
  60.1 3.2 %fusion.6 = (bf16[256,16,256]{2,0,1:T(8,128)(2,1)S(1)}, bf16[256,16,256]{2,0,1:T(8,128)(2,1)S(1)}, f32[256,16,256]{2,0,1:T(8,128)}) fusion(bf16[256,16,256]{2,1,0:T(8,128)(2,1)S(1)} %bitcast.221, bf16[256,256]{1,0:T(8,128)(2,1)S(1)} %collective-permute-done.1, pred[]{:T(512)S(6)} %eq.58, bf16[2,256,256]{2,1,0:T(8,128)(2,1)S(1)} %collective-permute-done, ...), kind=kOutput, calls=%fused_computation.15 | convolution fusion | flops 541589504 | bytes 11010049 | tf_op jit(solution)/shard_map/xa,abp->xbp/dot_general | solution.py:82
  63.3 2.5 %copy.103 = bf16[256,16,256]{2,1,0:T(8,128)(2,1)} copy(bf16[256,16,256]{2,0,1:T(8,128)(2,1)S(1)} %get-tuple-element.9) | data formatting | bytes 4194304 | tf_op jit(solution)/shard_map/convert_element_type | solution.py:12
  65.8 2.6 %copy.104 = bf16[256,16,256]{2,1,0:T(8,128)(2,1)} copy(bf16[256,16,256]{2,0,1:T(8,128)(2,1)S(1)} %get-tuple-element.8) | data formatting | bytes 4194304 | tf_op jit(solution)/shard_map/convert_element_type | solution.py:12
  71.1 3.3 %all-to-all-start.2 = ((f32[4,16,256]{2,1,0:T(8,128)}), f32[4,16,256]{2,1,0:T(8,128)S(1)}, u32[]{:S(2)}, u32[]{:S(2)}) async-start(f32[4,16,256]{2,1,0:T(8,128)} %select_select_fusion.1), calls=%async_computation.2 | async-start | bytes 131072 | tf_op jit(solution)/shard_map/all_to_all | solution.py:34
  74.6 3.0 %select_reduce_fusion.1 = (f32[256]{0:T(256)S(1)}, bf16[256,256]{1,0:T(8,128)(2,1)S(1)}) fusion(f32[256,256]{0,1:T(8,128)S(1)} %copy.102, f32[256,256]{1,0:T(8,128)S(1)} %convolution_bitcast_fusion.8, bf16[256,16,256]{2,0,1:T(8,128)(2,1)} %copy-done.4), kind=kOutput, calls=%fused_computation.159 | convolution fusion | flops 537263872 | bytes 2753536 | tf_op jit(solution)/shard_map/dot_general | solution.py:16
  82.9 5.5 %all-to-all-start.3 = ((bf16[16,5,16,256]{3,2,1,0:T(8,128)(2,1)}), bf16[16,5,16,256]{3,2,1,0:T(8,128)(2,1)}, u32[]{:S(2)}, u32[]{:S(2)}) async-start(bf16[16,5,16,256]{3,2,1,0:T(8,128)(2,1)} %pad_maximum_fusion), calls=%async_computation.3 | async-start | bytes 1310720 | tf_op jit(solution)/shard_map/all_to_all | solution.py:34
  88.3 3.8 %collective-permute-start.2 = (f32[256,256]{1,0:T(8,128)S(1)}, f32[256,256]{1,0:T(8,128)S(1)}, u32[]{:S(2)}, u32[]{:S(2)}) collective-permute-start(f32[256,256]{1,0:T(8,128)S(1)} %bitcast.229), channel_id=1, source_target_pairs={{0,128},{16,144},{32,160},{48,176},{64,192},{80,208},{96,224},{112... | collective-permute-start | bytes 786440 | tf_op jit(solution)/shard_map/ppermute | solution.py:38
  92.2 5.8 %all-to-all-done.3 = bf16[16,5,16,256]{3,2,1,0:T(8,128)(2,1)} async-done(((bf16[16,5,16,256]{3,2,1,0:T(8,128)(2,1)}), bf16[16,5,16,256]{3,2,1,0:T(8,128)(2,1)}, u32[]{:S(2)}, u32[]{:S(2)}) %all-to-all-start.3) | async-done | bytes 655392 | tf_op jit(solution)/shard_map/all_to_all | solution.py:34
  100.5 16.1 %collective-permute-done.2 = f32[256,256]{1,0:T(8,128)S(1)} collective-permute-done((f32[256,256]{1,0:T(8,128)S(1)}, f32[256,256]{1,0:T(8,128)S(1)}, u32[]{:S(2)}, u32[]{:S(2)}) %collective-permute-start.2) | collective-permute-done | bytes 262176 | tf_op jit(solution)/shard_map/ppermute | solution.py:38
  118.3 10.8 %all-to-all-start.4 = ((f32[4,16,256]{2,1,0:T(8,128)}), f32[4,16,256]{2,1,0:T(8,128)S(1)}, u32[]{:S(2)}, u32[]{:S(2)}) async-start(f32[4,16,256]{2,1,0:T(8,128)} %select_select_fusion), calls=%async_computation.4 | async-start | bytes 131072 | tf_op jit(solution)/shard_map/all_to_all | solution.py:34
  129.2 6.6 %copy.98 = f32[256,16,256]{2,1,0:T(8,128)} copy(f32[256,16,256]{2,0,1:T(8,128)} %get-tuple-element.28) | data formatting | bytes 8388608 | tf_op jit(solution)/shard_map/xa,abp->xbp/dot_general | solution.py:82
  136.8 5.4 %all-to-all-done.4 = f32[4,16,256]{2,1,0:T(8,128)S(1)} async-done(((f32[4,16,256]{2,1,0:T(8,128)}), f32[4,16,256]{2,1,0:T(8,128)S(1)}, u32[]{:S(2)}, u32[]{:S(2)}) %all-to-all-start.4) | async-done | bytes 65568 | tf_op jit(solution)/shard_map/all_to_all | solution.py:34
  143.1 7.3 %all-to-all-start.5 = ((bf16[16,4,16,256]{3,2,1,0:T(8,128)(2,1)}), bf16[16,4,16,256]{3,2,1,0:T(8,128)(2,1)S(1)}, u32[]{:S(2)}, u32[]{:S(2)}) async-start(bf16[16,4,16,256]{3,2,1,0:T(8,128)(2,1)} %broadcast_in_dim.128), calls=%async_computation.5 | async-start | bytes 1048576 | tf_op jit(solution)/shard_map/all_to_all | solution.py:34
  150.4 4.8 %fusion.5 = (bf16[4096,256]{1,0:T(8,128)(2,1)}, bf16[4096,256]{1,0:T(8,128)(2,1)}) fusion(f32[256,16,256]{2,1,0:T(8,128)} %copy.98), kind=kLoop, calls=%fused_computation.14 | loop fusion | flops 4194304 | bytes 8388608 | tf_op jit(solution)/shard_map/convert_element_type | solution.py:12
  155.2 3.9 %all-to-all-done.5 = bf16[16,4,16,256]{3,2,1,0:T(8,128)(2,1)S(1)} async-done(((bf16[16,4,16,256]{3,2,1,0:T(8,128)(2,1)}), bf16[16,4,16,256]{3,2,1,0:T(8,128)(2,1)S(1)}, u32[]{:S(2)}, u32[]{:S(2)}) %all-to-all-start.5) | async-done | bytes 524320 | tf_op jit(solution)/shard_map/all_to_all | solution.py:34
  166.6 1.3 reduce-precision_convert_fusion.9
  170.9 1.8 copy.117
  172.7 1.8 copy.112
  174.5 1.9 %select_reduce_fusion = (f32[]{:T(128)}, f32[256,256]{1,0:T(8,128)S(1)}) fusion(f32[256,256]{1,0:T(8,128)} %copy.117, f32[256,256]{1,0:T(8,128)} %fusion.15, f32[256]{0:T(256)S(1)} %bitcast.255, f32[1,16,16,256]{3,2,1,0:T(8,128)S(1)} %copy-done.8, f32[256,256]{1,0:T(8,128)} %copy.112, f32[256,256]{0,1:T(8,128)S(1)} %copy.110), kind=kLoop, calls=%fused_computation.154 | loop fusion | flops 720895 | bytes 1573892 | tf_op jit(solution)/shard_map/reduce_sum | solution.py:137
  183.3 2.2 %fusion.4 = bf16[4096,256]{1,0:T(8,128)(2,1)} fusion(f32[4096,256]{1,0:T(8,128)S(1)} %fusion.3, f32[4096,256]{1,0:T(8,128)S(1)} %convolution_add_fusion, bf16[4096,256]{1,0:T(8,128)(2,1)S(1)} %bitcast.224, f32[256,256]{1,0:T(8,128)S(1)} %fusion.11), kind=kOutput, calls=%fused_computation.13 | convolution fusion | flops 540213248 | bytes 12845056 | tf_op jit(solution)/shard_map/dot_general | solution.py:16
  (127 shorter events, 36.2 us)
Async XLA Ops:
  0.6 1.6 copy-start
  12.3 10.1 %copy-start.2 = (f32[1,256,256]{2,1,0:T(8,128)S(1)}, f32[1,256,256]{2,1,0:T(8,128)}, u32[]{:S(2)}) copy-start(f32[1,256,256]{2,1,0:T(8,128)} %param.7) | copy-start | bytes 786436
  13.2 18.1 %all-to-all-start = ((f32[16,2,16,256]{3,2,1,0:T(8,128)}), f32[16,2,16,256]{3,2,1,0:T(8,128)S(1)}, u32[]{:S(2)}, u32[]{:S(2)}) async-start(f32[16,2,16,256]{3,2,1,0:T(8,128)} %bitcast.219), calls=%async_computation | async-start | bytes 1048576 | tf_op jit(solution)/shard_map/all_to_all | solution.py:34
  22.4 47.0 %collective-permute-start.3 = (f32[256,256]{1,0:T(8,128)S(1)}, f32[256,256]{1,0:T(8,128)S(1)}, u32[]{:S(2)}, u32[]{:S(2)}) collective-permute-start(f32[256,256]{1,0:T(8,128)S(1)} %bitcast.228), channel_id=1, source_target_pairs={{0,32},{16,48},{32,0},{48,16},{64,96},{80,112},{96,64},{112,80},{1... | collective-permute-start | bytes 786440 | tf_op jit(solution)/shard_map/ppermute | solution.py:38
  32.0 12.2 %all-to-all-start.1 = ((bf16[16,2,16,256]{3,2,1,0:T(8,128)(2,1)}), bf16[16,2,16,256]{3,2,1,0:T(8,128)(2,1)S(1)}, u32[]{:S(2)}, u32[]{:S(2)}) async-start(bf16[16,2,16,256]{3,2,1,0:T(8,128)(2,1)} %broadcast_in_dim.114), calls=%async_computation.1 | async-start | bytes 524288 | tf_op jit(solution)/shard_map/all_to_all | solution.py:34
  44.3 13.3 %collective-permute-start = (bf16[2,256,256]{2,1,0:T(8,128)(2,1)S(1)}, bf16[2,256,256]{2,1,0:T(8,128)(2,1)S(1)}, u32[]{:S(2)}, u32[]{:S(2)}) collective-permute-start(bf16[2,256,256]{2,1,0:T(8,128)(2,1)S(1)} %bitcast.248), channel_id=1, source_target_pairs={{0,16},{16,0},{32,48},{48,32},{64,80},{80,64},{96,112},{112,96},{1... | collective-permute-start | bytes 786440 | tf_op jit(solution)/shard_map/ppermute | solution.py:38
  46.2 13.8 %copy-start.13 = (bf16[1,256,256]{2,1,0:T(8,128)(2,1)S(1)}, bf16[1,256,256]{2,1,0:T(8,128)(2,1)}, u32[]{:S(2)}) copy-start(bf16[1,256,256]{2,1,0:T(8,128)(2,1)} %param.5) | copy-start | bytes 393220
  46.3 13.8 %collective-permute-start.1 = (bf16[256,256]{1,0:T(8,128)(2,1)S(1)}, bf16[256,256]{1,0:T(8,128)(2,1)S(1)}, u32[]{:S(2)}, u32[]{:S(2)}) collective-permute-start(bf16[256,256]{1,0:T(8,128)(2,1)S(1)} %bitcast.250), channel_id=1, source_target_pairs={{0,496},{16,32},{32,16},{48,64},{64,48},{80,96},{96,80},{112,128},... | collective-permute-start | bytes 393224 | tf_op jit(solution)/shard_map/ppermute | solution.py:38
  63.3 5.4 %copy-start.4 = (bf16[256,16,256]{2,0,1:T(8,128)(2,1)}, bf16[256,16,256]{2,0,1:T(8,128)(2,1)S(1)}, u32[]{:S(2)}) copy-start(bf16[256,16,256]{2,0,1:T(8,128)(2,1)S(1)} %get-tuple-element.9) | copy-start | bytes 6291460
  71.1 10.8 %all-to-all-start.2 = ((f32[4,16,256]{2,1,0:T(8,128)}), f32[4,16,256]{2,1,0:T(8,128)S(1)}, u32[]{:S(2)}, u32[]{:S(2)}) async-start(f32[4,16,256]{2,1,0:T(8,128)} %select_select_fusion.1), calls=%async_computation.2 | async-start | bytes 131072 | tf_op jit(solution)/shard_map/all_to_all | solution.py:34
  77.6 1.6 copy-start.12
  79.2 1.6 copy-start.11
  82.9 15.1 %all-to-all-start.3 = ((bf16[16,5,16,256]{3,2,1,0:T(8,128)(2,1)}), bf16[16,5,16,256]{3,2,1,0:T(8,128)(2,1)}, u32[]{:S(2)}, u32[]{:S(2)}) async-start(bf16[16,5,16,256]{3,2,1,0:T(8,128)(2,1)} %pad_maximum_fusion), calls=%async_computation.3 | async-start | bytes 1310720 | tf_op jit(solution)/shard_map/all_to_all | solution.py:34
  88.3 28.3 %collective-permute-start.2 = (f32[256,256]{1,0:T(8,128)S(1)}, f32[256,256]{1,0:T(8,128)S(1)}, u32[]{:S(2)}, u32[]{:S(2)}) collective-permute-start(f32[256,256]{1,0:T(8,128)S(1)} %bitcast.229), channel_id=1, source_target_pairs={{0,128},{16,144},{32,160},{48,176},{64,192},{80,208},{96,224},{112... | collective-permute-start | bytes 786440 | tf_op jit(solution)/shard_map/ppermute | solution.py:38
  118.3 23.8 %all-to-all-start.4 = ((f32[4,16,256]{2,1,0:T(8,128)}), f32[4,16,256]{2,1,0:T(8,128)S(1)}, u32[]{:S(2)}, u32[]{:S(2)}) async-start(f32[4,16,256]{2,1,0:T(8,128)} %select_select_fusion), calls=%async_computation.4 | async-start | bytes 131072 | tf_op jit(solution)/shard_map/all_to_all | solution.py:34
  143.1 16.1 %all-to-all-start.5 = ((bf16[16,4,16,256]{3,2,1,0:T(8,128)(2,1)}), bf16[16,4,16,256]{3,2,1,0:T(8,128)(2,1)S(1)}, u32[]{:S(2)}, u32[]{:S(2)}) async-start(bf16[16,4,16,256]{3,2,1,0:T(8,128)(2,1)} %broadcast_in_dim.128), calls=%async_computation.5 | async-start | bytes 1048576 | tf_op jit(solution)/shard_map/all_to_all | solution.py:34
  160.9 1.9 %copy-start.6 = (f32[256,256]{0,1:T(8,128)}, f32[256,256]{0,1:T(8,128)S(1)}, u32[]{:S(2)}) copy-start(f32[256,256]{0,1:T(8,128)S(1)} %fusion.20) | copy-start | bytes 786436
  162.8 3.8 %copy-start.7 = (f32[256,256]{0,1:T(8,128)S(1)}, f32[256,256]{0,1:T(8,128)}, u32[]{:S(2)}) copy-start(f32[256,256]{0,1:T(8,128)} %copy-done.6) | copy-start | bytes 786436
  165.8 0.7 copy-start.9
  166.6 1.7 copy-start.10
  167.9 14.4 %copy-start.5 = (f32[256,256]{1,0:T(8,128)}, f32[256,256]{1,0:T(8,128)S(1)}, u32[]{:S(2)}) copy-start(f32[256,256]{1,0:T(8,128)S(1)} %get-tuple-element.34) | copy-start | bytes 786436
  169.5 5.0 %copy-start.8 = (f32[1,16,16,256]{3,2,1,0:T(8,128)S(1)}, f32[1,16,16,256]{3,2,1,0:T(8,128)}, u32[]{:S(2)}) copy-start(f32[1,16,16,256]{3,2,1,0:T(8,128)} %get-tuple-element.10) | copy-start | bytes 786436
  177.7 1.6 copy-start.3
  179.3 1.6 copy-start.1
where the time goes:
time: 187 us; the launch traced here: 185 us
  starting transfers between devices  60.1 us (32%)
  waiting for transfers between devices  46.2 us (25%)
  matrix products  33.4 us (18%)
  local copies, waits for them, and re-layouts  30.2 us (16%)
  other arithmetic  13.5 us (7%)
  between operations  2.13 us (1%)
    all_to_all x6, starting transfers between devices, exchange(): return lax.all_to_all(x, axis, 0, 0, axis_index_groups=groups, tiled=True)  40.9 us
    all_to_all x6, waiting for transfers between devices, exchange(): return lax.all_to_all(x, axis, 0, 0, axis_index_groups=groups, tiled=True)  29 us
    dot_general x55, matrix products, mm(): return lax.dot_general(a, b, (dims, ((), ())), preferred_element_type=f32)  25 us
    ppermute x4, starting transfers between devices, permuted(): lax.ppermute(x, axis, [(i, route(i)) for i in range(lax.axis_size(axis))])  19.1 us
    ppermute x4, waiting for transfers between devices, permuted(): lax.ppermute(x, axis, [(i, route(i)) for i in range(lax.axis_size(axis))])  17.3 us
    convert_element_type x4, local copies, waits for them, and re-layouts, split(): return (rounded.astype(bf16), (x - rounded).astype(bf16))  9.94 us
    dot_general x1, local copies, waits for them, and re-layouts, body(): jnp.einsum('xa,abp->xbp', mix, iso, preferred_element_type=f32)  6.61 us
    unnamed x28, local copies, waits for them, and re-layouts  5.04 us
  transfers between devices with their start and end apart: 10, of which 7 were waited for; matrix products, arithmetic and copies ran while one was open for 18% of the time, Pallas kernels for 0%

commit v1 on v0

v1 whole, which is shorter than its diff:
```python
import jax
import jax.numpy as jnp
from jax import lax
from jax.experimental import pallas as pl
from jax.experimental.pallas import tpu as pltpu
from jax.sharding import PartitionSpec as P

bf16 = jnp.bfloat16
f32 = jnp.float32
NN = ((1,), (0,))
NT = ((1,), (1,))
SIZE = 256
WIDTH = 16
ROWS = SIZE // WIDTH
FLAT = SIZE * ROWS
HALF = 128


def split(x):
    hi = x.astype(bf16)
    return hi, (x - hi.astype(f32)).astype(bf16)


def mm(a, b, dims=NN):
    return lax.dot_general(a, b, (dims, ((), ())), preferred_element_type=f32)


def mm3(a, b, dims=NN):
    ah, al = split(a)
    bh, bl = split(b)
    return mm(ah, bh, dims) + (mm(ah, bl, dims) + mm(al, bh, dims))


def sandwich(c, e):
    return mm3(mm3(c, e), c, NT)


def iotas():
    shape = (SIZE, SIZE)
    return lax.broadcasted_iota(jnp.int32, shape, 0), lax.broadcasted_iota(jnp.int32, shape, 1)


def call(kernel, name, outs, scratch=(), smem=0, unread=0, ins=0, flops=0, grid=None, in_specs=None, out_specs=None):
    vmem = pl.BlockSpec(memory_space=pltpu.VMEM)
    if in_specs is None:
        in_specs = (
            [pl.BlockSpec(memory_space=pltpu.SMEM)] * smem
            + [vmem] * (ins - smem - unread)
            + [pl.BlockSpec(memory_space=pl.ANY)] * unread
        )
        out_specs = [vmem] * len(outs)
    params = dict(grid=grid) if grid else {}
    return pl.pallas_call(
        kernel,
        name=name,
        out_shape=[jax.ShapeDtypeStruct(*o) for o in outs],
        in_specs=in_specs,
        out_specs=out_specs,
        scratch_shapes=scratch,
        compiler_params=pltpu.CompilerParams(vmem_limit_bytes=48 << 20),
        cost_estimate=pl.CostEstimate(flops=flops, bytes_accessed=4 << 20, transcendentals=0),
        **params,
    )


def spread_rows(iso_ref, wide_ref):
    wide = iso_ref[...].reshape(FLAT, SIZE).astype(f32)
    wide_ref[0] = wide[:, :HALF]
    wide_ref[1] = wide[:, HALF:]


def bond_slice(wide_ref, b):
    rows = pl.ds(b, SIZE, stride=ROWS)
    return jnp.concatenate([wide_ref[h, rows, :].astype(bf16) for h in range(2)], axis=1)


def ascend_kernel(iso_ref, left_ref, right_ref, out_ref, wide_ref, turned_ref, mapped_ref):
    edges = jnp.concatenate([left_ref[...], right_ref[...]], axis=0)
    spread_rows(iso_ref, wide_ref)
    for b in range(ROWS):
        block = bond_slice(wide_ref, b)
        here = slice(b * SIZE, (b + 1) * SIZE)
        turned_ref[:, here] = block.T
        for k, part in enumerate(split(mm(edges, block))):
            mapped_ref[k, here, :SIZE] = part[:SIZE]
            mapped_ref[k, here, SIZE:] = part[SIZE:]
    turned = turned_ref[...]
    total = mm(turned, mapped_ref[0]) + mm(turned, mapped_ref[1])
    for k in range(2):
        out_ref[:, k] = total[:, k * SIZE : (k + 1) * SIZE].reshape(WIDTH, ROWS, SIZE)


def norm_kernel(iso_ref, after_ref, out_ref):
    flat = iso_ref[...].reshape(FLAT, SIZE)
    out_ref[...] = mm(flat.T, flat)


def round_kernel(got_ref, after_ref, out_ref):
    share = got_ref[0]
    for i in range(1, WIDTH):
        share = share + got_ref[i]
    share = share.astype(bf16)
    for i in range(WIDTH):
        out_ref[i] = share


def slices(index_ref, env_ref, foreign_ref, out_ref):
    rows = pl.ds(index_ref[0] * ROWS, ROWS)
    own = env_ref[rows, :]
    crossed = mm3(mm3(foreign_ref[rows, :], env_ref[...]), foreign_ref[...], NT)
    for p in range(4):
        which = index_ref[1] ^ p
        out_ref[p] = jnp.where(which == 3, crossed, jnp.where(which == 0, 0.0, own))


def first_kernel(index_ref, own_ref, near_ref, couple_ref, foreign_ref, after_ref, env_ref, out_ref):
    def whole(ref):
        return (ref[:, 0].astype(f32) + ref[:, 1].astype(f32)).reshape(SIZE, SIZE)

    env_ref[...] = 0.5 * (whole(own_ref) + sandwich(couple_ref[...], whole(near_ref)))
    slices(index_ref, env_ref, foreign_ref, out_ref)


def gradient_kernel(index_ref, iso_ref, edge_ref, near_ref, far_ref, norm_ref, after_ref, hi_ref, lo_ref, out_ref, wide_ref, moved_ref):
    odd = index_ref[2] == 1

    def whole(ref, k):
        return ref[:, k].astype(f32).reshape(SIZE, SIZE)

    from_left = jnp.where(odd, whole(near_ref, 1), whole(far_ref, 1))
    from_right = jnp.where(odd, whole(far_ref, 0), whole(near_ref, 0))
    mix = (edge_ref[...].astype(f32) + from_left + from_right).astype(bf16)
    spread_rows(iso_ref, wide_ref)
    for b in range(ROWS):
        moved = mm(mix, bond_slice(wide_ref, b))
        for h in range(2):
            moved_ref[h, pl.ds(b, SIZE, stride=ROWS), :] = moved[:, h * HALF : (h + 1) * HALF]
    for h in range(2):
        columns = slice(h * HALF, (h + 1) * HALF)
        hi, lo = split(moved_ref[h])
        hi_ref[:, columns] = hi
        lo_ref[:, columns] = lo
    turned = iso_ref[...].reshape(FLAT, SIZE).T
    part_q = mm(turned, hi_ref[...]) + mm(turned, lo_ref[...])
    turned = hi_ref[...].T
    cross = mm(turned, lo_ref[...])
    part_r = mm(turned, hi_ref[...]) + (cross + cross.T)
    part_n = norm_ref[...]
    row, col = iotas()
    diag_n = jnp.sum(jnp.where(row == col, part_n, 0.0), axis=0, keepdims=True)
    diag_r = jnp.sum(jnp.where(row == col, part_r, 0.0), axis=0, keepdims=True)
    nh, nl = split(diag_n)
    _, rl = split(diag_r)
    extra = jnp.concatenate(
        [nh.astype(f32), nl.astype(f32), rl.astype(f32), jnp.zeros((ROWS - 3, SIZE), f32)], axis=0
    ).astype(bf16)
    packed = jnp.where(row < col, part_n, part_r)
    for i in range(WIDTH):
        out_ref[i, :ROWS] = extra
    out_ref[:, ROWS : 2 * ROWS] = part_q.astype(bf16).reshape(WIDTH, ROWS, SIZE)
    out_ref[:, 2 * ROWS :] = packed.astype(bf16).reshape(WIDTH, ROWS, SIZE)


def pack_kernel(got_ref, parts_ref, out_ref):
    hi, lo = split((got_ref[0] + got_ref[1]) + (got_ref[2] + got_ref[3]))
    for i in range(WIDTH):
        out_ref[i, :ROWS] = hi
        out_ref[i, ROWS : 2 * ROWS] = lo
    out_ref[:, 2 * ROWS :] = parts_ref[...]


def repeat_kernel(got_ref, sums_ref, out_ref):
    hi, lo = split((got_ref[0] + got_ref[1]) + (got_ref[2] + got_ref[3]))
    for i in range(WIDTH):
        out_ref[i, :ROWS] = hi
        out_ref[i, ROWS : 2 * ROWS] = lo
        out_ref[i, 2 * ROWS :] = sums_ref[...]


def two_levels(env_ref, got_ref, couple_ref):
    force = got_ref[:, :ROWS].astype(f32) + got_ref[:, ROWS : 2 * ROWS].astype(f32)
    return 0.25 * (env_ref[...] + sandwich(couple_ref[...], force.reshape(SIZE, SIZE)))


def second_kernel(index_ref, got_ref, old_ref, couple_ref, foreign_ref, env_ref, out_ref, sums_ref, extra_ref):
    env_ref[...] = two_levels(old_ref, got_ref, couple_ref)
    slices(index_ref, env_ref, foreign_ref, out_ref)
    total = got_ref[0, 2 * ROWS :].astype(f32)
    for i in range(1, WIDTH):
        total = total + got_ref[i, 2 * ROWS :].astype(f32)
    extra_ref[...] = total[:ROWS]
    sums_ref[...] = total[ROWS:].astype(bf16)


def polar_matrices(env, full_q, full_s, extra_ref):
    row, col = iotas()
    top = env.astype(bf16).astype(f32)
    lower = jnp.where(row > col, full_s, 0.0)
    upper = jnp.where(row < col, full_s, 0.0)
    diag_n = extra_ref[0:1, :] + extra_ref[1:2, :]
    full_n = upper + upper.T + jnp.where(row == col, diag_n, 0.0)
    full_r = lower + lower.T + jnp.where(row == col, full_s + extra_ref[2:3, :], 0.0)
    half = full_q + 0.5 * mm3(full_n, top)
    side = mm3(top.T, half)
    gram = full_r + side + side.T
    trace = jnp.sum(jnp.where(row == col, gram, 0.0), keepdims=True)
    factor = lax.rsqrt(trace + 1e-06)
    g = gram * (factor * factor)
    g2 = mm3(g, g)
    eye = jnp.where(row == col, 1.0, 0.0)
    poly = 2.25 * eye - 2.4375 * g + mm3(g2, 1.6875 * eye - 0.5625 * g + 0.0625 * g2)
    poly = poly * factor
    return poly, mm3(top, poly)


def final_kernel(got_ref, extra_ref, old_ref, couple_ref, iso_ref, hi_ref, lo_ref, env_ref, out_ref, map_ref):
    @pl.when(pl.program_id(0) == 0)
    def _():
        env = two_levels(old_ref, got_ref, couple_ref)
        env_ref[...] = env
        full_q = got_ref[:, 2 * ROWS : 3 * ROWS].astype(f32).reshape(SIZE, SIZE)
        full_s = got_ref[:, 3 * ROWS :].astype(f32).reshape(SIZE, SIZE)
        poly, low = polar_matrices(env, full_q, full_s, extra_ref)
        ph, pl_ = split(poly)
        lh, ll = split(low)
        for k, part in enumerate((ph, ph, pl_, lh, ll)):
            map_ref[k * SIZE : (k + 1) * SIZE] = part

    flat = iso_ref[...].reshape(-1, SIZE)
    hi = hi_ref[...]
    rows = jnp.concatenate([hi, lo_ref[...], hi, flat, flat], axis=1)
    out_ref[...] = mm(rows, map_ref[...]).astype(bf16).reshape(iso_ref.shape)


def exchange(x, axis, groups=None):
    return lax.all_to_all(x, axis, 0, 0, axis_index_groups=groups, tiled=True)


def permuted(x, axis, route):
    return lax.ppermute(x, axis, [(i, route(i)) for i in range(lax.axis_size(axis))])


square = ((SIZE, SIZE), f32)
sliced = ((4, ROWS, SIZE), f32)


def ascend(iso, left, right):
    return call(
        ascend_kernel,
        "ascend",
        [((WIDTH, 2, ROWS, SIZE), f32)],
        scratch=[
            pltpu.VMEM((2, FLAT, HALF), f32),
            pltpu.VMEM((SIZE, FLAT), bf16),
            pltpu.VMEM((2, FLAT, 2 * SIZE), bf16),
        ],
        ins=3,
        flops=6 << 29,
    )(iso, left, right)[0]


def norms(iso, after):
    return call(norm_kernel, "norms", [square], ins=2, unread=1, flops=1 << 29)(iso, after)[0]


def rounded(got, after):
    return call(round_kernel, "rounded", [((WIDTH, 2, ROWS, SIZE), bf16)], ins=2, unread=1)(got, after)[0]


def first(index, own, near, couple, foreign, after):
    return call(first_kernel, "first", [square, sliced], ins=6, smem=1, unread=1)(
        index, own, near, couple, foreign, after
    )


def gradient(index, iso, edge, near, far, norm, after):
    return call(
        gradient_kernel,
        "gradient",
        [((FLAT, SIZE), bf16), ((FLAT, SIZE), bf16), ((WIDTH, 3 * ROWS, SIZE), bf16)],
        scratch=[pltpu.VMEM((2, FLAT, HALF), f32), pltpu.VMEM((2, FLAT, HALF), f32)],
        ins=7,
        smem=1,
        unread=1,
        flops=5 << 29,
    )(index, iso, edge, near, far, norm, after)


def pack(got, parts):
    return call(pack_kernel, "pack", [((WIDTH, 5 * ROWS, SIZE), bf16)], ins=2)(got, parts)[0]


def repeat(got, sums):
    return call(repeat_kernel, "repeat", [((WIDTH, 4 * ROWS, SIZE), bf16)], ins=2)(got, sums)[0]


def second(index, got, old, couple, foreign):
    return call(
        second_kernel,
        "second",
        [square, sliced, ((2 * ROWS, SIZE), bf16), ((ROWS, SIZE), f32)],
        ins=5,
        smem=1,
    )(index, got, old, couple, foreign)


def final(got, extra, old, couple, iso, hi, lo, steps=4):
    vmem = pl.BlockSpec(memory_space=pltpu.VMEM)
    part = pl.BlockSpec((SIZE // steps, ROWS, SIZE), lambda i: (i, 0, 0))
    line = pl.BlockSpec((FLAT // steps, SIZE), lambda i: (i, 0))
    return call(
        final_kernel,
        "final",
        [square, (iso.shape, bf16)],
        scratch=[pltpu.VMEM((5 * SIZE, SIZE), bf16)],
        grid=(steps,),
        in_specs=[vmem] * 4 + [part, line, line],
        out_specs=[vmem, part],
        flops=5 << 29,
    )(got, extra, old, couple, iso, hi, lo)


def body(iso, edge_left, edge_right, coupling):
    iso, left, right, couple = iso[0], edge_left[0], edge_right[0], coupling[0]
    s = lax.axis_index("blk")
    j = lax.axis_index("bond")
    z = s // 2
    index_1 = jnp.stack([j, z % 4, s % 2]).astype(jnp.int32)
    index_2 = jnp.stack([j, z // 4, s % 2]).astype(jnp.int32)

    couple_1 = permuted(couple, "blk", lambda i: i ^ 2)
    couple_2 = permuted(couple, "blk", lambda i: i ^ 8)

    blocks = ascend(iso, left, right)
    norm = norms(iso, blocks)
    share = rounded(exchange(blocks, "bond"), norm)
    own = exchange(share, "bond")
    near = permuted(own, "blk", lambda i: i ^ 1)
    far = permuted(own, "blk", lambda i: (i + 1) % 32 if i % 2 else (i - 1) % 32)

    quads = [[(zq * 4 + zl) * 2 + c for zl in range(4)] for zq in range(4) for c in range(2)]
    strides = [[(zh * 4 + zl) * 2 + c for zh in range(4)] for zl in range(4) for c in range(2)]

    env, outgoing = first(index_1, own, near, couple, couple_1, couple_2)
    incoming = exchange(outgoing, "blk", quads)
    moved_hi, moved_lo, parts = gradient(index_1, iso, left, near, far, norm, outgoing)
    got = exchange(pack(incoming, parts), "bond")
    env, outgoing, sums, extra = second(index_2, got, env, couple, couple_2)
    incoming = exchange(outgoing, "blk", strides)
    got = exchange(repeat(incoming, sums), "bond")
    env, out = final(got, extra, env, couple, iso, moved_hi, moved_lo)
    return (out[None], env[None])


def solution(mesh):
    placed = (
        P("blk", None, "bond", None),
        P("blk", None, None),
        P("blk", None, None),
        P("blk", None, None),
    )
    return jax.shard_map(
        body,
        mesh=mesh,
        in_specs=placed,
        out_specs=(P("blk", None, "bond", None), P("blk", None, None)),
        check_vma=False,
    )
```

time: 187 us -> 150 us (0.80)
  the two profiles are of different devices: /device:TPU:2 before, /device:TPU:64 now
where the time goes in v1:
time: 150 us; the launch traced here: 149 us
  starting transfers between devices  39.9 us (27%)
  blocking collectives  38.1 us (25%)
  waiting for transfers between devices  36.4 us (24%)
  Pallas kernels  27.1 us (18%)
  local copies, waits for them, and re-layouts  6.77 us (5%)
    all_to_all x2, blocking collectives, exchange(): return lax.all_to_all(x, axis, 0, 0, axis_index_groups=groups, tiled=True)  38.1 us
    all_to_all x4, starting transfers between devices, exchange(): return lax.all_to_all(x, axis, 0, 0, axis_index_groups=groups, tiled=True)  23.1 us
    all_to_all x4, waiting for transfers between devices, exchange(): return lax.all_to_all(x, axis, 0, 0, axis_index_groups=groups, tiled=True)  23.1 us
    ppermute x4, starting transfers between devices, permuted(): lax.ppermute(x, axis, [(i, route(i)) for i in range(lax.axis_size(axis))])  16.8 us
    ppermute x4, waiting for transfers between devices, permuted(): lax.ppermute(x, axis, [(i, route(i)) for i in range(lax.axis_size(axis))])  13.3 us
    pallas_call x1, Pallas kernels, final(): call(final_kernel, 'final', [square, (iso.shape, bf16)], scratch=[pltpu.V...  8.13 us
    pallas_call x1, Pallas kernels, gradient(): call(gradient_kernel, 'gradient', [((FLAT, SIZE), bf16), ((FLAT, SIZE), b...  7.19 us
    unnamed x24, local copies, waits for them, and re-layouts  6.77 us
  transfers between devices with their start and end apart: 8, of which 4 were waited for; matrix products, arithmetic and copies ran while one was open for 0% of the time, Pallas kernels for 7%

profile of v1, /device:TPU:64, one launch (start us, length us, event | category | flops | bytes accessed | tf_op | source)
XLA Modules:
  0.0 149.3 jit_solution(5735529014421603002)
XLA Ops:
  0.6 0.0 copy-start
  0.6 1.6 %copy-done = bf16[1,256,16,256]{3,2,1,0:T(8,128)(2,1)S(1)} copy-done((bf16[1,256,16,256]{3,2,1,0:T(8,128)(2,1)S(1)}, bf16[1,256,16,256]{3,2,1,0:T(8,128)(2,1)}, u32[]{:S(2)}) %copy-start) | copy-done | bytes 2097176
  2.2 0.9 copy-done.6
  3.1 0.9 copy-done.7
  4.0 5.6 %ascend.1.after_ref = f32[16,2,16,256]{3,2,1,0:T(8,128)} custom-call(bf16[256,16,256]{2,1,0:T(8,128)(2,1)S(1)} %bitcast.11, bf16[256,256]{1,0:T(8,128)(2,1)S(1)} %bitcast.20, bf16[256,256]{1,0:T(8,128)(2,1)S(1)} %bitcast.19), custom_call_target="tpu_custom_call" | custom-call | flops 3221225472 | bytes 4194304 | tf_op jit(solution)/shard_map/ascend/pallas_call | solution.py:248
  9.7 7.0 %all-to-all-start = ((f32[16,2,16,256]{3,2,1,0:T(8,128)}), f32[16,2,16,256]{3,2,1,0:T(8,128)S(1)}, u32[]{:S(2)}, u32[]{:S(2)}) async-start(f32[16,2,16,256]{3,2,1,0:T(8,128)} %ascend.1.after_ref), calls=%async_computation | async-start | bytes 1048576 | tf_op jit(solution)/shard_map/all_to_all | solution.py:236
  16.7 0.0 copy-start.3
  16.7 0.8 norms.1.after_ref.norm_ref
  17.5 10.7 %all-to-all-done.got_ref = f32[16,2,16,256]{3,2,1,0:T(8,128)S(1)} async-done(((f32[16,2,16,256]{3,2,1,0:T(8,128)}), f32[16,2,16,256]{3,2,1,0:T(8,128)S(1)}, u32[]{:S(2)}, u32[]{:S(2)}) %all-to-all-start) | async-done | bytes 524320 | tf_op jit(solution)/shard_map/all_to_all | solution.py:236
  28.2 0.7 rounded.1
  29.0 3.5 %all-to-all-start.1 = ((bf16[16,2,16,256]{3,2,1,0:T(8,128)(2,1)}), bf16[16,2,16,256]{3,2,1,0:T(8,128)(2,1)S(1)}, u32[]{:S(2)}, u32[]{:S(2)}) async-start(bf16[16,2,16,256]{3,2,1,0:T(8,128)(2,1)} %rounded.1), calls=%async_computation.1 | async-start | bytes 524288 | tf_op jit(solution)/shard_map/all_to_all | solution.py:236
  32.5 9.1 %collective-permute-start.2 = (f32[256,256]{1,0:T(8,128)S(1)}, f32[256,256]{1,0:T(8,128)S(1)}, u32[]{:S(2)}, u32[]{:S(2)}) collective-permute-start(f32[256,256]{1,0:T(8,128)S(1)} %bitcast.14), channel_id=1, source_target_pairs={{0,128},{16,144},{32,160},{48,176},{64,192},{80,208},{96,224},{112... | collective-permute-start | bytes 786440 | tf_op jit(solution)/shard_map/ppermute | solution.py:240
  41.6 3.8 %collective-permute-start.1 = (f32[256,256]{1,0:T(8,128)S(1)}, f32[256,256]{1,0:T(8,128)S(1)}, u32[]{:S(2)}, u32[]{:S(2)}) collective-permute-start(f32[256,256]{1,0:T(8,128)S(1)} %bitcast.15), channel_id=1, source_target_pairs={{0,32},{16,48},{32,0},{48,16},{64,96},{80,112},{96,64},{112,80},{1... | collective-permute-start | bytes 786440 | tf_op jit(solution)/shard_map/ppermute | solution.py:240
  45.5 1.9 %collective-permute-start = (bf16[16,2,16,256]{3,2,1,0:T(8,128)(2,1)S(1)}, bf16[16,2,16,256]{3,2,1,0:T(8,128)(2,1)S(1)}, u32[]{:S(2)}, u32[]{:S(2)}) collective-permute-start(bf16[16,2,16,256]{3,2,1,0:T(8,128)(2,1)S(1)} %all-to-all-done.1.own_ref), channel_id=1, source_target_pairs={{0,16},{16,0},{32,48},{48,32},{64,80},{80,64},{96,112},{112,96},{1... | collective-permute-start | bytes 786440 | tf_op jit(solution)/shard_map/ppermute | solution.py:240
  47.4 1.9 %collective-permute-start.3 = (bf16[16,2,16,256]{3,2,1,0:T(8,128)(2,1)S(1)}, bf16[16,2,16,256]{3,2,1,0:T(8,128)(2,1)S(1)}, u32[]{:S(2)}, u32[]{:S(2)}) collective-permute-start(bf16[16,2,16,256]{3,2,1,0:T(8,128)(2,1)S(1)} %all-to-all-done.1.own_ref), channel_id=1, source_target_pairs={{0,496},{16,32},{32,16},{48,64},{64,48},{80,96},{96,80},{112,128},... | collective-permute-start | bytes 786440 | tf_op jit(solution)/shard_map/ppermute | solution.py:240
  49.4 0.1 add_add_fusion.1.index_ref
  49.5 7.0 %collective-permute-done.2.after_ref.foreign_ref = f32[256,256]{1,0:T(8,128)S(1)} collective-permute-done((f32[256,256]{1,0:T(8,128)S(1)}, f32[256,256]{1,0:T(8,128)S(1)}, u32[]{:S(2)}, u32[]{:S(2)}) %collective-permute-start.2) | collective-permute-done | bytes 262176 | tf_op jit(solution)/shard_map/ppermute | solution.py:240
  56.4 6.3 %collective-permute-done.1.foreign_ref = f32[256,256]{1,0:T(8,128)S(1)} collective-permute-done((f32[256,256]{1,0:T(8,128)S(1)}, f32[256,256]{1,0:T(8,128)S(1)}, u32[]{:S(2)}, u32[]{:S(2)}) %collective-permute-start.1) | collective-permute-done | bytes 262176 | tf_op jit(solution)/shard_map/ppermute | solution.py:240
  62.8 2.2 %first.1 = (f32[256,256]{1,0:T(8,128)S(1)}, f32[4,16,256]{2,1,0:T(8,128)}) custom-call(s32[3]{0:T(128)S(1)} %add_add_fusion.1.index_ref, bf16[16,2,16,256]{3,2,1,0:T(8,128)(2,1)S(1)} %all-to-all-done.1.own_ref, bf16[16,2,16,256]{3,2,1,0:T(8,128)(2,1)S(1)} %collective-permute-done.near_ref, f32[256,256]{1,0:T(8,128)S(1)} %bitcast.16, ...), custom_call_target="tpu_custom_call" | custom-call | bytes 4194304 | tf_op jit(solution)/shard_map/first/pallas_call | solution.py:271
  64.9 0.7 copy-done.4
  65.6 5.4 %all-to-all-start.2 = ((f32[4,16,256]{2,1,0:T(8,128)}), f32[4,16,256]{2,1,0:T(8,128)S(1)}, u32[]{:S(2)}, u32[]{:S(2)}) async-start(f32[4,16,256]{2,1,0:T(8,128)} %get-tuple-element.13.after_ref), calls=%async_computation.2 | async-start | bytes 131072 | tf_op jit(solution)/shard_map/all_to_all | solution.py:236
  71.0 7.2 %gradient.1 = (bf16[4096,256]{1,0:T(8,128)(2,1)S(1)}, bf16[4096,256]{1,0:T(8,128)(2,1)S(1)}, bf16[16,48,256]{2,1,0:T(8,128)(2,1)S(1)}) custom-call(s32[3]{0:T(128)S(1)} %add_add_fusion.1.index_ref, bf16[256,16,256]{2,1,0:T(8,128)(2,1)} %bitcast.10, bf16[256,256]{1,0:T(8,128)(2,1)S(1)} %bitcast.21, ...), custom_call_target="tpu_custom_call" | custom-call | flops 2684354560 | bytes 4194304 | tf_op jit(solution)/shard_map/gradient/pallas_call | solution.py:277
  78.3 1.3 copy-done.9
  79.6 1.3 copy-done.11
  80.9 0.9 pack.1
  81.8 7.2 %all-to-all-start.3 = ((bf16[16,80,256]{2,1,0:T(8,128)(2,1)}), bf16[16,80,256]{2,1,0:T(8,128)(2,1)S(1)}, u32[]{:S(2)}, u32[]{:S(2)}) async-start(bf16[16,80,256]{2,1,0:T(8,128)(2,1)} %pack.1), calls=%async_computation.3 | async-start | bytes 1310720 | tf_op jit(solution)/shard_map/all_to_all | solution.py:236
  89.0 0.1 add_add_fusion.index_ref
  89.1 12.4 %all-to-all-done.3.got_ref = bf16[16,80,256]{2,1,0:T(8,128)(2,1)S(1)} async-done(((bf16[16,80,256]{2,1,0:T(8,128)(2,1)}), bf16[16,80,256]{2,1,0:T(8,128)(2,1)S(1)}, u32[]{:S(2)}, u32[]{:S(2)}) %all-to-all-start.3) | async-done | bytes 655392 | tf_op jit(solution)/shard_map/all_to_all | solution.py:236
  101.4 1.6 %second.1 = (f32[256,256]{1,0:T(8,128)S(1)}, f32[4,16,256]{2,1,0:T(8,128)S(1)}, bf16[32,256]{1,0:T(8,128)(2,1)S(1)}, f32[16,256]{1,0:T(8,128)S(1)}) custom-call(s32[3]{0:T(128)S(1)} %add_add_fusion.index_ref, bf16[16,80,256]{2,1,0:T(8,128)(2,1)S(1)} %all-to-all-done.3.got_ref, f32[256,256]{1,0:T(8,128)S(1)} %copy-done.5, f32[256,256]{1,0:T(8,128)S(1)} %bitcast.17, ...), custom_call_target="tpu_custom_call" | custom-call | bytes 4194304 | tf_op jit(solution)/shard_map/second/pallas_call | solution.py:298
  103.0 24.9 %all_to_all.30.got_ref = f32[4,16,256]{2,1,0:T(8,128)S(1)} all-to-all(f32[4,16,256]{2,1,0:T(8,128)S(1)} %get-tuple-element.16), channel_id=1, replica_groups={{0,128,256,384},{16,144,272,400},{32,160,288,416},{48,176,304,432},{64,..., dimensions={0} | all-to-all | bytes 131072 | tf_op jit(solution)/shard_map/all_to_all | solution.py:236
  128.0 13.2 %all_to_all.31.got_ref = bf16[16,64,256]{2,1,0:T(8,128)(2,1)S(1)} all-to-all(bf16[16,64,256]{2,1,0:T(8,128)(2,1)S(1)} %repeat.1), channel_id=1, replica_groups=mesh['blk'=32,'bond'=16] {'bond'}, dimensions={0} | all-to-all | bytes 1048576 | tf_op jit(solution)/shard_map/all_to_all | solution.py:236
  141.1 8.1 %final.1 = (f32[256,256]{1,0:T(8,128)}, bf16[256,16,256]{2,1,0:T(8,128)(2,1)}) custom-call(bf16[16,64,256]{2,1,0:T(8,128)(2,1)S(1)} %all_to_all.31.got_ref, f32[16,256]{1,0:T(8,128)S(1)} %get-tuple-element.18.extra_ref, f32[256,256]{1,0:T(8,128)S(1)} %get-tuple-element.19.old_ref, f32[256,256]{1,0:T(8,128)S(1)} %bitcast.18, ...), custom_call_target="tpu_custom_call" | custom-call | flops 2684354560 | bytes 4194304 | tf_op jit(solution)/shard_map/final/pallas_call | solution.py:311
  (21 shorter events, 0.1 us)
Async XLA Ops:
  0.6 1.6 %copy-start = (bf16[1,256,16,256]{3,2,1,0:T(8,128)(2,1)S(1)}, bf16[1,256,16,256]{3,2,1,0:T(8,128)(2,1)}, u32[]{:S(2)}) copy-start(bf16[1,256,16,256]{3,2,1,0:T(8,128)(2,1)} %param.4) | copy-start | bytes 6291460
  2.2 0.9 copy-start.6
  3.1 0.9 copy-start.7
  4.0 12.7 %copy-start.1 = (bf16[1,256,16,256]{3,2,1,0:T(8,128)(2,1)S(1)}, bf16[1,256,16,256]{3,2,1,0:T(8,128)(2,1)}, u32[]{:S(2)}) copy-start(bf16[1,256,16,256]{3,2,1,0:T(8,128)(2,1)} %param.4) | copy-start | bytes 6291460
  9.7 18.6 %all-to-all-start = ((f32[16,2,16,256]{3,2,1,0:T(8,128)}), f32[16,2,16,256]{3,2,1,0:T(8,128)S(1)}, u32[]{:S(2)}, u32[]{:S(2)}) async-start(f32[16,2,16,256]{3,2,1,0:T(8,128)} %ascend.1.after_ref), calls=%async_computation | async-start | bytes 1048576 | tf_op jit(solution)/shard_map/all_to_all | solution.py:236
  16.7 15.8 %copy-start.3 = (f32[1,256,256]{2,1,0:T(8,128)S(1)}, f32[1,256,256]{2,1,0:T(8,128)}, u32[]{:S(2)}) copy-start(f32[1,256,256]{2,1,0:T(8,128)} %param.7) | copy-start | bytes 786436
  17.5 53.6 %copy-start.8 = (bf16[1,256,256]{2,1,0:T(8,128)(2,1)S(1)}, bf16[1,256,256]{2,1,0:T(8,128)(2,1)}, u32[]{:S(2)}) copy-start(bf16[1,256,256]{2,1,0:T(8,128)(2,1)} %param.5) | copy-start | bytes 393220
  29.0 16.5 %all-to-all-start.1 = ((bf16[16,2,16,256]{3,2,1,0:T(8,128)(2,1)}), bf16[16,2,16,256]{3,2,1,0:T(8,128)(2,1)S(1)}, u32[]{:S(2)}, u32[]{:S(2)}) async-start(bf16[16,2,16,256]{3,2,1,0:T(8,128)(2,1)} %rounded.1), calls=%async_computation.1 | async-start | bytes 524288 | tf_op jit(solution)/shard_map/all_to_all | solution.py:236
  32.5 23.9 %collective-permute-start.2 = (f32[256,256]{1,0:T(8,128)S(1)}, f32[256,256]{1,0:T(8,128)S(1)}, u32[]{:S(2)}, u32[]{:S(2)}) collective-permute-start(f32[256,256]{1,0:T(8,128)S(1)} %bitcast.14), channel_id=1, source_target_pairs={{0,128},{16,144},{32,160},{48,176},{64,192},{80,208},{96,224},{112... | collective-permute-start | bytes 786440 | tf_op jit(solution)/shard_map/ppermute | solution.py:240
  41.6 21.1 %collective-permute-start.1 = (f32[256,256]{1,0:T(8,128)S(1)}, f32[256,256]{1,0:T(8,128)S(1)}, u32[]{:S(2)}, u32[]{:S(2)}) collective-permute-start(f32[256,256]{1,0:T(8,128)S(1)} %bitcast.15), channel_id=1, source_target_pairs={{0,32},{16,48},{32,0},{48,16},{64,96},{80,112},{96,64},{112,80},{1... | collective-permute-start | bytes 786440 | tf_op jit(solution)/shard_map/ppermute | solution.py:240
  45.5 17.3 %collective-permute-start = (bf16[16,2,16,256]{3,2,1,0:T(8,128)(2,1)S(1)}, bf16[16,2,16,256]{3,2,1,0:T(8,128)(2,1)S(1)}, u32[]{:S(2)}, u32[]{:S(2)}) collective-permute-start(bf16[16,2,16,256]{3,2,1,0:T(8,128)(2,1)S(1)} %all-to-all-done.1.own_ref), channel_id=1, source_target_pairs={{0,16},{16,0},{32,48},{48,32},{64,80},{80,64},{96,112},{112,96},{1... | collective-permute-start | bytes 786440 | tf_op jit(solution)/shard_map/ppermute | solution.py:240
  47.4 23.6 %collective-permute-start.3 = (bf16[16,2,16,256]{3,2,1,0:T(8,128)(2,1)S(1)}, bf16[16,2,16,256]{3,2,1,0:T(8,128)(2,1)S(1)}, u32[]{:S(2)}, u32[]{:S(2)}) collective-permute-start(bf16[16,2,16,256]{3,2,1,0:T(8,128)(2,1)S(1)} %all-to-all-done.1.own_ref), channel_id=1, source_target_pairs={{0,496},{16,32},{32,16},{48,64},{64,48},{80,96},{96,80},{112,128},... | collective-permute-start | bytes 786440 | tf_op jit(solution)/shard_map/ppermute | solution.py:240
  64.9 0.7 copy-start.4
  65.6 15.3 %all-to-all-start.2 = ((f32[4,16,256]{2,1,0:T(8,128)}), f32[4,16,256]{2,1,0:T(8,128)S(1)}, u32[]{:S(2)}, u32[]{:S(2)}) async-start(f32[4,16,256]{2,1,0:T(8,128)} %get-tuple-element.13.after_ref), calls=%async_computation.2 | async-start | bytes 131072 | tf_op jit(solution)/shard_map/all_to_all | solution.py:236
  78.2 1.3 copy-start.9
  79.6 1.3 copy-start.11
  80.9 20.5 %copy-start.5 = (f32[256,256]{1,0:T(8,128)S(1)}, f32[256,256]{1,0:T(8,128)}, u32[]{:S(2)}) copy-start(f32[256,256]{1,0:T(8,128)} %copy-done.4) | copy-start | bytes 786436
  81.8 59.3 %copy-start.2 = (bf16[1,256,16,256]{3,2,1,0:T(8,128)(2,1)S(1)}, bf16[1,256,16,256]{3,2,1,0:T(8,128)(2,1)}, u32[]{:S(2)}) copy-start(bf16[1,256,16,256]{3,2,1,0:T(8,128)(2,1)} %param.4) | copy-start | bytes 6291460
  81.8 19.6 %all-to-all-start.3 = ((bf16[16,80,256]{2,1,0:T(8,128)(2,1)}), bf16[16,80,256]{2,1,0:T(8,128)(2,1)S(1)}, u32[]{:S(2)}, u32[]{:S(2)}) async-start(bf16[16,80,256]{2,1,0:T(8,128)(2,1)} %pack.1), calls=%async_computation.3 | async-start | bytes 1310720 | tf_op jit(solution)/shard_map/all_to_all | solution.py:236
  101.4 39.7 %copy-start.10 = (bf16[4096,256]{1,0:T(8,128)(2,1)S(1)}, bf16[4096,256]{1,0:T(8,128)(2,1)}, u32[]{:S(2)}) copy-start(bf16[4096,256]{1,0:T(8,128)(2,1)} %copy-done.9) | copy-start | bytes 6291460

commit v2 on v1

--- a/solution.py
+++ b/solution.py
@@ -14,6 +14,8 @@
 ROWS = SIZE // WIDTH
 FLAT = SIZE * ROWS
 HALF = 128
+CHUNKS = 4
+EXTRA = 8
 
 
 def split(x):
@@ -35,12 +37,16 @@
     return mm3(mm3(c, e), c, NT)
 
 
+def in_hbm(x):
+    return pltpu.with_memory_space_constraint(x, pltpu.HBM)
+
+
 def iotas():
     shape = (SIZE, SIZE)
     return lax.broadcasted_iota(jnp.int32, shape, 0), lax.broadcasted_iota(jnp.int32, shape, 1)
 
 
-def call(kernel, name, outs, scratch=(), smem=0, unread=0, ins=0, flops=0, grid=None, in_specs=None, out_specs=None):
+def call(kernel, name, outs, scratch=(), smem=0, unread=0, ins=0, flops=0, grant=16, grid=None, in_specs=None, out_specs=None):
     vmem = pl.BlockSpec(memory_space=pltpu.VMEM)
     if in_specs is None:
         in_specs = (
@@ -53,11 +59,11 @@
     return pl.pallas_call(
         kernel,
         name=name,
-        out_shape=[jax.ShapeDtypeStruct(*o) for o in outs],
+        out_shape=[o if isinstance(o, pl.MemoryRef) else jax.ShapeDtypeStruct(*o) for o in outs],
         in_specs=in_specs,
         out_specs=out_specs,
         scratch_shapes=scratch,
-        compiler_params=pltpu.CompilerParams(vmem_limit_bytes=48 << 20),
+        compiler_params=pltpu.CompilerParams(vmem_limit_bytes=grant << 20),
         cost_estimate=pl.CostEstimate(flops=flops, bytes_accessed=4 << 20, transcendentals=0),
         **params,
     )
@@ -74,9 +80,26 @@
     return jnp.concatenate([wide_ref[h, rows, :].astype(bf16) for h in range(2)], axis=1)
 
 
-def ascend_kernel(iso_ref, left_ref, right_ref, out_ref, wide_ref, turned_ref, mapped_ref):
-    edges = jnp.concatenate([left_ref[...], right_ref[...]], axis=0)
-    spread_rows(iso_ref, wide_ref)
+def ascend_kernel(iso_hbm, left_hbm, right_hbm, out_ref, iso_ref, edge_ref, wide_ref, turned_ref, mapped_ref, sems):
+    step = SIZE // CHUNKS
+    copies = []
+    for i in range(CHUNKS):
+        here = pl.ds(i * step, step)
+        copies.append(pltpu.make_async_copy(iso_hbm.at[here], iso_ref.at[here], sems.at[i]))
+    edge_copies = [
+        pltpu.make_async_copy(left_hbm, edge_ref.at[pl.ds(0, SIZE)], sems.at[CHUNKS]),
+        pltpu.make_async_copy(right_hbm, edge_ref.at[pl.ds(SIZE, SIZE)], sems.at[CHUNKS + 1]),
+    ]
+    for copy in copies + edge_copies:
+        copy.start()
+    for i, copy in enumerate(copies):
+        copy.wait()
+        wide = iso_ref[i * step : (i + 1) * step].reshape(step * ROWS, SIZE).astype(f32)
+        for h in range(2):
+            wide_ref[h, i * step * ROWS : (i + 1) * step * ROWS] = wide[:, h * HALF : (h + 1) * HALF]
+    for copy in edge_copies:
+        copy.wait()
+    edges = edge_ref[...]
     for b in range(ROWS):
         block = bond_slice(wide_ref, b)
         here = slice(b * SIZE, (b + 1) * SIZE)
@@ -95,7 +118,7 @@
     out_ref[...] = mm(flat.T, flat)
 
 
-def round_kernel(got_ref, after_ref, out_ref):
+def round_kernel(got_ref, after_ref, also_ref, out_ref):
     share = got_ref[0]
     for i in range(1, WIDTH):
         share = share + got_ref[i]
@@ -104,24 +127,24 @@
         out_ref[i] = share
 
 
-def slices(index_ref, env_ref, foreign_ref, out_ref):
-    rows = pl.ds(index_ref[0] * ROWS, ROWS)
-    own = env_ref[rows, :]
-    crossed = mm3(mm3(foreign_ref[rows, :], env_ref[...]), foreign_ref[...], NT)
+def slices(index_ref, place, env_ref, left, foreign, out_ref):
+    own = env_ref[pl.ds(index_ref[0] * ROWS, ROWS), :]
+    crossed = mm3(mm3(left, env_ref[...]), foreign, NT)
     for p in range(4):
-        which = index_ref[1] ^ p
+        which = index_ref[place] ^ p
         out_ref[p] = jnp.where(which == 3, crossed, jnp.where(which == 0, 0.0, own))
 
 
-def first_kernel(index_ref, own_ref, near_ref, couple_ref, foreign_ref, after_ref, env_ref, out_ref):
+def first_kernel(index_ref, own_ref, near_ref, couple_ref, foreign_ref, env_ref, out_ref):
     def whole(ref):
         return (ref[:, 0].astype(f32) + ref[:, 1].astype(f32)).reshape(SIZE, SIZE)
 
     env_ref[...] = 0.5 * (whole(own_ref) + sandwich(couple_ref[...], whole(near_ref)))
-    slices(index_ref, env_ref, foreign_ref, out_ref)
-
-
-def gradient_kernel(index_ref, iso_ref, edge_ref, near_ref, far_ref, norm_ref, after_ref, hi_ref, lo_ref, out_ref, wide_ref, moved_ref):
+    left = foreign_ref[pl.ds(index_ref[0] * ROWS, ROWS), :]
+    slices(index_ref, 1, env_ref, left, foreign_ref[...], out_ref)
+
+
+def gradient_kernel(index_ref, iso_ref, edge_ref, near_ref, far_ref, norm_ref, after_ref, hi_hbm, lo_hbm, out_ref, wide_ref, moved_ref, hi_ref, lo_ref, sems):
     odd = index_ref[2] == 1
 
     def whole(ref, k):
@@ -135,38 +158,52 @@
         moved = mm(mix, bond_slice(wide_ref, b))
         for h in range(2):
             moved_ref[h, pl.ds(b, SIZE, stride=ROWS), :] = moved[:, h * HALF : (h + 1) * HALF]
+    squares = []
     for h in range(2):
         columns = slice(h * HALF, (h + 1) * HALF)
-        hi, lo = split(moved_ref[h])
+        moved = moved_ref[h]
+        squares.append(jnp.sum(moved * moved, axis=0, keepdims=True))
+        hi, lo = split(moved)
         hi_ref[:, columns] = hi
         lo_ref[:, columns] = lo
+    copies = [
+        pltpu.make_async_copy(hi_ref, hi_hbm, sems.at[0]),
+        pltpu.make_async_copy(lo_ref, lo_hbm, sems.at[1]),
+    ]
+    for copy in copies:
+        copy.start()
     turned = iso_ref[...].reshape(FLAT, SIZE).T
-    part_q = mm(turned, hi_ref[...]) + mm(turned, lo_ref[...])
-    turned = hi_ref[...].T
-    cross = mm(turned, lo_ref[...])
-    part_r = mm(turned, hi_ref[...]) + (cross + cross.T)
+    part_q = mm(turned, hi_ref[...])
+    part_r = mm(hi_ref[...].T, hi_ref[...])
     part_n = norm_ref[...]
     row, col = iotas()
     diag_n = jnp.sum(jnp.where(row == col, part_n, 0.0), axis=0, keepdims=True)
-    diag_r = jnp.sum(jnp.where(row == col, part_r, 0.0), axis=0, keepdims=True)
+    diag_r = jnp.concatenate(squares, axis=1)
+    part_r = jnp.where(row == col, diag_r, part_r)
     nh, nl = split(diag_n)
     _, rl = split(diag_r)
     extra = jnp.concatenate(
-        [nh.astype(f32), nl.astype(f32), rl.astype(f32), jnp.zeros((ROWS - 3, SIZE), f32)], axis=0
+        [nh.astype(f32), nl.astype(f32), rl.astype(f32), jnp.zeros((EXTRA - 3, SIZE), f32)], axis=0
     ).astype(bf16)
     packed = jnp.where(row < col, part_n, part_r)
+    out_ref[:, :ROWS] = part_q.astype(bf16).reshape(WIDTH, ROWS, SIZE)
+    out_ref[:, ROWS : 2 * ROWS] = packed.astype(bf16).reshape(WIDTH, ROWS, SIZE)
     for i in range(WIDTH):
-        out_ref[i, :ROWS] = extra
-    out_ref[:, ROWS : 2 * ROWS] = part_q.astype(bf16).reshape(WIDTH, ROWS, SIZE)
-    out_ref[:, 2 * ROWS :] = packed.astype(bf16).reshape(WIDTH, ROWS, SIZE)
-
-
-def pack_kernel(got_ref, parts_ref, out_ref):
+        out_ref[i, 2 * ROWS :] = extra
+    for copy in copies:
+        copy.wait()
+
+
+def pack_kernel(got_ref, parts_ref, foreign_ref, out_ref):
     hi, lo = split((got_ref[0] + got_ref[1]) + (got_ref[2] + got_ref[3]))
+    foreign_hi, foreign_lo = split(foreign_ref[...])
     for i in range(WIDTH):
         out_ref[i, :ROWS] = hi
         out_ref[i, ROWS : 2 * ROWS] = lo
-    out_ref[:, 2 * ROWS :] = parts_ref[...]
+        out_ref[i, 4 * ROWS : 5 * ROWS] = foreign_hi
+        out_ref[i, 5 * ROWS : 6 * ROWS] = foreign_lo
+    out_ref[:, 2 * ROWS : 4 * ROWS] = parts_ref[:, : 2 * ROWS]
+    out_ref[:, 6 * ROWS :] = parts_ref[:, 2 * ROWS :]
 
 
 def repeat_kernel(got_ref, sums_ref, out_ref):
@@ -182,14 +219,24 @@
     return 0.25 * (env_ref[...] + sandwich(couple_ref[...], force.reshape(SIZE, SIZE)))
 
 
-def second_kernel(index_ref, got_ref, old_ref, couple_ref, foreign_ref, env_ref, out_ref, sums_ref, extra_ref):
+def second_kernel(index_ref, got_ref, old_ref, couple_ref, env_ref, out_ref, sums_ref, extra_ref):
     env_ref[...] = two_levels(old_ref, got_ref, couple_ref)
-    slices(index_ref, env_ref, foreign_ref, out_ref)
-    total = got_ref[0, 2 * ROWS :].astype(f32)
-    for i in range(1, WIDTH):
-        total = total + got_ref[i, 2 * ROWS :].astype(f32)
-    extra_ref[...] = total[:ROWS]
-    sums_ref[...] = total[ROWS:].astype(bf16)
+
+    def foreign(at):
+        hi, lo = slice(4 * ROWS, 5 * ROWS), slice(5 * ROWS, 6 * ROWS)
+        return got_ref[at, hi].astype(f32) + got_ref[at, lo].astype(f32)
+
+    left = foreign(index_ref[0])
+    slices(index_ref, 3, env_ref, left, foreign(slice(None)).reshape(SIZE, SIZE), out_ref)
+
+    def total(rows):
+        value = got_ref[0, rows].astype(f32)
+        for i in range(1, WIDTH):
+            value = value + got_ref[i, rows].astype(f32)
+        return value
+
+    extra_ref[...] = total(slice(6 * ROWS, 6 * ROWS + EXTRA))
+    sums_ref[...] = total(slice(2 * ROWS, 4 * ROWS)).astype(bf16)
 
 
 def polar_matrices(env, full_q, full_s, extra_ref):
@@ -226,10 +273,12 @@
         for k, part in enumerate((ph, ph, pl_, lh, ll)):
             map_ref[k * SIZE : (k + 1) * SIZE] = part
 
-    flat = iso_ref[...].reshape(-1, SIZE)
+    step = out_ref.shape[0]
+    here = pl.program_id(0) * step
+    flat = iso_ref[pl.ds(here, step)].reshape(-1, SIZE)
     hi = hi_ref[...]
     rows = jnp.concatenate([hi, lo_ref[...], hi, flat, flat], axis=1)
-    out_ref[...] = mm(rows, map_ref[...]).astype(bf16).reshape(iso_ref.shape)
+    out_ref[...] = mm(rows, map_ref[...]).astype(bf16).reshape(out_ref.shape)
 
 
 def exchange(x, axis, groups=None):
@@ -241,6 +290,7 @@
 
 
 square = ((SIZE, SIZE), f32)
+kept = pltpu.HBM((SIZE, SIZE), f32)
 sliced = ((4, ROWS, SIZE), f32)
 
 
@@ -250,26 +300,31 @@
         "ascend",
         [((WIDTH, 2, ROWS, SIZE), f32)],
         scratch=[
+            pltpu.VMEM((SIZE, ROWS, SIZE), bf16),
+            pltpu.VMEM((2 * SIZE, SIZE), bf16),
             pltpu.VMEM((2, FLAT, HALF), f32),
             pltpu.VMEM((SIZE, FLAT), bf16),
             pltpu.VMEM((2, FLAT, 2 * SIZE), bf16),
+            pltpu.SemaphoreType.DMA((CHUNKS + 2,)),
         ],
-        ins=3,
+        in_specs=[pl.BlockSpec(memory_space=pl.ANY)] * 3,
+        out_specs=[pl.BlockSpec(memory_space=pltpu.VMEM)],
+        grant=24,
         flops=6 << 29,
-    )(iso, left, right)[0]
+    )(in_hbm(iso), in_hbm(left), in_hbm(right))[0]
 
 
 def norms(iso, after):
     return call(norm_kernel, "norms", [square], ins=2, unread=1, flops=1 << 29)(iso, after)[0]
 
 
-def rounded(got, after):
-    return call(round_kernel, "rounded", [((WIDTH, 2, ROWS, SIZE), bf16)], ins=2, unread=1)(got, after)[0]
-
-
-def first(index, own, near, couple, foreign, after):
-    return call(first_kernel, "first", [square, sliced], ins=6, smem=1, unread=1)(
-        index, own, near, couple, foreign, after
+def rounded(got, *after):
+    return call(round_kernel, "rounded", [((WIDTH, 2, ROWS, SIZE), bf16)], ins=3, unread=2)(got, *after)[0]
+
+
+def first(index, own, near, couple, foreign):
+    return call(first_kernel, "first", [kept, sliced], ins=5, smem=1)(
+        index, own, near, couple, foreign
     )
 
 
@@ -277,31 +332,40 @@
     return call(
         gradient_kernel,
         "gradient",
-        [((FLAT, SIZE), bf16), ((FLAT, SIZE), bf16), ((WIDTH, 3 * ROWS, SIZE), bf16)],
-        scratch=[pltpu.VMEM((2, FLAT, HALF), f32), pltpu.VMEM((2, FLAT, HALF), f32)],
+        [pltpu.HBM((FLAT, SIZE), bf16), pltpu.HBM((FLAT, SIZE), bf16), ((WIDTH, 2 * ROWS + EXTRA, SIZE), bf16)],
+        scratch=[
+            pltpu.VMEM((2, FLAT, HALF), f32),
+            pltpu.VMEM((2, FLAT, HALF), f32),
+            pltpu.VMEM((FLAT, SIZE), bf16),
+            pltpu.VMEM((FLAT, SIZE), bf16),
+            pltpu.SemaphoreType.DMA((2,)),
+        ],
+        in_specs=[pl.BlockSpec(memory_space=pltpu.SMEM)] + [pl.BlockSpec(memory_space=pltpu.VMEM)] * 5 + [pl.BlockSpec(memory_space=pl.ANY)],
+        out_specs=[pl.BlockSpec(memory_space=pl.ANY)] * 2 + [pl.BlockSpec(memory_space=pltpu.VMEM)],
         ins=7,
         smem=1,
         unread=1,
-        flops=5 << 29,
-    )(index, iso, edge, near, far, norm, after)
-
-
-def pack(got, parts):
-    return call(pack_kernel, "pack", [((WIDTH, 5 * ROWS, SIZE), bf16)], ins=2)(got, parts)[0]
+        flops=3 << 29,
+        grant=28,
+    )(index, iso, in_hbm(edge), in_hbm(near), in_hbm(far), norm, after)
+
+
+def pack(got, parts, foreign):
+    return call(pack_kernel, "pack", [((WIDTH, 6 * ROWS + EXTRA, SIZE), bf16)], ins=3)(got, parts, foreign)[0]
 
 
 def repeat(got, sums):
     return call(repeat_kernel, "repeat", [((WIDTH, 4 * ROWS, SIZE), bf16)], ins=2)(got, sums)[0]
 
 
-def second(index, got, old, couple, foreign):
+def second(index, got, old, couple):
     return call(
         second_kernel,
         "second",
-        [square, sliced, ((2 * ROWS, SIZE), bf16), ((ROWS, SIZE), f32)],
-        ins=5,
+        [kept, sliced, ((2 * ROWS, SIZE), bf16), ((EXTRA, SIZE), f32)],
+        ins=4,
         smem=1,
-    )(index, got, old, couple, foreign)
+    )(index, got, in_hbm(old), couple)
 
 
 def final(got, extra, old, couple, iso, hi, lo, steps=4):
@@ -314,10 +378,10 @@
         [square, (iso.shape, bf16)],
         scratch=[pltpu.VMEM((5 * SIZE, SIZE), bf16)],
         grid=(steps,),
-        in_specs=[vmem] * 4 + [part, line, line],
+        in_specs=[vmem] * 5 + [line] * 2,
         out_specs=[vmem, part],
         flops=5 << 29,
-    )(got, extra, old, couple, iso, hi, lo)
+    )(got, extra, in_hbm(old), couple, iso, in_hbm(hi), in_hbm(lo))
 
 
 def body(iso, edge_left, edge_right, coupling):
@@ -325,15 +389,15 @@
     s = lax.axis_index("blk")
     j = lax.axis_index("bond")
     z = s // 2
-    index_1 = jnp.stack([j, z % 4, s % 2]).astype(jnp.int32)
-    index_2 = jnp.stack([j, z // 4, s % 2]).astype(jnp.int32)
+    index = jnp.stack([j, z % 4, s % 2, z // 4]).astype(jnp.int32)
 
     couple_1 = permuted(couple, "blk", lambda i: i ^ 2)
-    couple_2 = permuted(couple, "blk", lambda i: i ^ 8)
+    part_2 = lax.dynamic_slice_in_dim(couple, j * ROWS, ROWS, 0)
+    part_2 = permuted(part_2, "blk", lambda i: i ^ 8)
 
     blocks = ascend(iso, left, right)
     norm = norms(iso, blocks)
-    share = rounded(exchange(blocks, "bond"), norm)
+    share = rounded(exchange(blocks, "bond"), norm, part_2)
     own = exchange(share, "bond")
     near = permuted(own, "blk", lambda i: i ^ 1)
     far = permuted(own, "blk", lambda i: (i + 1) % 32 if i % 2 else (i - 1) % 32)
@@ -341,11 +405,11 @@
     quads = [[(zq * 4 + zl) * 2 + c for zl in range(4)] for zq in range(4) for c in range(2)]
     strides = [[(zh * 4 + zl) * 2 + c for zh in range(4)] for zl in range(4) for c in range(2)]
 
-    env, outgoing = first(index_1, own, near, couple, couple_1, couple_2)
+    env, outgoing = first(index, own, near, couple, couple_1)
     incoming = exchange(outgoing, "blk", quads)
-    moved_hi, moved_lo, parts = gradient(index_1, iso, left, near, far, norm, outgoing)
-    got = exchange(pack(incoming, parts), "bond")
-    env, outgoing, sums, extra = second(index_2, got, env, couple, couple_2)
+    moved_hi, moved_lo, parts = gradient(index, iso, left, near, far, norm, outgoing)
+    got = exchange(pack(incoming, parts, part_2), "bond")
+    env, outgoing, sums, extra = second(index, got, env, couple)
     incoming = exchange(outgoing, "blk", strides)
     got = exchange(repeat(incoming, sums), "bond")
     env, out = final(got, extra, env, couple, iso, moved_hi, moved_lo)

time: 150 us -> 129 us (0.86)
  waiting for transfers between devices: 36.4 us -> 6.62 us
  blocking collectives: 38.1 us -> 50.9 us
  local copies, waits for them, and re-layouts: 6.77 us -> 0.02 us
  Pallas kernels: 27.1 us -> 28.8 us
  starting transfers between devices: 39.9 us -> 41.4 us
    all_to_all x4 -> x3, waiting for transfers between devices: 23.1 us -> 5.68 us  [exchange(): return lax.all_to_all(x, axis, 0, 0, axis_index_groups=groups, tiled=True)]
    all_to_all x2 -> x3, blocking collectives: 38.1 us -> 50.9 us  [exchange(): return lax.all_to_all(x, axis, 0, 0, axis_index_groups=groups, tiled=True)]
    ppermute x4, waiting for transfers between devices: 13.3 us -> 0.94 us  [permuted(): lax.ppermute(x, axis, [(i, route(i)) for i in range(lax.axis_size(axis))])]
    unnamed x24 -> x6, local copies, waits for them, and re-layouts: 6.77 us -> 0.01 us
    pallas_call x1, Pallas kernels: 5.63 us -> 7.25 us  [ascend(): call(ascend_kernel, 'ascend', [((WIDTH, 2, ROWS, SIZE), f32)], scratch=[p...]
    all_to_all x4 -> x3, starting transfers between devices: 23.1 us -> 24.6 us  [exchange(): return lax.all_to_all(x, axis, 0, 0, axis_index_groups=groups, tiled=True)]
  transfers between devices with their start and end apart: 8 -> 7, of which waited for: 4 -> 3; matrix products, arithmetic and copies ran while one was open for 0% -> 0% of each run, Pallas kernels for 7% -> 8%
where the time goes in v2:
time: 129 us
  blocking collectives  50.9 us (39%)
  starting transfers between devices  41.4 us (32%)
  Pallas kernels  28.8 us (22%)
  waiting for transfers between devices  6.62 us (5%)
    all_to_all x3, blocking collectives, exchange(): return lax.all_to_all(x, axis, 0, 0, axis_index_groups=groups, tiled=True)  50.9 us
    all_to_all x3, starting transfers between devices, exchange(): return lax.all_to_all(x, axis, 0, 0, axis_index_groups=groups, tiled=True)  24.6 us
    ppermute x4, starting transfers between devices, permuted(): lax.ppermute(x, axis, [(i, route(i)) for i in range(lax.axis_size(axis))])  16.8 us
    pallas_call x1, Pallas kernels, final(): call(final_kernel, 'final', [square, (iso.shape, bf16)], scratch=[pltpu.V...  8.55 us
    pallas_call x1, Pallas kernels, ascend(): call(ascend_kernel, 'ascend', [((WIDTH, 2, ROWS, SIZE), f32)], scratch=[p...  7.25 us
    pallas_call x1, Pallas kernels, gradient(): call(gradient_kernel, 'gradient', [pltpu.HBM((FLAT, SIZE), bf16), pltpu.H...  7.02 us
    all_to_all x3, waiting for transfers between devices, exchange(): return lax.all_to_all(x, axis, 0, 0, axis_index_groups=groups, tiled=True)  5.68 us
  transfers between devices with their start and end apart: 7, of which 3 were waited for; matrix products, arithmetic and copies ran while one was open for 0% of the time, Pallas kernels for 8%

profile of v2, /device:TPU:64, one launch (start us, length us, event | category | flops | bytes accessed | tf_op | source)
XLA Modules:
  0.0 128.7 jit_solution(15492874103416055589)
XLA Ops:
  0.6 0.0 copy-start.1
  0.6 0.0 copy-start
  0.6 7.3 %ascend.1.after_ref = f32[16,2,16,256]{3,2,1,0:T(8,128)} custom-call(bf16[256,16,256]{2,1,0:T(8,128)(2,1)} %bitcast.12, bf16[256,256]{1,0:T(8,128)(2,1)} %bitcast.21, bf16[256,256]{1,0:T(8,128)(2,1)} %bitcast.20), custom_call_target="tpu_custom_call" | custom-call | flops 3221225472 | bytes 4194304 | tf_op jit(solution)/shard_map/ascend/pallas_call | solution.py:298
  7.9 7.0 %all-to-all-start = ((f32[16,2,16,256]{3,2,1,0:T(8,128)}), f32[16,2,16,256]{3,2,1,0:T(8,128)S(1)}, u32[]{:S(2)}, u32[]{:S(2)}) async-start(f32[16,2,16,256]{3,2,1,0:T(8,128)} %ascend.1.after_ref), calls=%async_computation | async-start | bytes 1048576 | tf_op jit(solution)/shard_map/all_to_all | solution.py:285
  15.0 0.0 copy-done.1
  15.0 9.1 %collective-permute-start = (f32[16,256]{1,0:T(8,128)S(1)}, f32[16,256]{1,0:T(8,128)S(1)}, u32[]{:S(2)}, u32[]{:S(2)}) collective-permute-start(f32[16,256]{1,0:T(8,128)S(1)} %dynamic-slice_bitcast_fusion), channel_id=1, source_target_pairs={{0,128},{16,144},{32,160},{48,176},{64,192},{80,208},{96,224},{112... | collective-permute-start | bytes 49160 | tf_op jit(solution)/shard_map/ppermute | solution.py:289
  24.1 0.0 copy-done
  24.1 0.8 norms.1.after_ref.norm_ref
  24.9 0.9 collective-permute-done.also_ref.foreign_ref
  25.8 0.7 all-to-all-done.got_ref
  26.5 0.7 rounded.1
  27.2 6.6 %all-to-all-start.1 = ((bf16[16,2,16,256]{3,2,1,0:T(8,128)(2,1)}), bf16[16,2,16,256]{3,2,1,0:T(8,128)(2,1)S(1)}, u32[]{:S(2)}, u32[]{:S(2)}) async-start(bf16[16,2,16,256]{3,2,1,0:T(8,128)(2,1)} %rounded.1), calls=%async_computation.1 | async-start | bytes 524288 | tf_op jit(solution)/shard_map/all_to_all | solution.py:285
  33.9 3.7 %collective-permute-start.2 = (f32[256,256]{1,0:T(8,128)S(1)}, f32[256,256]{1,0:T(8,128)S(1)}, u32[]{:S(2)}, u32[]{:S(2)}) collective-permute-start(f32[256,256]{1,0:T(8,128)S(1)} %bitcast.16), channel_id=1, source_target_pairs={{0,32},{16,48},{32,0},{48,16},{64,96},{80,112},{96,64},{112,80},{1... | collective-permute-start | bytes 786440 | tf_op jit(solution)/shard_map/ppermute | solution.py:289
  37.6 5.0 %all-to-all-done.1.own_ref = bf16[16,2,16,256]{3,2,1,0:T(8,128)(2,1)S(1)} async-done(((bf16[16,2,16,256]{3,2,1,0:T(8,128)(2,1)}), bf16[16,2,16,256]{3,2,1,0:T(8,128)(2,1)S(1)}, u32[]{:S(2)}, u32[]{:S(2)}) %all-to-all-start.1) | async-done | bytes 262176 | tf_op jit(solution)/shard_map/all_to_all | solution.py:285
  42.6 1.9 %collective-permute-start.1 = (bf16[16,2,16,256]{3,2,1,0:T(8,128)(2,1)S(1)}, bf16[16,2,16,256]{3,2,1,0:T(8,128)(2,1)S(1)}, u32[]{:S(2)}, u32[]{:S(2)}) collective-permute-start(bf16[16,2,16,256]{3,2,1,0:T(8,128)(2,1)S(1)} %all-to-all-done.1.own_ref), channel_id=1, source_target_pairs={{0,16},{16,0},{32,48},{48,32},{64,80},{80,64},{96,112},{112,96},{1... | collective-permute-start | bytes 786440 | tf_op jit(solution)/shard_map/ppermute | solution.py:289
  44.5 2.1 %collective-permute-start.3 = (bf16[16,2,16,256]{3,2,1,0:T(8,128)(2,1)S(1)}, bf16[16,2,16,256]{3,2,1,0:T(8,128)(2,1)}, u32[]{:S(2)}, u32[]{:S(2)}) collective-permute-start(bf16[16,2,16,256]{3,2,1,0:T(8,128)(2,1)S(1)} %all-to-all-done.1.own_ref), channel_id=1, source_target_pairs={{0,496},{16,32},{32,16},{48,64},{64,48},{80,96},{96,80},{112,128},... | collective-permute-start | bytes 786440 | tf_op jit(solution)/shard_map/ppermute | solution.py:289
  46.7 0.1 pad_add_fusion.index_ref
  46.7 0.0 collective-permute-done.2.foreign_ref
  46.7 0.0 collective-permute-done.1.near_ref
  46.7 0.0 copy-start.2
  46.7 2.2 %first.1 = (f32[256,256]{1,0:T(8,128)}, f32[4,16,256]{2,1,0:T(8,128)}) custom-call(s32[4]{0:T(128)S(1)} %pad_add_fusion.index_ref, bf16[16,2,16,256]{3,2,1,0:T(8,128)(2,1)S(1)} %all-to-all-done.1.own_ref, bf16[16,2,16,256]{3,2,1,0:T(8,128)(2,1)S(1)} %collective-permute-done.1.near_ref, f32[256,256]{1,0:T(8,128)S(1)} %bitcast.17, ...), custom_call_target="tpu_custom_call" | custom-call | bytes 4194304 | tf_op jit(solution)/shard_map/first/pallas_call | solution.py:326
  48.9 10.9 %all-to-all-start.2 = ((f32[4,16,256]{2,1,0:T(8,128)}), f32[4,16,256]{2,1,0:T(8,128)S(1)}, u32[]{:S(2)}, u32[]{:S(2)}) async-start(f32[4,16,256]{2,1,0:T(8,128)} %get-tuple-element.13.after_ref), calls=%async_computation.2 | async-start | bytes 131072 | tf_op jit(solution)/shard_map/all_to_all | solution.py:285
  59.9 0.0 collective-permute-done.3.far_ref
  59.9 0.0 copy-done.2
  59.9 7.0 %gradient.1 = (bf16[4096,256]{1,0:T(8,128)(2,1)}, bf16[4096,256]{1,0:T(8,128)(2,1)}, bf16[16,40,256]{2,1,0:T(8,128)(2,1)S(1)}) custom-call(s32[4]{0:T(128)S(1)} %pad_add_fusion.index_ref, bf16[256,16,256]{2,1,0:T(8,128)(2,1)S(1)} %bitcast.14, bf16[256,256]{1,0:T(8,128)(2,1)} %bitcast.22, bf16[16,2,16,256]{3,2,1,0:T(8,128)(2,1)} %copy-done.2, ...), custom_call_target="tpu_custom_call" | custom-call | flops 1610612736 | bytes 4194304 | tf_op jit(solution)/shard_map/gradient/pallas_call | solution.py:332
  66.9 0.0 all-to-all-done.2.got_ref
  66.9 0.1 pack.1
  67.0 14.8 %all_to_all.30.got_ref = bf16[16,104,256]{2,1,0:T(8,128)(2,1)S(1)} all-to-all(bf16[16,104,256]{2,1,0:T(8,128)(2,1)S(1)} %pack.1), channel_id=1, replica_groups=mesh['blk'=32,'bond'=16] {'bond'}, dimensions={0} | all-to-all | bytes 1703936 | tf_op jit(solution)/shard_map/all_to_all | solution.py:285
  81.8 2.2 %second.1 = (f32[256,256]{1,0:T(8,128)}, f32[4,16,256]{2,1,0:T(8,128)S(1)}, bf16[32,256]{1,0:T(8,128)(2,1)S(1)}, f32[8,256]{1,0:T(8,128)S(1)}) custom-call(s32[4]{0:T(128)S(1)} %pad_add_fusion.index_ref, bf16[16,104,256]{2,1,0:T(8,128)(2,1)S(1)} %all_to_all.30.got_ref, f32[256,256]{1,0:T(8,128)} %get-tuple-element.15.old_ref, f32[256,256]{1,0:T(8,128)S(1)} %bitcast.18), custom_call_target="tpu_custom_call" | custom-call | bytes 4194304 | tf_op jit(solution)/shard_map/second/pallas_call | solution.py:362
  84.0 22.9 %all_to_all.31.got_ref = f32[4,16,256]{2,1,0:T(8,128)S(1)} all-to-all(f32[4,16,256]{2,1,0:T(8,128)S(1)} %get-tuple-element.16), channel_id=1, replica_groups={{0,128,256,384},{16,144,272,400},{32,160,288,416},{48,176,304,432},{64,..., dimensions={0} | all-to-all | bytes 131072 | tf_op jit(solution)/shard_map/all_to_all | solution.py:285
  106.9 13.2 %all_to_all.32.got_ref = bf16[16,64,256]{2,1,0:T(8,128)(2,1)S(1)} all-to-all(bf16[16,64,256]{2,1,0:T(8,128)(2,1)S(1)} %repeat.1), channel_id=1, replica_groups=mesh['blk'=32,'bond'=16] {'bond'}, dimensions={0} | all-to-all | bytes 1048576 | tf_op jit(solution)/shard_map/all_to_all | solution.py:285
  120.1 8.6 %final.1 = (f32[256,256]{1,0:T(8,128)}, bf16[256,16,256]{2,1,0:T(8,128)(2,1)}) custom-call(bf16[16,64,256]{2,1,0:T(8,128)(2,1)S(1)} %all_to_all.32.got_ref, f32[8,256]{1,0:T(8,128)S(1)} %get-tuple-element.18.extra_ref, f32[256,256]{1,0:T(8,128)} %get-tuple-element.19.old_ref, f32[256,256]{1,0:T(8,128)S(1)} %bitcast.19, bf16[256,16,256]{2,1,0:T(8,128)(2,1)S(1)} %bitcast.15, ...), custom_call_target="tpu_custom_call" | custom-call | flops 2684354560 | bytes 4194304 | tf_op jit(solution)/shard_map/final/pallas_call | solution.py:375
  (2 shorter events, 0.0 us)
Async XLA Ops:
  0.6 14.3 %copy-start.1 = (f32[1,256,256]{2,1,0:T(8,128)S(1)}, f32[1,256,256]{2,1,0:T(8,128)}, u32[]{:S(2)}) copy-start(f32[1,256,256]{2,1,0:T(8,128)} %param.7) | copy-start | bytes 786436
  0.6 23.4 %copy-start = (bf16[1,256,16,256]{3,2,1,0:T(8,128)(2,1)S(1)}, bf16[1,256,16,256]{3,2,1,0:T(8,128)(2,1)}, u32[]{:S(2)}) copy-start(bf16[1,256,16,256]{3,2,1,0:T(8,128)(2,1)} %param.4) | copy-start | bytes 6291460
  7.9 18.6 %all-to-all-start = ((f32[16,2,16,256]{3,2,1,0:T(8,128)}), f32[16,2,16,256]{3,2,1,0:T(8,128)S(1)}, u32[]{:S(2)}, u32[]{:S(2)}) async-start(f32[16,2,16,256]{3,2,1,0:T(8,128)} %ascend.1.after_ref), calls=%async_computation | async-start | bytes 1048576 | tf_op jit(solution)/shard_map/all_to_all | solution.py:285
  15.0 10.8 %collective-permute-start = (f32[16,256]{1,0:T(8,128)S(1)}, f32[16,256]{1,0:T(8,128)S(1)}, u32[]{:S(2)}, u32[]{:S(2)}) collective-permute-start(f32[16,256]{1,0:T(8,128)S(1)} %dynamic-slice_bitcast_fusion), channel_id=1, source_target_pairs={{0,128},{16,144},{32,160},{48,176},{64,192},{80,208},{96,224},{112... | collective-permute-start | bytes 49160 | tf_op jit(solution)/shard_map/ppermute | solution.py:289
  27.2 15.3 %all-to-all-start.1 = ((bf16[16,2,16,256]{3,2,1,0:T(8,128)(2,1)}), bf16[16,2,16,256]{3,2,1,0:T(8,128)(2,1)S(1)}, u32[]{:S(2)}, u32[]{:S(2)}) async-start(bf16[16,2,16,256]{3,2,1,0:T(8,128)(2,1)} %rounded.1), calls=%async_computation.1 | async-start | bytes 524288 | tf_op jit(solution)/shard_map/all_to_all | solution.py:285
  33.9 12.9 %collective-permute-start.2 = (f32[256,256]{1,0:T(8,128)S(1)}, f32[256,256]{1,0:T(8,128)S(1)}, u32[]{:S(2)}, u32[]{:S(2)}) collective-permute-start(f32[256,256]{1,0:T(8,128)S(1)} %bitcast.16), channel_id=1, source_target_pairs={{0,32},{16,48},{32,0},{48,16},{64,96},{80,112},{96,64},{112,80},{1... | collective-permute-start | bytes 786440 | tf_op jit(solution)/shard_map/ppermute | solution.py:289
  42.6 4.2 %collective-permute-start.1 = (bf16[16,2,16,256]{3,2,1,0:T(8,128)(2,1)S(1)}, bf16[16,2,16,256]{3,2,1,0:T(8,128)(2,1)S(1)}, u32[]{:S(2)}, u32[]{:S(2)}) collective-permute-start(bf16[16,2,16,256]{3,2,1,0:T(8,128)(2,1)S(1)} %all-to-all-done.1.own_ref), channel_id=1, source_target_pairs={{0,16},{16,0},{32,48},{48,32},{64,80},{80,64},{96,112},{112,96},{1... | collective-permute-start | bytes 786440 | tf_op jit(solution)/shard_map/ppermute | solution.py:289
  44.5 15.4 %collective-permute-start.3 = (bf16[16,2,16,256]{3,2,1,0:T(8,128)(2,1)S(1)}, bf16[16,2,16,256]{3,2,1,0:T(8,128)(2,1)}, u32[]{:S(2)}, u32[]{:S(2)}) collective-permute-start(bf16[16,2,16,256]{3,2,1,0:T(8,128)(2,1)S(1)} %all-to-all-done.1.own_ref), channel_id=1, source_target_pairs={{0,496},{16,32},{32,16},{48,64},{64,48},{80,96},{96,80},{112,128},... | collective-permute-start | bytes 786440 | tf_op jit(solution)/shard_map/ppermute | solution.py:289
  46.7 13.1 %copy-start.2 = (bf16[16,2,16,256]{3,2,1,0:T(8,128)(2,1)}, bf16[16,2,16,256]{3,2,1,0:T(8,128)(2,1)S(1)}, u32[]{:S(2)}) copy-start(bf16[16,2,16,256]{3,2,1,0:T(8,128)(2,1)S(1)} %collective-permute-done.1.near_ref) | copy-start | bytes 786436
  48.9 18.0 %all-to-all-start.2 = ((f32[4,16,256]{2,1,0:T(8,128)}), f32[4,16,256]{2,1,0:T(8,128)S(1)}, u32[]{:S(2)}, u32[]{:S(2)}) async-start(f32[4,16,256]{2,1,0:T(8,128)} %get-tuple-element.13.after_ref), calls=%async_computation.2 | async-start | bytes 131072 | tf_op jit(solution)/shard_map/all_to_all | solution.py:285

commit v3 on v2

--- a/solution.py
+++ b/solution.py
@@ -16,6 +16,7 @@
 HALF = 128
 CHUNKS = 4
 EXTRA = 8
+PARTS = 8
 
 
 def split(x):
@@ -48,13 +49,14 @@
 
 def call(kernel, name, outs, scratch=(), smem=0, unread=0, ins=0, flops=0, grant=16, grid=None, in_specs=None, out_specs=None):
     vmem = pl.BlockSpec(memory_space=pltpu.VMEM)
+    any_place = pl.BlockSpec(memory_space=pl.ANY)
     if in_specs is None:
         in_specs = (
             [pl.BlockSpec(memory_space=pltpu.SMEM)] * smem
             + [vmem] * (ins - smem - unread)
-            + [pl.BlockSpec(memory_space=pl.ANY)] * unread
+            + [any_place] * unread
         )
-        out_specs = [vmem] * len(outs)
+        out_specs = [any_place if isinstance(o, pl.MemoryRef) else vmem for o in outs]
     params = dict(grid=grid) if grid else {}
     return pl.pallas_call(
         kernel,
@@ -113,9 +115,22 @@
         out_ref[:, k] = total[:, k * SIZE : (k + 1) * SIZE].reshape(WIDTH, ROWS, SIZE)
 
 
-def norm_kernel(iso_ref, after_ref, out_ref):
-    flat = iso_ref[...].reshape(FLAT, SIZE)
-    out_ref[...] = mm(flat.T, flat)
+def prepare_kernel(iso_ref, after_ref, block_hbm, turned_hbm, norm_ref, wide_ref, block_ref, turned_ref, sems):
+    spread_rows(iso_ref, wide_ref)
+    for b in range(ROWS):
+        block = bond_slice(wide_ref, b)
+        here = slice(b * SIZE, (b + 1) * SIZE)
+        block_ref[here] = block
+        turned_ref[:, here] = block.T
+    copies = [
+        pltpu.make_async_copy(block_ref, block_hbm, sems.at[0]),
+        pltpu.make_async_copy(turned_ref, turned_hbm, sems.at[1]),
+    ]
+    for copy in copies:
+        copy.start()
+    norm_ref[...] = mm(turned_ref[...], block_ref[...])
+    for copy in copies:
+        copy.wait()
 
 
 def round_kernel(got_ref, after_ref, also_ref, out_ref):
@@ -135,16 +150,27 @@
         out_ref[p] = jnp.where(which == 3, crossed, jnp.where(which == 0, 0.0, own))
 
 
-def first_kernel(index_ref, own_ref, near_ref, couple_ref, foreign_ref, env_ref, out_ref):
+def first_kernel(index_ref, own_ref, near_ref, couple_ref, foreign_ref, env_hbm, out_ref, env_ref, sem):
     def whole(ref):
         return (ref[:, 0].astype(f32) + ref[:, 1].astype(f32)).reshape(SIZE, SIZE)
 
     env_ref[...] = 0.5 * (whole(own_ref) + sandwich(couple_ref[...], whole(near_ref)))
+    copy = pltpu.make_async_copy(env_ref, env_hbm, sem)
+    copy.start()
     left = foreign_ref[pl.ds(index_ref[0] * ROWS, ROWS), :]
     slices(index_ref, 1, env_ref, left, foreign_ref[...], out_ref)
-
-
-def gradient_kernel(index_ref, iso_ref, edge_ref, near_ref, far_ref, norm_ref, after_ref, hi_hbm, lo_hbm, out_ref, wide_ref, moved_ref, hi_ref, lo_ref, sems):
+    copy.wait()
+
+
+def gradient_kernel(index_ref, edge_ref, near_ref, far_ref, norm_ref, block_hbm, turned_hbm, after_ref, mix_ref, out_ref, moved_ref, flipped_ref, block_ref, turned_ref, sems):
+    copies = []
+    step = FLAT // CHUNKS
+    for i in range(CHUNKS):
+        here = pl.ds(i * step, step)
+        copies.append(pltpu.make_async_copy(block_hbm.at[here], block_ref.at[here], sems.at[2 * i]))
+        copies.append(pltpu.make_async_copy(turned_hbm.at[:, here], turned_ref.at[:, here], sems.at[2 * i + 1]))
+    for copy in copies:
+        copy.start()
     odd = index_ref[2] == 1
 
     def whole(ref, k):
@@ -153,32 +179,24 @@
     from_left = jnp.where(odd, whole(near_ref, 1), whole(far_ref, 1))
     from_right = jnp.where(odd, whole(far_ref, 0), whole(near_ref, 0))
     mix = (edge_ref[...].astype(f32) + from_left + from_right).astype(bf16)
-    spread_rows(iso_ref, wide_ref)
+    mix_ref[...] = mix
+    squares = jnp.zeros((8, SIZE), f32)
     for b in range(ROWS):
-        moved = mm(mix, bond_slice(wide_ref, b))
-        for h in range(2):
-            moved_ref[h, pl.ds(b, SIZE, stride=ROWS), :] = moved[:, h * HALF : (h + 1) * HALF]
-    squares = []
-    for h in range(2):
-        columns = slice(h * HALF, (h + 1) * HALF)
-        moved = moved_ref[h]
-        squares.append(jnp.sum(moved * moved, axis=0, keepdims=True))
-        hi, lo = split(moved)
-        hi_ref[:, columns] = hi
-        lo_ref[:, columns] = lo
-    copies = [
-        pltpu.make_async_copy(hi_ref, hi_hbm, sems.at[0]),
-        pltpu.make_async_copy(lo_ref, lo_hbm, sems.at[1]),
-    ]
-    for copy in copies:
-        copy.start()
-    turned = iso_ref[...].reshape(FLAT, SIZE).T
-    part_q = mm(turned, hi_ref[...])
-    part_r = mm(hi_ref[...].T, hi_ref[...])
+        if b % (ROWS // CHUNKS) == 0:
+            at = 2 * b // (ROWS // CHUNKS)
+            copies[at].wait()
+            copies[at + 1].wait()
+        here = slice(b * SIZE, (b + 1) * SIZE)
+        moved = mm(mix, block_ref[here])
+        squares = squares + jnp.sum((moved * moved).reshape(SIZE // 8, 8, SIZE), axis=0)
+        moved_ref[here] = moved.astype(bf16)
+        flipped_ref[:, here] = mm(turned_ref[:, here], mix, NT).astype(bf16)
+    part_q = mm(turned_ref[...], moved_ref[...])
+    part_r = mm(flipped_ref[...], moved_ref[...])
     part_n = norm_ref[...]
     row, col = iotas()
     diag_n = jnp.sum(jnp.where(row == col, part_n, 0.0), axis=0, keepdims=True)
-    diag_r = jnp.concatenate(squares, axis=1)
+    diag_r = jnp.sum(squares, axis=0, keepdims=True)
     part_r = jnp.where(row == col, diag_r, part_r)
     nh, nl = split(diag_n)
     _, rl = split(diag_r)
@@ -190,6 +208,25 @@
     out_ref[:, ROWS : 2 * ROWS] = packed.astype(bf16).reshape(WIDTH, ROWS, SIZE)
     for i in range(WIDTH):
         out_ref[i, 2 * ROWS :] = extra
+
+
+def lines_kernel(mix_ref, block_ref, after_ref, hi_hbm, lo_hbm, moved_ref, hi_ref, lo_ref, sems):
+    mix = mix_ref[...]
+    for b in range(ROWS):
+        moved = mm(mix, block_ref[b * SIZE : (b + 1) * SIZE])
+        for h in range(2):
+            moved_ref[h, pl.ds(b, SIZE, stride=ROWS), :] = moved[:, h * HALF : (h + 1) * HALF]
+    for h in range(2):
+        columns = slice(h * HALF, (h + 1) * HALF)
+        hi, lo = split(moved_ref[h])
+        hi_ref[:, columns] = hi
+        lo_ref[:, columns] = lo
+    copies = [
+        pltpu.make_async_copy(hi_ref, hi_hbm, sems.at[0]),
+        pltpu.make_async_copy(lo_ref, lo_hbm, sems.at[1]),
+    ]
+    for copy in copies:
+        copy.start()
     for copy in copies:
         copy.wait()
 
@@ -206,7 +243,7 @@
     out_ref[:, 6 * ROWS :] = parts_ref[:, 2 * ROWS :]
 
 
-def repeat_kernel(got_ref, sums_ref, out_ref):
+def repeat_kernel(got_ref, sums_ref, after_ref, out_ref):
     hi, lo = split((got_ref[0] + got_ref[1]) + (got_ref[2] + got_ref[3]))
     for i in range(WIDTH):
         out_ref[i, :ROWS] = hi
@@ -219,8 +256,10 @@
     return 0.25 * (env_ref[...] + sandwich(couple_ref[...], force.reshape(SIZE, SIZE)))
 
 
-def second_kernel(index_ref, got_ref, old_ref, couple_ref, env_ref, out_ref, sums_ref, extra_ref):
+def second_kernel(index_ref, got_ref, old_ref, couple_ref, env_hbm, out_ref, sums_ref, extra_ref, env_ref, sem):
     env_ref[...] = two_levels(old_ref, got_ref, couple_ref)
+    copy = pltpu.make_async_copy(env_ref, env_hbm, sem)
+    copy.start()
 
     def foreign(at):
         hi, lo = slice(4 * ROWS, 5 * ROWS), slice(5 * ROWS, 6 * ROWS)
@@ -237,48 +276,69 @@
 
     extra_ref[...] = total(slice(6 * ROWS, 6 * ROWS + EXTRA))
     sums_ref[...] = total(slice(2 * ROWS, 4 * ROWS)).astype(bf16)
+    copy.wait()
+
+
+def mm2(a, b, dims=NN):
+    ah, al = split(a)
+    return mm(ah, b, dims) + mm(al, b, dims)
 
 
 def polar_matrices(env, full_q, full_s, extra_ref):
     row, col = iotas()
-    top = env.astype(bf16).astype(f32)
+    on = row == col
+    top = env.astype(bf16)
     lower = jnp.where(row > col, full_s, 0.0)
     upper = jnp.where(row < col, full_s, 0.0)
-    diag_n = extra_ref[0:1, :] + extra_ref[1:2, :]
-    full_n = upper + upper.T + jnp.where(row == col, diag_n, 0.0)
-    full_r = lower + lower.T + jnp.where(row == col, full_s + extra_ref[2:3, :], 0.0)
-    half = full_q + 0.5 * mm3(full_n, top)
-    side = mm3(top.T, half)
+    full_n = upper + upper.T + jnp.where(on, extra_ref[0:1, :] + extra_ref[1:2, :], 0.0)
+    full_r = lower + lower.T + jnp.where(on, full_s + extra_ref[2:3, :], 0.0)
+    half = full_q + 0.5 * mm2(full_n, top)
+    hh, hl = split(half)
+    turned = top.T
+    side = mm(turned, hh) + mm(turned, hl)
     gram = full_r + side + side.T
-    trace = jnp.sum(jnp.where(row == col, gram, 0.0), keepdims=True)
+    trace = jnp.sum(jnp.where(on, gram, 0.0), keepdims=True)
     factor = lax.rsqrt(trace + 1e-06)
     g = gram * (factor * factor)
     g2 = mm3(g, g)
-    eye = jnp.where(row == col, 1.0, 0.0)
+    eye = jnp.where(on, 1.0, 0.0)
     poly = 2.25 * eye - 2.4375 * g + mm3(g2, 1.6875 * eye - 0.5625 * g + 0.0625 * g2)
     poly = poly * factor
-    return poly, mm3(top, poly)
-
-
-def final_kernel(got_ref, extra_ref, old_ref, couple_ref, iso_ref, hi_ref, lo_ref, env_ref, out_ref, map_ref):
-    @pl.when(pl.program_id(0) == 0)
-    def _():
-        env = two_levels(old_ref, got_ref, couple_ref)
-        env_ref[...] = env
-        full_q = got_ref[:, 2 * ROWS : 3 * ROWS].astype(f32).reshape(SIZE, SIZE)
-        full_s = got_ref[:, 3 * ROWS :].astype(f32).reshape(SIZE, SIZE)
-        poly, low = polar_matrices(env, full_q, full_s, extra_ref)
-        ph, pl_ = split(poly)
-        lh, ll = split(low)
-        for k, part in enumerate((ph, ph, pl_, lh, ll)):
-            map_ref[k * SIZE : (k + 1) * SIZE] = part
-
-    step = out_ref.shape[0]
-    here = pl.program_id(0) * step
-    flat = iso_ref[pl.ds(here, step)].reshape(-1, SIZE)
-    hi = hi_ref[...]
-    rows = jnp.concatenate([hi, lo_ref[...], hi, flat, flat], axis=1)
-    out_ref[...] = mm(rows, map_ref[...]).astype(bf16).reshape(out_ref.shape)
+    ph, pl_ = split(poly)
+    return ph, pl_, mm(top, ph) + mm(top, pl_)
+
+
+def final_kernel(got_ref, extra_ref, old_ref, couple_ref, iso_ref, hi_hbm, lo_hbm, env_hbm, out_hbm, map_ref, hi_ref, lo_ref, env_ref, out_ref, sems):
+    incoming = [
+        pltpu.make_async_copy(hi_hbm, hi_ref, sems.at[0]),
+        pltpu.make_async_copy(lo_hbm, lo_ref, sems.at[1]),
+    ]
+    for copy in incoming:
+        copy.start()
+    env = two_levels(old_ref, got_ref, couple_ref)
+    env_ref[...] = env
+    outgoing = [pltpu.make_async_copy(env_ref, env_hbm, sems.at[2])]
+    outgoing[0].start()
+    full_q = got_ref[:, 2 * ROWS : 3 * ROWS].astype(f32).reshape(SIZE, SIZE)
+    full_s = got_ref[:, 3 * ROWS :].astype(f32).reshape(SIZE, SIZE)
+    ph, pl_, low = polar_matrices(env, full_q, full_s, extra_ref)
+    for k, part in enumerate((ph, ph, pl_, *split(low))):
+        map_ref[k * SIZE : (k + 1) * SIZE] = part
+    for copy in incoming:
+        copy.wait()
+    step = SIZE // PARTS
+    for i in range(PARTS):
+        here = pl.ds(i * step, step)
+        lines = pl.ds(i * step * ROWS, step * ROWS)
+        flat = iso_ref[here].reshape(-1, SIZE)
+        hi = hi_ref[lines]
+        rows = jnp.concatenate([hi, lo_ref[lines], hi, flat, flat], axis=1)
+        out_ref[here] = mm(rows, map_ref[...]).astype(bf16).reshape(step, ROWS, SIZE)
+        copy = pltpu.make_async_copy(out_ref.at[here], out_hbm.at[here], sems.at[3 + i])
+        copy.start()
+        outgoing.append(copy)
+    for copy in outgoing:
+        copy.wait()
 
 
 def exchange(x, axis, groups=None):
@@ -291,6 +351,7 @@
 
 square = ((SIZE, SIZE), f32)
 kept = pltpu.HBM((SIZE, SIZE), f32)
+held = [pltpu.VMEM((SIZE, SIZE), f32), pltpu.SemaphoreType.DMA]
 sliced = ((4, ROWS, SIZE), f32)
 
 
@@ -314,8 +375,21 @@
     )(in_hbm(iso), in_hbm(left), in_hbm(right))[0]
 
 
-def norms(iso, after):
-    return call(norm_kernel, "norms", [square], ins=2, unread=1, flops=1 << 29)(iso, after)[0]
+def prepare(iso, after):
+    return call(
+        prepare_kernel,
+        "prepare",
+        [pltpu.HBM((FLAT, SIZE), bf16), pltpu.HBM((SIZE, FLAT), bf16), square],
+        scratch=[
+            pltpu.VMEM((2, FLAT, HALF), f32),
+            pltpu.VMEM((FLAT, SIZE), bf16),
+            pltpu.VMEM((SIZE, FLAT), bf16),
+            pltpu.SemaphoreType.DMA((2,)),
+        ],
+        ins=2,
+        unread=1,
+        flops=1 << 29,
+    )(iso, after)
 
 
 def rounded(got, *after):
@@ -323,39 +397,57 @@
 
 
 def first(index, own, near, couple, foreign):
-    return call(first_kernel, "first", [kept, sliced], ins=5, smem=1)(
+    return call(first_kernel, "first", [kept, sliced], scratch=held, ins=5, smem=1)(
         index, own, near, couple, foreign
     )
 
 
-def gradient(index, iso, edge, near, far, norm, after):
+def gradient(index, block, turned, edge, near, far, norm, after):
     return call(
         gradient_kernel,
         "gradient",
-        [pltpu.HBM((FLAT, SIZE), bf16), pltpu.HBM((FLAT, SIZE), bf16), ((WIDTH, 2 * ROWS + EXTRA, SIZE), bf16)],
+        [((SIZE, SIZE), bf16), ((WIDTH, 2 * ROWS + EXTRA, SIZE), bf16)],
+        scratch=[
+            pltpu.VMEM((FLAT, SIZE), bf16),
+            pltpu.VMEM((SIZE, FLAT), bf16),
+            pltpu.VMEM((FLAT, SIZE), bf16),
+            pltpu.VMEM((SIZE, FLAT), bf16),
+            pltpu.SemaphoreType.DMA((2 * CHUNKS,)),
+        ],
+        ins=8,
+        smem=1,
+        unread=3,
+        flops=4 << 29,
+        grant=20,
+    )(index, in_hbm(edge), in_hbm(near), in_hbm(far), norm, in_hbm(block), in_hbm(turned), after)
+
+
+def lines(mix, block, after):
+    return call(
+        lines_kernel,
+        "lines",
+        [pltpu.HBM((FLAT, SIZE), bf16), pltpu.HBM((FLAT, SIZE), bf16)],
         scratch=[
             pltpu.VMEM((2, FLAT, HALF), f32),
-            pltpu.VMEM((2, FLAT, HALF), f32),
             pltpu.VMEM((FLAT, SIZE), bf16),
             pltpu.VMEM((FLAT, SIZE), bf16),
             pltpu.SemaphoreType.DMA((2,)),
         ],
-        in_specs=[pl.BlockSpec(memory_space=pltpu.SMEM)] + [pl.BlockSpec(memory_space=pltpu.VMEM)] * 5 + [pl.BlockSpec(memory_space=pl.ANY)],
-        out_specs=[pl.BlockSpec(memory_space=pl.ANY)] * 2 + [pl.BlockSpec(memory_space=pltpu.VMEM)],
-        ins=7,
-        smem=1,
-        unread=1,
-        flops=3 << 29,
-        grant=28,
-    )(index, iso, in_hbm(edge), in_hbm(near), in_hbm(far), norm, after)
+        in_specs=[pl.BlockSpec(memory_space=pltpu.VMEM)] * 2 + [pl.BlockSpec(memory_space=pl.ANY)],
+        out_specs=[pl.BlockSpec(memory_space=pl.ANY)] * 2,
+        flops=1 << 29,
+        grant=20,
+    )(mix, block, after)
 
 
 def pack(got, parts, foreign):
     return call(pack_kernel, "pack", [((WIDTH, 6 * ROWS + EXTRA, SIZE), bf16)], ins=3)(got, parts, foreign)[0]
 
 
-def repeat(got, sums):
-    return call(repeat_kernel, "repeat", [((WIDTH, 4 * ROWS, SIZE), bf16)], ins=2)(got, sums)[0]
+def repeat(got, sums, after):
+    return call(repeat_kernel, "repeat", [((WIDTH, 4 * ROWS, SIZE), bf16)], ins=3, unread=1)(
+        got, sums, in_hbm(after)
+    )[0]
 
 
 def second(index, got, old, couple):
@@ -363,24 +455,31 @@
         second_kernel,
         "second",
         [kept, sliced, ((2 * ROWS, SIZE), bf16), ((EXTRA, SIZE), f32)],
+        scratch=held,
         ins=4,
         smem=1,
     )(index, got, in_hbm(old), couple)
 
 
-def final(got, extra, old, couple, iso, hi, lo, steps=4):
+def final(got, extra, old, couple, iso, hi, lo):
     vmem = pl.BlockSpec(memory_space=pltpu.VMEM)
-    part = pl.BlockSpec((SIZE // steps, ROWS, SIZE), lambda i: (i, 0, 0))
-    line = pl.BlockSpec((FLAT // steps, SIZE), lambda i: (i, 0))
+    any_place = pl.BlockSpec(memory_space=pl.ANY)
     return call(
         final_kernel,
         "final",
-        [square, (iso.shape, bf16)],
-        scratch=[pltpu.VMEM((5 * SIZE, SIZE), bf16)],
-        grid=(steps,),
-        in_specs=[vmem] * 5 + [line] * 2,
-        out_specs=[vmem, part],
+        [pltpu.HBM((SIZE, SIZE), f32), pltpu.HBM(iso.shape, bf16)],
+        scratch=[
+            pltpu.VMEM((5 * SIZE, SIZE), bf16),
+            pltpu.VMEM((FLAT, SIZE), bf16),
+            pltpu.VMEM((FLAT, SIZE), bf16),
+            pltpu.VMEM((SIZE, SIZE), f32),
+            pltpu.VMEM((SIZE, ROWS, SIZE), bf16),
+            pltpu.SemaphoreType.DMA((3 + PARTS,)),
+        ],
+        in_specs=[vmem] * 5 + [any_place] * 2,
+        out_specs=[any_place] * 2,
         flops=5 << 29,
+        grant=20,
     )(got, extra, in_hbm(old), couple, iso, in_hbm(hi), in_hbm(lo))
 
 
@@ -396,7 +495,7 @@
     part_2 = permuted(part_2, "blk", lambda i: i ^ 8)
 
     blocks = ascend(iso, left, right)
-    norm = norms(iso, blocks)
+    block, turned, norm = prepare(iso, blocks)
     share = rounded(exchange(blocks, "bond"), norm, part_2)
     own = exchange(share, "bond")
     near = permuted(own, "blk", lambda i: i ^ 1)
@@ -407,11 +506,12 @@
 
     env, outgoing = first(index, own, near, couple, couple_1)
     incoming = exchange(outgoing, "blk", quads)
-    moved_hi, moved_lo, parts = gradient(index, iso, left, near, far, norm, outgoing)
+    mix, parts = gradient(index, block, turned, left, near, far, norm, outgoing)
     got = exchange(pack(incoming, parts, part_2), "bond")
     env, outgoing, sums, extra = second(index, got, env, couple)
     incoming = exchange(outgoing, "blk", strides)
-    got = exchange(repeat(incoming, sums), "bond")
+    moved_hi, moved_lo = lines(mix, block, outgoing)
+    got = exchange(repeat(incoming, sums, moved_hi), "bond")
     env, out = final(got, extra, env, couple, iso, moved_hi, moved_lo)
     return (out[None], env[None])
 

time: 129 us -> 128 us (level)
  blocking collectives: 50.9 us -> 28.2 us
  starting transfers between devices: 41.4 us -> 49.1 us
  waiting for transfers between devices: 6.62 us -> 12.5 us
  Pallas kernels: 28.8 us -> 34.4 us
  local copies, waits for them, and re-layouts: 0.02 us -> 1.61 us
    all_to_all x3 -> x2, blocking collectives: 50.9 us -> 28.2 us  [exchange(): return lax.all_to_all(x, axis, 0, 0, axis_index_groups=groups, tiled=True)]
    all_to_all x3 -> x4, starting transfers between devices: 24.6 us -> 32.1 us  [exchange(): return lax.all_to_all(x, axis, 0, 0, axis_index_groups=groups, tiled=True)]
    all_to_all x3 -> x4, waiting for transfers between devices: 5.68 us -> 12.5 us  [exchange(): return lax.all_to_all(x, axis, 0, 0, axis_index_groups=groups, tiled=True)]
    pallas_call x5 -> x6, Pallas kernels: 18.5 us -> 23.5 us  [the longest x1 7.13 us: final(): call(final_kernel, 'final', [pltpu.HBM((SIZE, SIZE), f32), pltpu.HBM(iso....]
    unnamed x6 -> x8, local copies, waits for them, and re-layouts: 0.01 us -> 1.6 us
  transfers between devices with their start and end apart: 7 -> 8, of which waited for: 3 -> 2; matrix products, arithmetic and copies ran while one was open for 0% -> 0% of each run, Pallas kernels for 8% -> 13%
where the time goes in v3:
time: 128 us; the launch traced here: 127 us
  starting transfers between devices  49.1 us (38%)
  Pallas kernels  34.4 us (27%)
  blocking collectives  28.2 us (22%)
  waiting for transfers between devices  12.5 us (10%)
  local copies, waits for them, and re-layouts  1.61 us (1%)
    all_to_all x4, starting transfers between devices, exchange(): return lax.all_to_all(x, axis, 0, 0, axis_index_groups=groups, tiled=True)  32.1 us
    all_to_all x2, blocking collectives, exchange(): return lax.all_to_all(x, axis, 0, 0, axis_index_groups=groups, tiled=True)  28.2 us
    ppermute x4, starting transfers between devices, permuted(): lax.ppermute(x, axis, [(i, route(i)) for i in range(lax.axis_size(axis))])  16.9 us
    all_to_all x4, waiting for transfers between devices, exchange(): return lax.all_to_all(x, axis, 0, 0, axis_index_groups=groups, tiled=True)  12.5 us
    pallas_call x1, Pallas kernels, ascend(): call(ascend_kernel, 'ascend', [((WIDTH, 2, ROWS, SIZE), f32)], scratch=[p...  7.24 us
    pallas_call x1, Pallas kernels, final(): call(final_kernel, 'final', [pltpu.HBM((SIZE, SIZE), f32), pltpu.HBM(iso....  7.13 us
    pallas_call x1, Pallas kernels, gradient(): call(gradient_kernel, 'gradient', [((SIZE, SIZE), bf16), ((WIDTH, 2 * ROW...  5.29 us
    pallas_call x1, Pallas kernels, prepare(): call(prepare_kernel, 'prepare', [pltpu.HBM((FLAT, SIZE), bf16), pltpu.HBM...  4.3 us
  transfers between devices with their start and end apart: 8, of which 2 were waited for; matrix products, arithmetic and copies ran while one was open for 0% of the time, Pallas kernels for 13%

profile of v3, /device:TPU:64, one launch (start us, length us, event | category | flops | bytes accessed | tf_op | source)
XLA Modules:
  0.0 126.9 jit_solution(962273705717426030)
XLA Ops:
  0.6 0.0 copy-start.2
  0.6 0.0 copy-start
  0.6 7.2 %ascend.1.after_ref = f32[16,2,16,256]{3,2,1,0:T(8,128)} custom-call(bf16[256,16,256]{2,1,0:T(8,128)(2,1)} %bitcast.12, bf16[256,256]{1,0:T(8,128)(2,1)} %bitcast.20, bf16[256,256]{1,0:T(8,128)(2,1)} %bitcast.19), custom_call_target="tpu_custom_call" | custom-call | flops 3221225472 | bytes 4194304 | tf_op jit(solution)/shard_map/ascend/pallas_call | solution.py:359
  7.9 7.0 %all-to-all-start = ((f32[16,2,16,256]{3,2,1,0:T(8,128)}), f32[16,2,16,256]{3,2,1,0:T(8,128)S(1)}, u32[]{:S(2)}, u32[]{:S(2)}) async-start(f32[16,2,16,256]{3,2,1,0:T(8,128)} %ascend.1.after_ref), calls=%async_computation | async-start | bytes 1048576 | tf_op jit(solution)/shard_map/all_to_all | solution.py:345
  15.0 0.0 copy-done.2
  15.0 9.1 %collective-permute-start = (f32[16,256]{1,0:T(8,128)S(1)}, f32[16,256]{1,0:T(8,128)S(1)}, u32[]{:S(2)}, u32[]{:S(2)}) collective-permute-start(f32[16,256]{1,0:T(8,128)S(1)} %dynamic-slice_bitcast_fusion), channel_id=1, source_target_pairs={{0,128},{16,144},{32,160},{48,176},{64,192},{80,208},{96,224},{112... | collective-permute-start | bytes 49160 | tf_op jit(solution)/shard_map/ppermute | solution.py:349
  24.1 4.3 %prepare.1 = (bf16[4096,256]{1,0:T(8,128)(2,1)}, bf16[256,4096]{1,0:T(8,128)(2,1)}, f32[256,256]{1,0:T(8,128)S(1)}) custom-call(bf16[256,16,256]{2,1,0:T(8,128)(2,1)S(1)} %bitcast.13, f32[16,2,16,256]{3,2,1,0:T(8,128)} %ascend.1.after_ref), custom_call_target="tpu_custom_call" | custom-call | flops 536870912 | bytes 4194304 | tf_op jit(solution)/shard_map/prepare/pallas_call | solution.py:379
  28.4 0.0 collective-permute-done.also_ref.foreign_ref
  28.4 0.0 all-to-all-done.got_ref
  28.4 0.8 rounded.1
  29.2 7.2 %all-to-all-start.1 = ((bf16[16,2,16,256]{3,2,1,0:T(8,128)(2,1)}), bf16[16,2,16,256]{3,2,1,0:T(8,128)(2,1)S(1)}, u32[]{:S(2)}, u32[]{:S(2)}) async-start(bf16[16,2,16,256]{3,2,1,0:T(8,128)(2,1)} %rounded.1), calls=%async_computation.1 | async-start | bytes 524288 | tf_op jit(solution)/shard_map/all_to_all | solution.py:345
  36.4 3.8 %collective-permute-start.2 = (f32[256,256]{1,0:T(8,128)S(1)}, f32[256,256]{1,0:T(8,128)S(1)}, u32[]{:S(2)}, u32[]{:S(2)}) collective-permute-start(f32[256,256]{1,0:T(8,128)S(1)} %bitcast.15), channel_id=1, source_target_pairs={{0,32},{16,48},{32,0},{48,16},{64,96},{80,112},{96,64},{112,80},{1... | collective-permute-start | bytes 786440 | tf_op jit(solution)/shard_map/ppermute | solution.py:349
  40.2 4.9 %all-to-all-done.1.own_ref = bf16[16,2,16,256]{3,2,1,0:T(8,128)(2,1)S(1)} async-done(((bf16[16,2,16,256]{3,2,1,0:T(8,128)(2,1)}), bf16[16,2,16,256]{3,2,1,0:T(8,128)(2,1)S(1)}, u32[]{:S(2)}, u32[]{:S(2)}) %all-to-all-start.1) | async-done | bytes 262176 | tf_op jit(solution)/shard_map/all_to_all | solution.py:345
  45.1 1.9 %collective-permute-start.1 = (bf16[16,2,16,256]{3,2,1,0:T(8,128)(2,1)S(1)}, bf16[16,2,16,256]{3,2,1,0:T(8,128)(2,1)S(1)}, u32[]{:S(2)}, u32[]{:S(2)}) collective-permute-start(bf16[16,2,16,256]{3,2,1,0:T(8,128)(2,1)S(1)} %all-to-all-done.1.own_ref), channel_id=1, source_target_pairs={{0,16},{16,0},{32,48},{48,32},{64,80},{80,64},{96,112},{112,96},{1... | collective-permute-start | bytes 786440 | tf_op jit(solution)/shard_map/ppermute | solution.py:349
  47.0 2.1 %collective-permute-start.3 = (bf16[16,2,16,256]{3,2,1,0:T(8,128)(2,1)S(1)}, bf16[16,2,16,256]{3,2,1,0:T(8,128)(2,1)}, u32[]{:S(2)}, u32[]{:S(2)}) collective-permute-start(bf16[16,2,16,256]{3,2,1,0:T(8,128)(2,1)S(1)} %all-to-all-done.1.own_ref), channel_id=1, source_target_pairs={{0,496},{16,32},{32,16},{48,64},{64,48},{80,96},{96,80},{112,128},... | collective-permute-start | bytes 786440 | tf_op jit(solution)/shard_map/ppermute | solution.py:349
  49.2 0.1 pad_add_fusion.index_ref
  49.3 0.0 collective-permute-done.2.foreign_ref
  49.3 0.0 collective-permute-done.1.near_ref
  49.3 2.5 %first.1 = (f32[256,256]{1,0:T(8,128)}, f32[4,16,256]{2,1,0:T(8,128)}) custom-call(s32[4]{0:T(128)S(1)} %pad_add_fusion.index_ref, bf16[16,2,16,256]{3,2,1,0:T(8,128)(2,1)S(1)} %all-to-all-done.1.own_ref, bf16[16,2,16,256]{3,2,1,0:T(8,128)(2,1)S(1)} %collective-permute-done.1.near_ref, f32[256,256]{1,0:T(8,128)S(1)} %bitcast.16, ...), custom_call_target="tpu_custom_call" | custom-call | bytes 4194304 | tf_op jit(solution)/shard_map/first/pallas_call | solution.py:400
  51.8 8.7 %all-to-all-start.2 = ((f32[4,16,256]{2,1,0:T(8,128)}), f32[4,16,256]{2,1,0:T(8,128)S(1)}, u32[]{:S(2)}, u32[]{:S(2)}) async-start(f32[4,16,256]{2,1,0:T(8,128)} %get-tuple-element.18.after_ref), calls=%async_computation.2 | async-start | bytes 131072 | tf_op jit(solution)/shard_map/all_to_all | solution.py:345
  60.5 0.0 collective-permute-done.3.far_ref
  60.5 5.3 %gradient.1 = (bf16[256,256]{1,0:T(8,128)(2,1)S(1)}, bf16[16,40,256]{2,1,0:T(8,128)(2,1)S(1)}) custom-call(s32[4]{0:T(128)S(1)} %pad_add_fusion.index_ref, bf16[256,256]{1,0:T(8,128)(2,1)} %bitcast.21, bf16[16,2,16,256]{3,2,1,0:T(8,128)(2,1)} %copy-done.3, bf16[16,2,16,256]{3,2,1,0:T(8,128)(2,1)} %collective-permute-done.3.far_ref, ...), custom_call_target="tpu_custom_call" | custom-call | flops 2147483648 | bytes 4194304 | tf_op jit(solution)/shard_map/gradient/pallas_call | solution.py:406
  65.8 0.0 all-to-all-done.2.got_ref
  65.8 0.1 pack.1
  65.8 15.0 %all_to_all.30.got_ref = bf16[16,104,256]{2,1,0:T(8,128)(2,1)S(1)} all-to-all(bf16[16,104,256]{2,1,0:T(8,128)(2,1)S(1)} %pack.1), channel_id=1, replica_groups=mesh['blk'=32,'bond'=16] {'bond'}, dimensions={0} | all-to-all | bytes 1703936 | tf_op jit(solution)/shard_map/all_to_all | solution.py:345
  80.8 2.9 %second.1 = (f32[256,256]{1,0:T(8,128)}, f32[4,16,256]{2,1,0:T(8,128)}, bf16[32,256]{1,0:T(8,128)(2,1)S(1)}, f32[8,256]{1,0:T(8,128)S(1)}) custom-call(s32[4]{0:T(128)S(1)} %pad_add_fusion.index_ref, bf16[16,104,256]{2,1,0:T(8,128)(2,1)S(1)} %all_to_all.30.got_ref, f32[256,256]{1,0:T(8,128)} %get-tuple-element.22.old_ref, f32[256,256]{1,0:T(8,128)S(1)} %bitcast.17), custom_call_target="tpu_custom_call" | custom-call | bytes 4194304 | tf_op jit(solution)/shard_map/second/pallas_call | solution.py:454
  83.7 9.2 %all-to-all-start.4 = ((f32[4,16,256]{2,1,0:T(8,128)}), f32[4,16,256]{2,1,0:T(8,128)S(1)}, u32[]{:S(2)}, u32[]{:S(2)}) async-start(f32[4,16,256]{2,1,0:T(8,128)} %get-tuple-element.23.after_ref), calls=%async_computation.4 | async-start | bytes 131072 | tf_op jit(solution)/shard_map/all_to_all | solution.py:345
  92.9 1.6 %copy-done.1 = bf16[4096,256]{1,0:T(8,128)(2,1)S(1)} copy-done((bf16[4096,256]{1,0:T(8,128)(2,1)S(1)}, bf16[4096,256]{1,0:T(8,128)(2,1)}, u32[]{:S(2)}) %copy-start.1) | copy-done | bytes 2097176
  94.5 4.2 %lines.1 = (bf16[4096,256]{1,0:T(8,128)(2,1)}, bf16[4096,256]{1,0:T(8,128)(2,1)}) custom-call(bf16[256,256]{1,0:T(8,128)(2,1)S(1)} %get-tuple-element.25.mix_ref, bf16[4096,256]{1,0:T(8,128)(2,1)S(1)} %copy-done.1, f32[4,16,256]{2,1,0:T(8,128)} %get-tuple-element.23.after_ref), custom_call_target="tpu_custom_call" | custom-call | flops 536870912 | bytes 4194304 | tf_op jit(solution)/shard_map/lines/pallas_call | solution.py:426
  98.7 7.6 %all-to-all-done.4.got_ref = f32[4,16,256]{2,1,0:T(8,128)S(1)} async-done(((f32[4,16,256]{2,1,0:T(8,128)}), f32[4,16,256]{2,1,0:T(8,128)S(1)}, u32[]{:S(2)}, u32[]{:S(2)}) %all-to-all-start.4) | async-done | bytes 65568 | tf_op jit(solution)/shard_map/all_to_all | solution.py:345
  106.4 13.2 %all_to_all.31.got_ref = bf16[16,64,256]{2,1,0:T(8,128)(2,1)S(1)} all-to-all(bf16[16,64,256]{2,1,0:T(8,128)(2,1)S(1)} %repeat.1), channel_id=1, replica_groups=mesh['blk'=32,'bond'=16] {'bond'}, dimensions={0} | all-to-all | bytes 1048576 | tf_op jit(solution)/shard_map/all_to_all | solution.py:345
  119.6 7.1 %final.1 = (f32[256,256]{1,0:T(8,128)}, bf16[256,16,256]{2,1,0:T(8,128)(2,1)}) custom-call(bf16[16,64,256]{2,1,0:T(8,128)(2,1)S(1)} %all_to_all.31.got_ref, f32[8,256]{1,0:T(8,128)S(1)} %get-tuple-element.27.extra_ref, f32[256,256]{1,0:T(8,128)} %get-tuple-element.28.old_ref, f32[256,256]{1,0:T(8,128)S(1)} %bitcast.18, bf16[256,16,256]{2,1,0:T(8,128)(2,1)S(1)} %bitcast.14, ...), custom_call_target="tpu_custom_call" | custom-call | flops 2684354560 | bytes 4194304 | tf_op jit(solution)/shard_map/final/pallas_call | solution.py:467
  (6 shorter events, 0.1 us)
Async XLA Ops:
  0.6 14.3 %copy-start.2 = (f32[1,256,256]{2,1,0:T(8,128)S(1)}, f32[1,256,256]{2,1,0:T(8,128)}, u32[]{:S(2)}) copy-start(f32[1,256,256]{2,1,0:T(8,128)} %param.7) | copy-start | bytes 786436
  0.6 23.5 %copy-start = (bf16[1,256,16,256]{3,2,1,0:T(8,128)(2,1)S(1)}, bf16[1,256,16,256]{3,2,1,0:T(8,128)(2,1)}, u32[]{:S(2)}) copy-start(bf16[1,256,16,256]{3,2,1,0:T(8,128)(2,1)} %param.4) | copy-start | bytes 6291460
  7.9 20.5 %all-to-all-start = ((f32[16,2,16,256]{3,2,1,0:T(8,128)}), f32[16,2,16,256]{3,2,1,0:T(8,128)S(1)}, u32[]{:S(2)}, u32[]{:S(2)}) async-start(f32[16,2,16,256]{3,2,1,0:T(8,128)} %ascend.1.after_ref), calls=%async_computation | async-start | bytes 1048576 | tf_op jit(solution)/shard_map/all_to_all | solution.py:345
  15.0 13.4 %collective-permute-start = (f32[16,256]{1,0:T(8,128)S(1)}, f32[16,256]{1,0:T(8,128)S(1)}, u32[]{:S(2)}, u32[]{:S(2)}) collective-permute-start(f32[16,256]{1,0:T(8,128)S(1)} %dynamic-slice_bitcast_fusion), channel_id=1, source_target_pairs={{0,128},{16,144},{32,160},{48,176},{64,192},{80,208},{96,224},{112... | collective-permute-start | bytes 49160 | tf_op jit(solution)/shard_map/ppermute | solution.py:349
  29.2 15.9 %all-to-all-start.1 = ((bf16[16,2,16,256]{3,2,1,0:T(8,128)(2,1)}), bf16[16,2,16,256]{3,2,1,0:T(8,128)(2,1)S(1)}, u32[]{:S(2)}, u32[]{:S(2)}) async-start(bf16[16,2,16,256]{3,2,1,0:T(8,128)(2,1)} %rounded.1), calls=%async_computation.1 | async-start | bytes 524288 | tf_op jit(solution)/shard_map/all_to_all | solution.py:345
  36.4 12.9 %collective-permute-start.2 = (f32[256,256]{1,0:T(8,128)S(1)}, f32[256,256]{1,0:T(8,128)S(1)}, u32[]{:S(2)}, u32[]{:S(2)}) collective-permute-start(f32[256,256]{1,0:T(8,128)S(1)} %bitcast.15), channel_id=1, source_target_pairs={{0,32},{16,48},{32,0},{48,16},{64,96},{80,112},{96,64},{112,80},{1... | collective-permute-start | bytes 786440 | tf_op jit(solution)/shard_map/ppermute | solution.py:349
  45.1 4.2 %collective-permute-start.1 = (bf16[16,2,16,256]{3,2,1,0:T(8,128)(2,1)S(1)}, bf16[16,2,16,256]{3,2,1,0:T(8,128)(2,1)S(1)}, u32[]{:S(2)}, u32[]{:S(2)}) collective-permute-start(bf16[16,2,16,256]{3,2,1,0:T(8,128)(2,1)S(1)} %all-to-all-done.1.own_ref), channel_id=1, source_target_pairs={{0,16},{16,0},{32,48},{48,32},{64,80},{80,64},{96,112},{112,96},{1... | collective-permute-start | bytes 786440 | tf_op jit(solution)/shard_map/ppermute | solution.py:349
  47.0 13.5 %collective-permute-start.3 = (bf16[16,2,16,256]{3,2,1,0:T(8,128)(2,1)S(1)}, bf16[16,2,16,256]{3,2,1,0:T(8,128)(2,1)}, u32[]{:S(2)}, u32[]{:S(2)}) collective-permute-start(bf16[16,2,16,256]{3,2,1,0:T(8,128)(2,1)S(1)} %all-to-all-done.1.own_ref), channel_id=1, source_target_pairs={{0,496},{16,32},{32,16},{48,64},{64,48},{80,96},{96,80},{112,128},... | collective-permute-start | bytes 786440 | tf_op jit(solution)/shard_map/ppermute | solution.py:349
  49.3 11.2 %copy-start.3 = (bf16[16,2,16,256]{3,2,1,0:T(8,128)(2,1)}, bf16[16,2,16,256]{3,2,1,0:T(8,128)(2,1)S(1)}, u32[]{:S(2)}) copy-start(bf16[16,2,16,256]{3,2,1,0:T(8,128)(2,1)S(1)} %collective-permute-done.1.near_ref) | copy-start | bytes 786436
  51.8 14.0 %all-to-all-start.2 = ((f32[4,16,256]{2,1,0:T(8,128)}), f32[4,16,256]{2,1,0:T(8,128)S(1)}, u32[]{:S(2)}, u32[]{:S(2)}) async-start(f32[4,16,256]{2,1,0:T(8,128)} %get-tuple-element.18.after_ref), calls=%async_computation.2 | async-start | bytes 131072 | tf_op jit(solution)/shard_map/all_to_all | solution.py:345
  83.7 22.6 %all-to-all-start.4 = ((f32[4,16,256]{2,1,0:T(8,128)}), f32[4,16,256]{2,1,0:T(8,128)S(1)}, u32[]{:S(2)}, u32[]{:S(2)}) async-start(f32[4,16,256]{2,1,0:T(8,128)} %get-tuple-element.23.after_ref), calls=%async_computation.4 | async-start | bytes 131072 | tf_op jit(solution)/shard_map/all_to_all | solution.py:345
  92.9 1.6 %copy-start.1 = (bf16[4096,256]{1,0:T(8,128)(2,1)S(1)}, bf16[4096,256]{1,0:T(8,128)(2,1)}, u32[]{:S(2)}) copy-start(bf16[4096,256]{1,0:T(8,128)(2,1)} %get-tuple-element.19.block_hbm.block_ref) | copy-start | bytes 6291460

commit v4 on v3

--- a/solution.py
+++ b/solution.py
@@ -16,7 +16,7 @@
 HALF = 128
 CHUNKS = 4
 EXTRA = 8
-PARTS = 8
+PARTS = 2
 
 
 def split(x):
@@ -56,7 +56,7 @@
             + [vmem] * (ins - smem - unread)
             + [any_place] * unread
         )
-        out_specs = [any_place if isinstance(o, pl.MemoryRef) else vmem for o in outs]
+        out_specs = [vmem] * len(outs)
     params = dict(grid=grid) if grid else {}
     return pl.pallas_call(
         kernel,
@@ -150,19 +150,16 @@
         out_ref[p] = jnp.where(which == 3, crossed, jnp.where(which == 0, 0.0, own))
 
 
-def first_kernel(index_ref, own_ref, near_ref, couple_ref, foreign_ref, env_hbm, out_ref, env_ref, sem):
+def first_kernel(index_ref, own_ref, near_ref, couple_ref, foreign_ref, env_ref, out_ref):
     def whole(ref):
         return (ref[:, 0].astype(f32) + ref[:, 1].astype(f32)).reshape(SIZE, SIZE)
 
     env_ref[...] = 0.5 * (whole(own_ref) + sandwich(couple_ref[...], whole(near_ref)))
-    copy = pltpu.make_async_copy(env_ref, env_hbm, sem)
-    copy.start()
     left = foreign_ref[pl.ds(index_ref[0] * ROWS, ROWS), :]
     slices(index_ref, 1, env_ref, left, foreign_ref[...], out_ref)
-    copy.wait()
-
-
-def gradient_kernel(index_ref, edge_ref, near_ref, far_ref, norm_ref, block_hbm, turned_hbm, after_ref, mix_ref, out_ref, moved_ref, flipped_ref, block_ref, turned_ref, sems):
+
+
+def gradient_kernel(index_ref, edge_ref, near_ref, far_ref, norm_ref, block_hbm, turned_hbm, after_ref, hi_hbm, lo_hbm, out_ref, moved_ref, low_ref, flipped_ref, block_ref, turned_ref, sems):
     copies = []
     step = FLAT // CHUNKS
     for i in range(CHUNKS):
@@ -179,7 +176,6 @@
     from_left = jnp.where(odd, whole(near_ref, 1), whole(far_ref, 1))
     from_right = jnp.where(odd, whole(far_ref, 0), whole(near_ref, 0))
     mix = (edge_ref[...].astype(f32) + from_left + from_right).astype(bf16)
-    mix_ref[...] = mix
     squares = jnp.zeros((8, SIZE), f32)
     for b in range(ROWS):
         if b % (ROWS // CHUNKS) == 0:
@@ -189,8 +185,14 @@
         here = slice(b * SIZE, (b + 1) * SIZE)
         moved = mm(mix, block_ref[here])
         squares = squares + jnp.sum((moved * moved).reshape(SIZE // 8, 8, SIZE), axis=0)
-        moved_ref[here] = moved.astype(bf16)
+        moved_ref[here], low_ref[here] = split(moved)
         flipped_ref[:, here] = mm(turned_ref[:, here], mix, NT).astype(bf16)
+    outgoing = [
+        pltpu.make_async_copy(moved_ref, hi_hbm, sems.at[2 * CHUNKS]),
+        pltpu.make_async_copy(low_ref, lo_hbm, sems.at[2 * CHUNKS + 1]),
+    ]
+    for copy in outgoing:
+        copy.start()
     part_q = mm(turned_ref[...], moved_ref[...])
     part_r = mm(flipped_ref[...], moved_ref[...])
     part_n = norm_ref[...]
@@ -208,26 +210,7 @@
     out_ref[:, ROWS : 2 * ROWS] = packed.astype(bf16).reshape(WIDTH, ROWS, SIZE)
     for i in range(WIDTH):
         out_ref[i, 2 * ROWS :] = extra
-
-
-def lines_kernel(mix_ref, block_ref, after_ref, hi_hbm, lo_hbm, moved_ref, hi_ref, lo_ref, sems):
-    mix = mix_ref[...]
-    for b in range(ROWS):
-        moved = mm(mix, block_ref[b * SIZE : (b + 1) * SIZE])
-        for h in range(2):
-            moved_ref[h, pl.ds(b, SIZE, stride=ROWS), :] = moved[:, h * HALF : (h + 1) * HALF]
-    for h in range(2):
-        columns = slice(h * HALF, (h + 1) * HALF)
-        hi, lo = split(moved_ref[h])
-        hi_ref[:, columns] = hi
-        lo_ref[:, columns] = lo
-    copies = [
-        pltpu.make_async_copy(hi_ref, hi_hbm, sems.at[0]),
-        pltpu.make_async_copy(lo_ref, lo_hbm, sems.at[1]),
-    ]
-    for copy in copies:
-        copy.start()
-    for copy in copies:
+    for copy in outgoing:
         copy.wait()
 
 
@@ -243,7 +226,7 @@
     out_ref[:, 6 * ROWS :] = parts_ref[:, 2 * ROWS :]
 
 
-def repeat_kernel(got_ref, sums_ref, after_ref, out_ref):
+def repeat_kernel(got_ref, sums_ref, out_ref):
     hi, lo = split((got_ref[0] + got_ref[1]) + (got_ref[2] + got_ref[3]))
     for i in range(WIDTH):
         out_ref[i, :ROWS] = hi
@@ -256,10 +239,8 @@
     return 0.25 * (env_ref[...] + sandwich(couple_ref[...], force.reshape(SIZE, SIZE)))
 
 
-def second_kernel(index_ref, got_ref, old_ref, couple_ref, env_hbm, out_ref, sums_ref, extra_ref, env_ref, sem):
+def second_kernel(index_ref, got_ref, old_ref, couple_ref, env_ref, out_ref, sums_ref, extra_ref):
     env_ref[...] = two_levels(old_ref, got_ref, couple_ref)
-    copy = pltpu.make_async_copy(env_ref, env_hbm, sem)
-    copy.start()
 
     def foreign(at):
         hi, lo = slice(4 * ROWS, 5 * ROWS), slice(5 * ROWS, 6 * ROWS)
@@ -276,7 +257,6 @@
 
     extra_ref[...] = total(slice(6 * ROWS, 6 * ROWS + EXTRA))
     sums_ref[...] = total(slice(2 * ROWS, 4 * ROWS)).astype(bf16)
-    copy.wait()
 
 
 def mm2(a, b, dims=NN):
@@ -308,16 +288,17 @@
     return ph, pl_, mm(top, ph) + mm(top, pl_)
 
 
-def final_kernel(got_ref, extra_ref, old_ref, couple_ref, iso_ref, hi_hbm, lo_hbm, env_hbm, out_hbm, map_ref, hi_ref, lo_ref, env_ref, out_ref, sems):
+def final_kernel(got_ref, extra_ref, old_ref, couple_ref, block_hbm, hi_hbm, lo_hbm, env_hbm, out_hbm, map_ref, block_ref, hi_ref, lo_ref, env_ref, wide_ref, out_ref, sems):
     incoming = [
         pltpu.make_async_copy(hi_hbm, hi_ref, sems.at[0]),
         pltpu.make_async_copy(lo_hbm, lo_ref, sems.at[1]),
+        pltpu.make_async_copy(block_hbm, block_ref, sems.at[2]),
     ]
     for copy in incoming:
         copy.start()
     env = two_levels(old_ref, got_ref, couple_ref)
     env_ref[...] = env
-    outgoing = [pltpu.make_async_copy(env_ref, env_hbm, sems.at[2])]
+    outgoing = [pltpu.make_async_copy(env_ref, env_hbm, sems.at[3])]
     outgoing[0].start()
     full_q = got_ref[:, 2 * ROWS : 3 * ROWS].astype(f32).reshape(SIZE, SIZE)
     full_s = got_ref[:, 3 * ROWS :].astype(f32).reshape(SIZE, SIZE)
@@ -328,13 +309,20 @@
         copy.wait()
     step = SIZE // PARTS
     for i in range(PARTS):
+        for b in range(ROWS):
+            here = pl.ds(b * SIZE + i * step, step)
+            hi = hi_ref[here]
+            flat = block_ref[here]
+            rows = jnp.concatenate([hi, lo_ref[here], hi, flat, flat], axis=1)
+            value = mm(rows, map_ref[...])
+            for h in range(2):
+                wide_ref[h, pl.ds(i * step * ROWS + b, step, stride=ROWS), :] = value[:, h * HALF : (h + 1) * HALF]
+        lines = pl.ds(i * step * ROWS, step * ROWS)
         here = pl.ds(i * step, step)
-        lines = pl.ds(i * step * ROWS, step * ROWS)
-        flat = iso_ref[here].reshape(-1, SIZE)
-        hi = hi_ref[lines]
-        rows = jnp.concatenate([hi, lo_ref[lines], hi, flat, flat], axis=1)
-        out_ref[here] = mm(rows, map_ref[...]).astype(bf16).reshape(step, ROWS, SIZE)
-        copy = pltpu.make_async_copy(out_ref.at[here], out_hbm.at[here], sems.at[3 + i])
+        for h in range(2):
+            part = wide_ref[h, lines].astype(bf16).reshape(step, ROWS, HALF)
+            out_ref[here, :, h * HALF : (h + 1) * HALF] = part
+        copy = pltpu.make_async_copy(out_ref.at[here], out_hbm.at[here], sems.at[4 + i])
         copy.start()
         outgoing.append(copy)
     for copy in outgoing:
@@ -351,7 +339,6 @@
 
 square = ((SIZE, SIZE), f32)
 kept = pltpu.HBM((SIZE, SIZE), f32)
-held = [pltpu.VMEM((SIZE, SIZE), f32), pltpu.SemaphoreType.DMA]
 sliced = ((4, ROWS, SIZE), f32)
 
 
@@ -386,8 +373,8 @@
             pltpu.VMEM((SIZE, FLAT), bf16),
             pltpu.SemaphoreType.DMA((2,)),
         ],
-        ins=2,
-        unread=1,
+        in_specs=[pl.BlockSpec(memory_space=pltpu.VMEM), pl.BlockSpec(memory_space=pl.ANY)],
+        out_specs=[pl.BlockSpec(memory_space=pl.ANY)] * 2 + [pl.BlockSpec(memory_space=pltpu.VMEM)],
         flops=1 << 29,
     )(iso, after)
 
@@ -397,90 +384,73 @@
 
 
 def first(index, own, near, couple, foreign):
-    return call(first_kernel, "first", [kept, sliced], scratch=held, ins=5, smem=1)(
+    return call(first_kernel, "first", [kept, sliced], ins=5, smem=1)(
         index, own, near, couple, foreign
     )
 
 
 def gradient(index, block, turned, edge, near, far, norm, after):
+    vmem = pl.BlockSpec(memory_space=pltpu.VMEM)
+    any_place = pl.BlockSpec(memory_space=pl.ANY)
     return call(
         gradient_kernel,
         "gradient",
-        [((SIZE, SIZE), bf16), ((WIDTH, 2 * ROWS + EXTRA, SIZE), bf16)],
+        [pltpu.HBM((FLAT, SIZE), bf16), pltpu.HBM((FLAT, SIZE), bf16), ((WIDTH, 2 * ROWS + EXTRA, SIZE), bf16)],
         scratch=[
             pltpu.VMEM((FLAT, SIZE), bf16),
+            pltpu.VMEM((FLAT, SIZE), bf16),
             pltpu.VMEM((SIZE, FLAT), bf16),
             pltpu.VMEM((FLAT, SIZE), bf16),
             pltpu.VMEM((SIZE, FLAT), bf16),
-            pltpu.SemaphoreType.DMA((2 * CHUNKS,)),
+            pltpu.SemaphoreType.DMA((2 * CHUNKS + 2,)),
         ],
-        ins=8,
-        smem=1,
-        unread=3,
+        in_specs=[pl.BlockSpec(memory_space=pltpu.SMEM)] + [vmem] * 4 + [any_place] * 3,
+        out_specs=[any_place] * 2 + [vmem],
         flops=4 << 29,
         grant=20,
     )(index, in_hbm(edge), in_hbm(near), in_hbm(far), norm, in_hbm(block), in_hbm(turned), after)
 
 
-def lines(mix, block, after):
-    return call(
-        lines_kernel,
-        "lines",
-        [pltpu.HBM((FLAT, SIZE), bf16), pltpu.HBM((FLAT, SIZE), bf16)],
-        scratch=[
-            pltpu.VMEM((2, FLAT, HALF), f32),
-            pltpu.VMEM((FLAT, SIZE), bf16),
-            pltpu.VMEM((FLAT, SIZE), bf16),
-            pltpu.SemaphoreType.DMA((2,)),
-        ],
-        in_specs=[pl.BlockSpec(memory_space=pltpu.VMEM)] * 2 + [pl.BlockSpec(memory_space=pl.ANY)],
-        out_specs=[pl.BlockSpec(memory_space=pl.ANY)] * 2,
-        flops=1 << 29,
-        grant=20,
-    )(mix, block, after)
-
-
 def pack(got, parts, foreign):
     return call(pack_kernel, "pack", [((WIDTH, 6 * ROWS + EXTRA, SIZE), bf16)], ins=3)(got, parts, foreign)[0]
 
 
-def repeat(got, sums, after):
-    return call(repeat_kernel, "repeat", [((WIDTH, 4 * ROWS, SIZE), bf16)], ins=3, unread=1)(
-        got, sums, in_hbm(after)
-    )[0]
+def repeat(got, sums):
+    return call(repeat_kernel, "repeat", [((WIDTH, 4 * ROWS, SIZE), bf16)], ins=2)(got, sums)[0]
 
 
 def second(index, got, old, couple):
     return call(
         second_kernel,
         "second",
-        [kept, sliced, ((2 * ROWS, SIZE), bf16), ((EXTRA, SIZE), f32)],
-        scratch=held,
+        [square, sliced, ((2 * ROWS, SIZE), bf16), ((EXTRA, SIZE), f32)],
         ins=4,
         smem=1,
     )(index, got, in_hbm(old), couple)
 
 
-def final(got, extra, old, couple, iso, hi, lo):
+def final(got, extra, old, couple, block, hi, lo):
     vmem = pl.BlockSpec(memory_space=pltpu.VMEM)
     any_place = pl.BlockSpec(memory_space=pl.ANY)
     return call(
         final_kernel,
         "final",
-        [pltpu.HBM((SIZE, SIZE), f32), pltpu.HBM(iso.shape, bf16)],
+        [pltpu.HBM((SIZE, SIZE), f32), pltpu.HBM((SIZE, ROWS, SIZE), bf16)],
         scratch=[
             pltpu.VMEM((5 * SIZE, SIZE), bf16),
             pltpu.VMEM((FLAT, SIZE), bf16),
             pltpu.VMEM((FLAT, SIZE), bf16),
+            pltpu.VMEM((FLAT, SIZE), bf16),
             pltpu.VMEM((SIZE, SIZE), f32),
+            pltpu.VMEM((2, FLAT, HALF), f32),
             pltpu.VMEM((SIZE, ROWS, SIZE), bf16),
-            pltpu.SemaphoreType.DMA((3 + PARTS,)),
+            pltpu.SemaphoreType.DMA((4 + PARTS,)),
         ],
-        in_specs=[vmem] * 5 + [any_place] * 2,
+        in_specs=[vmem] * 4 + [any_place] * 3,
         out_specs=[any_place] * 2,
         flops=5 << 29,
-        grant=20,
-    )(got, extra, in_hbm(old), couple, iso, in_hbm(hi), in_hbm(lo))
+        grant=24,
+    )(got, extra, old, couple, in_hbm(block), in_hbm(hi), in_hbm(lo))
 
 
 def body(iso, edge_left, edge_right, coupling):
@@ -506,13 +476,12 @@
 
     env, outgoing = first(index, own, near, couple, couple_1)
     incoming = exchange(outgoing, "blk", quads)
-    mix, parts = gradient(index, block, turned, left, near, far, norm, outgoing)
+    moved_hi, moved_lo, parts = gradient(index, block, turned, left, near, far, norm, outgoing)
     got = exchange(pack(incoming, parts, part_2), "bond")
     env, outgoing, sums, extra = second(index, got, env, couple)
     incoming = exchange(outgoing, "blk", strides)
-    moved_hi, moved_lo = lines(mix, block, outgoing)
-    got = exchange(repeat(incoming, sums, moved_hi), "bond")
-    env, out = final(got, extra, env, couple, iso, moved_hi, moved_lo)
+    got = exchange(repeat(incoming, sums), "bond")
+    env, out = final(got, extra, env, couple, block, moved_hi, moved_lo)
     return (out[None], env[None])
 
 

time: 128 us -> 129 us (level)
  blocking collectives: 28.2 us -> 50.6 us
  starting transfers between devices: 49.1 us -> 39.9 us
  waiting for transfers between devices: 12.5 us -> 4.88 us
  Pallas kernels: 34.4 us -> 30.9 us
    all_to_all x2 -> x3, blocking collectives: 28.2 us -> 50.6 us  [exchange(): return lax.all_to_all(x, axis, 0, 0, axis_index_groups=groups, tiled=True)]
    all_to_all x4 -> x3, starting transfers between devices: 32.1 us -> 22.9 us  [exchange(): return lax.all_to_all(x, axis, 0, 0, axis_index_groups=groups, tiled=True)]
    all_to_all x4 -> x3, waiting for transfers between devices: 12.5 us -> 4.87 us  [exchange(): return lax.all_to_all(x, axis, 0, 0, axis_index_groups=groups, tiled=True)]
    pallas_call x6 -> x5, Pallas kernels: 22.1 us -> 18.5 us  [the longest x1 8.12 us: final(): call(final_kernel, 'final', [pltpu.HBM((SIZE, SIZE), f32), pltpu.HBM((SIZ...]
  transfers between devices with their start and end apart: 8 -> 7, of which waited for: 2 -> 1; matrix products, arithmetic and copies ran while one was open for 0% -> 0% of each run, Pallas kernels for 13% -> 10%
where the time goes in v4:
time: 129 us; the launch traced here: 128 us
  blocking collectives  50.6 us (39%)
  starting transfers between devices  39.9 us (31%)
  Pallas kernels  30.9 us (24%)
  waiting for transfers between devices  4.88 us (4%)
    all_to_all x3, blocking collectives, exchange(): return lax.all_to_all(x, axis, 0, 0, axis_index_groups=groups, tiled=True)  50.6 us
    all_to_all x3, starting transfers between devices, exchange(): return lax.all_to_all(x, axis, 0, 0, axis_index_groups=groups, tiled=True)  22.9 us
    ppermute x4, starting transfers between devices, permuted(): lax.ppermute(x, axis, [(i, route(i)) for i in range(lax.axis_size(axis))])  16.9 us
    pallas_call x1, Pallas kernels, final(): call(final_kernel, 'final', [pltpu.HBM((SIZE, SIZE), f32), pltpu.HBM((SIZ...  8.12 us
    pallas_call x1, Pallas kernels, ascend(): call(ascend_kernel, 'ascend', [((WIDTH, 2, ROWS, SIZE), f32)], scratch=[p...  7.26 us
    pallas_call x1, Pallas kernels, gradient(): call(gradient_kernel, 'gradient', [pltpu.HBM((FLAT, SIZE), bf16), pltpu.H...  6.24 us
    all_to_all x3, waiting for transfers between devices, exchange(): return lax.all_to_all(x, axis, 0, 0, axis_index_groups=groups, tiled=True)  4.87 us
    pallas_call x1, Pallas kernels, prepare(): call(prepare_kernel, 'prepare', [pltpu.HBM((FLAT, SIZE), bf16), pltpu.HBM...  4.29 us
  transfers between devices with their start and end apart: 7, of which 1 were waited for; matrix products, arithmetic and copies ran while one was open for 0% of the time, Pallas kernels for 10%

profile of v4, /device:TPU:64, one launch (start us, length us, event | category | flops | bytes accessed | tf_op | source)
XLA Modules:
  0.0 128.1 jit_solution(18413139426759108655)
XLA Ops:
  0.6 0.0 copy-start.1
  0.6 0.0 copy-start
  0.6 7.3 %ascend.1.after_ref = f32[16,2,16,256]{3,2,1,0:T(8,128)} custom-call(bf16[256,16,256]{2,1,0:T(8,128)(2,1)} %bitcast.12, bf16[256,256]{1,0:T(8,128)(2,1)} %bitcast.19, bf16[256,256]{1,0:T(8,128)(2,1)} %bitcast.18), custom_call_target="tpu_custom_call" | custom-call | flops 3221225472 | bytes 4194304 | tf_op jit(solution)/shard_map/ascend/pallas_call | solution.py:346
  7.9 7.0 %all-to-all-start = ((f32[16,2,16,256]{3,2,1,0:T(8,128)}), f32[16,2,16,256]{3,2,1,0:T(8,128)S(1)}, u32[]{:S(2)}, u32[]{:S(2)}) async-start(f32[16,2,16,256]{3,2,1,0:T(8,128)} %ascend.1.after_ref), calls=%async_computation | async-start | bytes 1048576 | tf_op jit(solution)/shard_map/all_to_all | solution.py:333
  15.0 0.0 copy-done.1
  15.0 9.1 %collective-permute-start = (f32[16,256]{1,0:T(8,128)S(1)}, f32[16,256]{1,0:T(8,128)S(1)}, u32[]{:S(2)}, u32[]{:S(2)}) collective-permute-start(f32[16,256]{1,0:T(8,128)S(1)} %dynamic-slice_bitcast_fusion), channel_id=1, source_target_pairs={{0,128},{16,144},{32,160},{48,176},{64,192},{80,208},{96,224},{112... | collective-permute-start | bytes 49160 | tf_op jit(solution)/shard_map/ppermute | solution.py:337
  24.1 0.0 copy-done
  24.1 4.3 %prepare.1 = (bf16[4096,256]{1,0:T(8,128)(2,1)}, bf16[256,4096]{1,0:T(8,128)(2,1)}, f32[256,256]{1,0:T(8,128)S(1)}) custom-call(bf16[256,16,256]{2,1,0:T(8,128)(2,1)S(1)} %bitcast.13, f32[16,2,16,256]{3,2,1,0:T(8,128)} %ascend.1.after_ref), custom_call_target="tpu_custom_call" | custom-call | flops 536870912 | bytes 4194304 | tf_op jit(solution)/shard_map/prepare/pallas_call | solution.py:366
  28.4 0.0 collective-permute-done.also_ref.foreign_ref
  28.4 0.0 all-to-all-done.got_ref
  28.4 0.8 rounded.1
  29.2 7.2 %all-to-all-start.1 = ((bf16[16,2,16,256]{3,2,1,0:T(8,128)(2,1)}), bf16[16,2,16,256]{3,2,1,0:T(8,128)(2,1)S(1)}, u32[]{:S(2)}, u32[]{:S(2)}) async-start(bf16[16,2,16,256]{3,2,1,0:T(8,128)(2,1)} %rounded.1), calls=%async_computation.1 | async-start | bytes 524288 | tf_op jit(solution)/shard_map/all_to_all | solution.py:333
  36.4 3.8 %collective-permute-start.2 = (f32[256,256]{1,0:T(8,128)S(1)}, f32[256,256]{1,0:T(8,128)S(1)}, u32[]{:S(2)}, u32[]{:S(2)}) collective-permute-start(f32[256,256]{1,0:T(8,128)S(1)} %bitcast.14), channel_id=1, source_target_pairs={{0,32},{16,48},{32,0},{48,16},{64,96},{80,112},{96,64},{112,80},{1... | collective-permute-start | bytes 786440 | tf_op jit(solution)/shard_map/ppermute | solution.py:337
  40.2 4.9 %all-to-all-done.1.own_ref = bf16[16,2,16,256]{3,2,1,0:T(8,128)(2,1)S(1)} async-done(((bf16[16,2,16,256]{3,2,1,0:T(8,128)(2,1)}), bf16[16,2,16,256]{3,2,1,0:T(8,128)(2,1)S(1)}, u32[]{:S(2)}, u32[]{:S(2)}) %all-to-all-start.1) | async-done | bytes 262176 | tf_op jit(solution)/shard_map/all_to_all | solution.py:333
  45.1 1.9 %collective-permute-start.1 = (bf16[16,2,16,256]{3,2,1,0:T(8,128)(2,1)S(1)}, bf16[16,2,16,256]{3,2,1,0:T(8,128)(2,1)S(1)}, u32[]{:S(2)}, u32[]{:S(2)}) collective-permute-start(bf16[16,2,16,256]{3,2,1,0:T(8,128)(2,1)S(1)} %all-to-all-done.1.own_ref), channel_id=1, source_target_pairs={{0,16},{16,0},{32,48},{48,32},{64,80},{80,64},{96,112},{112,96},{1... | collective-permute-start | bytes 786440 | tf_op jit(solution)/shard_map/ppermute | solution.py:337
  47.0 2.1 %collective-permute-start.3 = (bf16[16,2,16,256]{3,2,1,0:T(8,128)(2,1)S(1)}, bf16[16,2,16,256]{3,2,1,0:T(8,128)(2,1)S(1)}, u32[]{:S(2)}, u32[]{:S(2)}) collective-permute-start(bf16[16,2,16,256]{3,2,1,0:T(8,128)(2,1)S(1)} %all-to-all-done.1.own_ref), channel_id=1, source_target_pairs={{0,496},{16,32},{32,16},{48,64},{64,48},{80,96},{96,80},{112,128},... | collective-permute-start | bytes 786440 | tf_op jit(solution)/shard_map/ppermute | solution.py:337
  49.2 0.1 pad_add_fusion.index_ref
  49.3 0.0 collective-permute-done.2.foreign_ref
  49.3 0.0 collective-permute-done.1.near_ref
  49.3 2.2 %first.1 = (f32[256,256]{1,0:T(8,128)}, f32[4,16,256]{2,1,0:T(8,128)}) custom-call(s32[4]{0:T(128)S(1)} %pad_add_fusion.index_ref, bf16[16,2,16,256]{3,2,1,0:T(8,128)(2,1)S(1)} %all-to-all-done.1.own_ref, bf16[16,2,16,256]{3,2,1,0:T(8,128)(2,1)S(1)} %collective-permute-done.1.near_ref, f32[256,256]{1,0:T(8,128)S(1)} %bitcast.15, ...), custom_call_target="tpu_custom_call" | custom-call | bytes 4194304 | tf_op jit(solution)/shard_map/first/pallas_call | solution.py:387
  51.4 8.7 %all-to-all-start.2 = ((f32[4,16,256]{2,1,0:T(8,128)}), f32[4,16,256]{2,1,0:T(8,128)S(1)}, u32[]{:S(2)}, u32[]{:S(2)}) async-start(f32[4,16,256]{2,1,0:T(8,128)} %get-tuple-element.17.after_ref), calls=%async_computation.2 | async-start | bytes 131072 | tf_op jit(solution)/shard_map/all_to_all | solution.py:333
  60.1 0.0 collective-permute-done.3.far_ref
  60.1 0.0 copy-done.2
  60.1 0.7 copy-done.3
  60.8 6.2 %gradient.1 = (bf16[4096,256]{1,0:T(8,128)(2,1)}, bf16[4096,256]{1,0:T(8,128)(2,1)}, bf16[16,40,256]{2,1,0:T(8,128)(2,1)S(1)}) custom-call(s32[4]{0:T(128)S(1)} %pad_add_fusion.index_ref, bf16[256,256]{1,0:T(8,128)(2,1)} %bitcast.20, bf16[16,2,16,256]{3,2,1,0:T(8,128)(2,1)} %copy-done.2, bf16[16,2,16,256]{3,2,1,0:T(8,128)(2,1)} %copy-done.3, ...), custom_call_target="tpu_custom_call" | custom-call | flops 2147483648 | bytes 4194304 | tf_op jit(solution)/shard_map/gradient/pallas_call | solution.py:395
  67.1 0.0 all-to-all-done.2.got_ref
  67.1 0.1 pack.1
  67.2 15.0 %all_to_all.30.got_ref = bf16[16,104,256]{2,1,0:T(8,128)(2,1)S(1)} all-to-all(bf16[16,104,256]{2,1,0:T(8,128)(2,1)S(1)} %pack.1), channel_id=1, replica_groups=mesh['blk'=32,'bond'=16] {'bond'}, dimensions={0} | all-to-all | bytes 1703936 | tf_op jit(solution)/shard_map/all_to_all | solution.py:333
  82.1 2.0 %second.1 = (f32[256,256]{1,0:T(8,128)S(1)}, f32[4,16,256]{2,1,0:T(8,128)S(1)}, bf16[32,256]{1,0:T(8,128)(2,1)S(1)}, f32[8,256]{1,0:T(8,128)S(1)}) custom-call(s32[4]{0:T(128)S(1)} %pad_add_fusion.index_ref, bf16[16,104,256]{2,1,0:T(8,128)(2,1)S(1)} %all_to_all.30.got_ref, f32[256,256]{1,0:T(8,128)} %get-tuple-element.21.old_ref, f32[256,256]{1,0:T(8,128)S(1)} %bitcast.16), custom_call_target="tpu_custom_call" | custom-call | bytes 4194304 | tf_op jit(solution)/shard_map/second/pallas_call | solution.py:423
  84.1 22.4 %all_to_all.31.got_ref = f32[4,16,256]{2,1,0:T(8,128)S(1)} all-to-all(f32[4,16,256]{2,1,0:T(8,128)S(1)} %get-tuple-element.22), channel_id=1, replica_groups={{0,128,256,384},{16,144,272,400},{32,160,288,416},{48,176,304,432},{64,..., dimensions={0} | all-to-all | bytes 131072 | tf_op jit(solution)/shard_map/all_to_all | solution.py:333
  106.6 13.2 %all_to_all.32.got_ref = bf16[16,64,256]{2,1,0:T(8,128)(2,1)S(1)} all-to-all(bf16[16,64,256]{2,1,0:T(8,128)(2,1)S(1)} %repeat.1), channel_id=1, replica_groups=mesh['blk'=32,'bond'=16] {'bond'}, dimensions={0} | all-to-all | bytes 1048576 | tf_op jit(solution)/shard_map/all_to_all | solution.py:333
  119.8 8.1 %final.1 = (f32[256,256]{1,0:T(8,128)}, bf16[256,16,256]{2,1,0:T(8,128)(2,1)}) custom-call(bf16[16,64,256]{2,1,0:T(8,128)(2,1)S(1)} %all_to_all.32.got_ref, f32[8,256]{1,0:T(8,128)S(1)} %get-tuple-element.24.extra_ref, f32[256,256]{1,0:T(8,128)S(1)} %get-tuple-element.25.old_ref, f32[256,256]{1,0:T(8,128)S(1)} %bitcast.17, ...), custom_call_target="tpu_custom_call" | custom-call | flops 2684354560 | bytes 4194304 | tf_op jit(solution)/shard_map/final/pallas_call | solution.py:435
  (4 shorter events, 0.0 us)
Async XLA Ops:
  0.6 14.3 %copy-start.1 = (f32[1,256,256]{2,1,0:T(8,128)S(1)}, f32[1,256,256]{2,1,0:T(8,128)}, u32[]{:S(2)}) copy-start(f32[1,256,256]{2,1,0:T(8,128)} %param.7) | copy-start | bytes 786436
  0.6 23.5 %copy-start = (bf16[1,256,16,256]{3,2,1,0:T(8,128)(2,1)S(1)}, bf16[1,256,16,256]{3,2,1,0:T(8,128)(2,1)}, u32[]{:S(2)}) copy-start(bf16[1,256,16,256]{3,2,1,0:T(8,128)(2,1)} %param.4) | copy-start | bytes 6291460
  7.9 20.5 %all-to-all-start = ((f32[16,2,16,256]{3,2,1,0:T(8,128)}), f32[16,2,16,256]{3,2,1,0:T(8,128)S(1)}, u32[]{:S(2)}, u32[]{:S(2)}) async-start(f32[16,2,16,256]{3,2,1,0:T(8,128)} %ascend.1.after_ref), calls=%async_computation | async-start | bytes 1048576 | tf_op jit(solution)/shard_map/all_to_all | solution.py:333
  15.0 13.4 %collective-permute-start = (f32[16,256]{1,0:T(8,128)S(1)}, f32[16,256]{1,0:T(8,128)S(1)}, u32[]{:S(2)}, u32[]{:S(2)}) collective-permute-start(f32[16,256]{1,0:T(8,128)S(1)} %dynamic-slice_bitcast_fusion), channel_id=1, source_target_pairs={{0,128},{16,144},{32,160},{48,176},{64,192},{80,208},{96,224},{112... | collective-permute-start | bytes 49160 | tf_op jit(solution)/shard_map/ppermute | solution.py:337
  29.2 15.9 %all-to-all-start.1 = ((bf16[16,2,16,256]{3,2,1,0:T(8,128)(2,1)}), bf16[16,2,16,256]{3,2,1,0:T(8,128)(2,1)S(1)}, u32[]{:S(2)}, u32[]{:S(2)}) async-start(bf16[16,2,16,256]{3,2,1,0:T(8,128)(2,1)} %rounded.1), calls=%async_computation.1 | async-start | bytes 524288 | tf_op jit(solution)/shard_map/all_to_all | solution.py:333
  36.4 12.9 %collective-permute-start.2 = (f32[256,256]{1,0:T(8,128)S(1)}, f32[256,256]{1,0:T(8,128)S(1)}, u32[]{:S(2)}, u32[]{:S(2)}) collective-permute-start(f32[256,256]{1,0:T(8,128)S(1)} %bitcast.14), channel_id=1, source_target_pairs={{0,32},{16,48},{32,0},{48,16},{64,96},{80,112},{96,64},{112,80},{1... | collective-permute-start | bytes 786440 | tf_op jit(solution)/shard_map/ppermute | solution.py:337
  45.1 4.2 %collective-permute-start.1 = (bf16[16,2,16,256]{3,2,1,0:T(8,128)(2,1)S(1)}, bf16[16,2,16,256]{3,2,1,0:T(8,128)(2,1)S(1)}, u32[]{:S(2)}, u32[]{:S(2)}) collective-permute-start(bf16[16,2,16,256]{3,2,1,0:T(8,128)(2,1)S(1)} %all-to-all-done.1.own_ref), channel_id=1, source_target_pairs={{0,16},{16,0},{32,48},{48,32},{64,80},{80,64},{96,112},{112,96},{1... | collective-permute-start | bytes 786440 | tf_op jit(solution)/shard_map/ppermute | solution.py:337
  47.0 13.1 %collective-permute-start.3 = (bf16[16,2,16,256]{3,2,1,0:T(8,128)(2,1)S(1)}, bf16[16,2,16,256]{3,2,1,0:T(8,128)(2,1)S(1)}, u32[]{:S(2)}, u32[]{:S(2)}) collective-permute-start(bf16[16,2,16,256]{3,2,1,0:T(8,128)(2,1)S(1)} %all-to-all-done.1.own_ref), channel_id=1, source_target_pairs={{0,496},{16,32},{32,16},{48,64},{64,48},{80,96},{96,80},{112,128},... | collective-permute-start | bytes 786440 | tf_op jit(solution)/shard_map/ppermute | solution.py:337
  49.3 10.9 %copy-start.2 = (bf16[16,2,16,256]{3,2,1,0:T(8,128)(2,1)}, bf16[16,2,16,256]{3,2,1,0:T(8,128)(2,1)S(1)}, u32[]{:S(2)}) copy-start(bf16[16,2,16,256]{3,2,1,0:T(8,128)(2,1)S(1)} %collective-permute-done.1.near_ref) | copy-start | bytes 786436
  51.4 15.6 %all-to-all-start.2 = ((f32[4,16,256]{2,1,0:T(8,128)}), f32[4,16,256]{2,1,0:T(8,128)S(1)}, u32[]{:S(2)}, u32[]{:S(2)}) async-start(f32[4,16,256]{2,1,0:T(8,128)} %get-tuple-element.17.after_ref), calls=%async_computation.2 | async-start | bytes 131072 | tf_op jit(solution)/shard_map/all_to_all | solution.py:333
  60.1 0.7 copy-start.3

commit v5 on v4

--- a/solution.py
+++ b/solution.py
@@ -102,15 +102,19 @@
     for copy in edge_copies:
         copy.wait()
     edges = edge_ref[...]
-    for b in range(ROWS):
-        block = bond_slice(wide_ref, b)
-        here = slice(b * SIZE, (b + 1) * SIZE)
-        turned_ref[:, here] = block.T
-        for k, part in enumerate(split(mm(edges, block))):
-            mapped_ref[k, here, :SIZE] = part[:SIZE]
-            mapped_ref[k, here, SIZE:] = part[SIZE:]
-    turned = turned_ref[...]
-    total = mm(turned, mapped_ref[0]) + mm(turned, mapped_ref[1])
+    total = jnp.zeros((SIZE, 2 * SIZE), f32)
+    for b in range(ROWS + 2):
+        if b < ROWS:
+            block = bond_slice(wide_ref, b)
+            here = slice(b * SIZE, (b + 1) * SIZE)
+            turned_ref[:, here] = block.T
+            for k, part in enumerate(split(mm(edges, block))):
+                mapped_ref[k, here, :SIZE] = part[:SIZE]
+                mapped_ref[k, here, SIZE:] = part[SIZE:]
+        if b >= 2 and b % 2 == 1:
+            past = slice((b - 3) * SIZE, (b - 1) * SIZE)
+            turned = turned_ref[:, past]
+            total = total + (mm(turned, mapped_ref[0, past]) + mm(turned, mapped_ref[1, past]))
     for k in range(2):
         out_ref[:, k] = total[:, k * SIZE : (k + 1) * SIZE].reshape(WIDTH, ROWS, SIZE)
 
@@ -177,22 +181,23 @@
     from_right = jnp.where(odd, whole(far_ref, 0), whole(near_ref, 0))
     mix = (edge_ref[...].astype(f32) + from_left + from_right).astype(bf16)
     squares = jnp.zeros((8, SIZE), f32)
+    outgoing = []
     for b in range(ROWS):
-        if b % (ROWS // CHUNKS) == 0:
-            at = 2 * b // (ROWS // CHUNKS)
-            copies[at].wait()
-            copies[at + 1].wait()
+        i, first_of = divmod(b, ROWS // CHUNKS)
+        if first_of == 0:
+            copies[2 * i].wait()
+            copies[2 * i + 1].wait()
         here = slice(b * SIZE, (b + 1) * SIZE)
         moved = mm(mix, block_ref[here])
         squares = squares + jnp.sum((moved * moved).reshape(SIZE // 8, 8, SIZE), axis=0)
         moved_ref[here], low_ref[here] = split(moved)
         flipped_ref[:, here] = mm(turned_ref[:, here], mix, NT).astype(bf16)
-    outgoing = [
-        pltpu.make_async_copy(moved_ref, hi_hbm, sems.at[2 * CHUNKS]),
-        pltpu.make_async_copy(low_ref, lo_hbm, sems.at[2 * CHUNKS + 1]),
-    ]
-    for copy in outgoing:
-        copy.start()
+        if first_of == ROWS // CHUNKS - 1:
+            here = pl.ds(i * step, step)
+            for k, (ref, hbm) in enumerate(((moved_ref, hi_hbm), (low_ref, lo_hbm))):
+                copy = pltpu.make_async_copy(ref.at[here], hbm.at[here], sems.at[2 * (CHUNKS + i) + k])
+                copy.start()
+                outgoing.append(copy)
     part_q = mm(turned_ref[...], moved_ref[...])
     part_r = mm(flipped_ref[...], moved_ref[...])
     part_n = norm_ref[...]
@@ -288,25 +293,19 @@
     return ph, pl_, mm(top, ph) + mm(top, pl_)
 
 
-def final_kernel(got_ref, extra_ref, old_ref, couple_ref, block_hbm, hi_hbm, lo_hbm, env_hbm, out_hbm, map_ref, block_ref, hi_ref, lo_ref, env_ref, wide_ref, out_ref, sems):
-    incoming = [
-        pltpu.make_async_copy(hi_hbm, hi_ref, sems.at[0]),
-        pltpu.make_async_copy(lo_hbm, lo_ref, sems.at[1]),
-        pltpu.make_async_copy(block_hbm, block_ref, sems.at[2]),
-    ]
-    for copy in incoming:
-        copy.start()
+def final_kernel(got_ref, extra_ref, old_ref, couple_ref, hi_ref, lo_ref, block_hbm, env_hbm, out_hbm, map_ref, env_ref, block_ref, wide_ref, out_ref, sems):
+    incoming = pltpu.make_async_copy(block_hbm, block_ref, sems.at[1 + PARTS])
+    incoming.start()
     env = two_levels(old_ref, got_ref, couple_ref)
     env_ref[...] = env
-    outgoing = [pltpu.make_async_copy(env_ref, env_hbm, sems.at[3])]
+    outgoing = [pltpu.make_async_copy(env_ref, env_hbm, sems.at[0])]
     outgoing[0].start()
     full_q = got_ref[:, 2 * ROWS : 3 * ROWS].astype(f32).reshape(SIZE, SIZE)
     full_s = got_ref[:, 3 * ROWS :].astype(f32).reshape(SIZE, SIZE)
     ph, pl_, low = polar_matrices(env, full_q, full_s, extra_ref)
     for k, part in enumerate((ph, ph, pl_, *split(low))):
         map_ref[k * SIZE : (k + 1) * SIZE] = part
-    for copy in incoming:
-        copy.wait()
+    incoming.wait()
     step = SIZE // PARTS
     for i in range(PARTS):
         for b in range(ROWS):
@@ -322,7 +321,7 @@
         for h in range(2):
             part = wide_ref[h, lines].astype(bf16).reshape(step, ROWS, HALF)
             out_ref[here, :, h * HALF : (h + 1) * HALF] = part
-        copy = pltpu.make_async_copy(out_ref.at[here], out_hbm.at[here], sems.at[4 + i])
+        copy = pltpu.make_async_copy(out_ref.at[here], out_hbm.at[here], sems.at[1 + i])
         copy.start()
         outgoing.append(copy)
     for copy in outgoing:
@@ -402,13 +401,13 @@
             pltpu.VMEM((SIZE, FLAT), bf16),
             pltpu.VMEM((FLAT, SIZE), bf16),
             pltpu.VMEM((SIZE, FLAT), bf16),
-            pltpu.SemaphoreType.DMA((2 * CHUNKS + 2,)),
+            pltpu.SemaphoreType.DMA((4 * CHUNKS,)),
         ],
         in_specs=[pl.BlockSpec(memory_space=pltpu.SMEM)] + [vmem] * 4 + [any_place] * 3,
         out_specs=[any_place] * 2 + [vmem],
         flops=4 << 29,
         grant=20,
-    )(index, in_hbm(edge), in_hbm(near), in_hbm(far), norm, in_hbm(block), in_hbm(turned), after)
+    )(index, in_hbm(edge), in_hbm(near), far, norm, in_hbm(block), in_hbm(turned), after)
 
 
 def pack(got, parts, foreign):
@@ -429,7 +428,7 @@
     )(index, got, in_hbm(old), couple)
 
 
-def final(got, extra, old, couple, block, hi, lo):
+def final(got, extra, old, couple, hi, lo, block):
     vmem = pl.BlockSpec(memory_space=pltpu.VMEM)
     any_place = pl.BlockSpec(memory_space=pl.ANY)
     return call(
@@ -438,19 +437,17 @@
         [pltpu.HBM((SIZE, SIZE), f32), pltpu.HBM((SIZE, ROWS, SIZE), bf16)],
         scratch=[
             pltpu.VMEM((5 * SIZE, SIZE), bf16),
+            pltpu.VMEM((SIZE, SIZE), f32),
             pltpu.VMEM((FLAT, SIZE), bf16),
-            pltpu.VMEM((FLAT, SIZE), bf16),
-            pltpu.VMEM((FLAT, SIZE), bf16),
-            pltpu.VMEM((SIZE, SIZE), f32),
             pltpu.VMEM((2, FLAT, HALF), f32),
             pltpu.VMEM((SIZE, ROWS, SIZE), bf16),
-            pltpu.SemaphoreType.DMA((4 + PARTS,)),
+            pltpu.SemaphoreType.DMA((2 + PARTS,)),
         ],
-        in_specs=[vmem] * 4 + [any_place] * 3,
+        in_specs=[vmem] * 6 + [any_place],
         out_specs=[any_place] * 2,
         flops=5 << 29,
-        grant=24,
-    )(got, extra, old, couple, in_hbm(block), in_hbm(hi), in_hbm(lo))
+        grant=20,
+    )(got, extra, old, couple, hi, lo, in_hbm(block))
 
 
 def body(iso, edge_left, edge_right, coupling):
@@ -481,7 +478,7 @@
     env, outgoing, sums, extra = second(index, got, env, couple)
     incoming = exchange(outgoing, "blk", strides)
     got = exchange(repeat(incoming, sums), "bond")
-    env, out = final(got, extra, env, couple, block, moved_hi, moved_lo)
+    env, out = final(got, extra, env, couple, moved_hi, moved_lo, block)
     return (out[None], env[None])
 
 

time: 129 us -> 126 us (0.977)
  Pallas kernels: 30.9 us -> 28.6 us
  transfers between devices with their start and end apart: 7 -> 7, of which waited for: 1 -> 1; matrix products, arithmetic and copies ran while one was open for 0% -> 0% of each run, Pallas kernels for 10% -> 9%
where the time goes in v5:
time: 126 us; the launch traced here: 125 us
  blocking collectives  50.9 us (40%)
  starting transfers between devices  39.9 us (32%)
  Pallas kernels  28.6 us (23%)
  waiting for transfers between devices  4.88 us (4%)
    all_to_all x3, blocking collectives, exchange(): return lax.all_to_all(x, axis, 0, 0, axis_index_groups=groups, tiled=True)  50.9 us
    all_to_all x3, starting transfers between devices, exchange(): return lax.all_to_all(x, axis, 0, 0, axis_index_groups=groups, tiled=True)  22.9 us
    ppermute x4, starting transfers between devices, permuted(): lax.ppermute(x, axis, [(i, route(i)) for i in range(lax.axis_size(axis))])  16.9 us
    pallas_call x1, Pallas kernels, final(): call(final_kernel, 'final', [pltpu.HBM((SIZE, SIZE), f32), pltpu.HBM((SIZ...  7.42 us
    pallas_call x1, Pallas kernels, ascend(): call(ascend_kernel, 'ascend', [((WIDTH, 2, ROWS, SIZE), f32)], scratch=[p...  6.61 us
    pallas_call x1, Pallas kernels, gradient(): call(gradient_kernel, 'gradient', [pltpu.HBM((FLAT, SIZE), bf16), pltpu.H...  5.31 us
    all_to_all x3, waiting for transfers between devices, exchange(): return lax.all_to_all(x, axis, 0, 0, axis_index_groups=groups, tiled=True)  4.87 us
    pallas_call x1, Pallas kernels, prepare(): call(prepare_kernel, 'prepare', [pltpu.HBM((FLAT, SIZE), bf16), pltpu.HBM...  4.29 us
  transfers between devices with their start and end apart: 7, of which 1 were waited for; matrix products, arithmetic and copies ran while one was open for 0% of the time, Pallas kernels for 9%

profile of v5, /device:TPU:64, one launch (start us, length us, event | category | flops | bytes accessed | tf_op | source)
XLA Modules:
  0.0 125.4 jit_solution(5722660425939866635)
XLA Ops:
  0.6 0.0 copy-start.1
  0.6 0.0 copy-start
  0.6 6.6 %ascend.1.after_ref = f32[16,2,16,256]{3,2,1,0:T(8,128)} custom-call(bf16[256,16,256]{2,1,0:T(8,128)(2,1)} %bitcast.12, bf16[256,256]{1,0:T(8,128)(2,1)} %bitcast.19, bf16[256,256]{1,0:T(8,128)(2,1)} %bitcast.18), custom_call_target="tpu_custom_call" | custom-call | flops 3221225472 | bytes 4194304 | tf_op jit(solution)/shard_map/ascend/pallas_call | solution.py:345
  7.3 7.1 %all-to-all-start = ((f32[16,2,16,256]{3,2,1,0:T(8,128)}), f32[16,2,16,256]{3,2,1,0:T(8,128)S(1)}, u32[]{:S(2)}, u32[]{:S(2)}) async-start(f32[16,2,16,256]{3,2,1,0:T(8,128)} %ascend.1.after_ref), calls=%async_computation | async-start | bytes 1048576 | tf_op jit(solution)/shard_map/all_to_all | solution.py:332
  14.3 0.0 copy-done.1
  14.4 9.1 %collective-permute-start = (f32[16,256]{1,0:T(8,128)S(1)}, f32[16,256]{1,0:T(8,128)S(1)}, u32[]{:S(2)}, u32[]{:S(2)}) collective-permute-start(f32[16,256]{1,0:T(8,128)S(1)} %dynamic-slice_bitcast_fusion), channel_id=1, source_target_pairs={{0,128},{16,144},{32,160},{48,176},{64,192},{80,208},{96,224},{112... | collective-permute-start | bytes 49160 | tf_op jit(solution)/shard_map/ppermute | solution.py:336
  23.5 0.0 copy-done
  23.5 4.3 %prepare.1 = (bf16[4096,256]{1,0:T(8,128)(2,1)}, bf16[256,4096]{1,0:T(8,128)(2,1)}, f32[256,256]{1,0:T(8,128)S(1)}) custom-call(bf16[256,16,256]{2,1,0:T(8,128)(2,1)S(1)} %bitcast.13, f32[16,2,16,256]{3,2,1,0:T(8,128)} %ascend.1.after_ref), custom_call_target="tpu_custom_call" | custom-call | flops 536870912 | bytes 4194304 | tf_op jit(solution)/shard_map/prepare/pallas_call | solution.py:365
  27.8 0.0 collective-permute-done.also_ref.foreign_ref
  27.8 0.0 all-to-all-done.got_ref
  27.8 0.8 rounded.1
  28.5 7.2 %all-to-all-start.1 = ((bf16[16,2,16,256]{3,2,1,0:T(8,128)(2,1)}), bf16[16,2,16,256]{3,2,1,0:T(8,128)(2,1)S(1)}, u32[]{:S(2)}, u32[]{:S(2)}) async-start(bf16[16,2,16,256]{3,2,1,0:T(8,128)(2,1)} %rounded.1), calls=%async_computation.1 | async-start | bytes 524288 | tf_op jit(solution)/shard_map/all_to_all | solution.py:332
  35.8 3.8 %collective-permute-start.2 = (f32[256,256]{1,0:T(8,128)S(1)}, f32[256,256]{1,0:T(8,128)S(1)}, u32[]{:S(2)}, u32[]{:S(2)}) collective-permute-start(f32[256,256]{1,0:T(8,128)S(1)} %bitcast.14), channel_id=1, source_target_pairs={{0,32},{16,48},{32,0},{48,16},{64,96},{80,112},{96,64},{112,80},{1... | collective-permute-start | bytes 786440 | tf_op jit(solution)/shard_map/ppermute | solution.py:336
  39.6 4.9 %all-to-all-done.1.own_ref = bf16[16,2,16,256]{3,2,1,0:T(8,128)(2,1)S(1)} async-done(((bf16[16,2,16,256]{3,2,1,0:T(8,128)(2,1)}), bf16[16,2,16,256]{3,2,1,0:T(8,128)(2,1)S(1)}, u32[]{:S(2)}, u32[]{:S(2)}) %all-to-all-start.1) | async-done | bytes 262176 | tf_op jit(solution)/shard_map/all_to_all | solution.py:332
  44.4 1.9 %collective-permute-start.1 = (bf16[16,2,16,256]{3,2,1,0:T(8,128)(2,1)S(1)}, bf16[16,2,16,256]{3,2,1,0:T(8,128)(2,1)S(1)}, u32[]{:S(2)}, u32[]{:S(2)}) collective-permute-start(bf16[16,2,16,256]{3,2,1,0:T(8,128)(2,1)S(1)} %all-to-all-done.1.own_ref), channel_id=1, source_target_pairs={{0,16},{16,0},{32,48},{48,32},{64,80},{80,64},{96,112},{112,96},{1... | collective-permute-start | bytes 786440 | tf_op jit(solution)/shard_map/ppermute | solution.py:336
  46.4 2.1 %collective-permute-start.3 = (bf16[16,2,16,256]{3,2,1,0:T(8,128)(2,1)S(1)}, bf16[16,2,16,256]{3,2,1,0:T(8,128)(2,1)S(1)}, u32[]{:S(2)}, u32[]{:S(2)}) collective-permute-start(bf16[16,2,16,256]{3,2,1,0:T(8,128)(2,1)S(1)} %all-to-all-done.1.own_ref), channel_id=1, source_target_pairs={{0,496},{16,32},{32,16},{48,64},{64,48},{80,96},{96,80},{112,128},... | collective-permute-start | bytes 786440 | tf_op jit(solution)/shard_map/ppermute | solution.py:336
  48.5 0.1 pad_add_fusion.index_ref
  48.6 0.0 collective-permute-done.2.foreign_ref
  48.6 0.0 collective-permute-done.1.near_ref
  48.6 2.2 %first.1 = (f32[256,256]{1,0:T(8,128)}, f32[4,16,256]{2,1,0:T(8,128)}) custom-call(s32[4]{0:T(128)S(1)} %pad_add_fusion.index_ref, bf16[16,2,16,256]{3,2,1,0:T(8,128)(2,1)S(1)} %all-to-all-done.1.own_ref, bf16[16,2,16,256]{3,2,1,0:T(8,128)(2,1)S(1)} %collective-permute-done.1.near_ref, f32[256,256]{1,0:T(8,128)S(1)} %bitcast.15, ...), custom_call_target="tpu_custom_call" | custom-call | bytes 4194304 | tf_op jit(solution)/shard_map/first/pallas_call | solution.py:386
  50.8 8.7 %all-to-all-start.2 = ((f32[4,16,256]{2,1,0:T(8,128)}), f32[4,16,256]{2,1,0:T(8,128)S(1)}, u32[]{:S(2)}, u32[]{:S(2)}) async-start(f32[4,16,256]{2,1,0:T(8,128)} %get-tuple-element.17.after_ref), calls=%async_computation.2 | async-start | bytes 131072 | tf_op jit(solution)/shard_map/all_to_all | solution.py:332
  59.5 0.0 collective-permute-done.3.far_ref
  59.5 0.0 copy-done.2
  59.5 5.3 %gradient.1 = (bf16[4096,256]{1,0:T(8,128)(2,1)}, bf16[4096,256]{1,0:T(8,128)(2,1)}, bf16[16,40,256]{2,1,0:T(8,128)(2,1)S(1)}) custom-call(s32[4]{0:T(128)S(1)} %pad_add_fusion.index_ref, bf16[256,256]{1,0:T(8,128)(2,1)} %bitcast.20, bf16[16,2,16,256]{3,2,1,0:T(8,128)(2,1)} %copy-done.2, bf16[16,2,16,256]{3,2,1,0:T(8,128)(2,1)S(1)} %collective-permute-done.3.far_ref, ...), custom_call_target="tpu_custom_call" | custom-call | flops 2147483648 | bytes 4194304 | tf_op jit(solution)/shard_map/gradient/pallas_call | solution.py:394
  64.8 0.0 all-to-all-done.2.got_ref
  64.8 0.1 pack.1
  64.9 15.3 %all_to_all.30.got_ref = bf16[16,104,256]{2,1,0:T(8,128)(2,1)S(1)} all-to-all(bf16[16,104,256]{2,1,0:T(8,128)(2,1)S(1)} %pack.1), channel_id=1, replica_groups=mesh['blk'=32,'bond'=16] {'bond'}, dimensions={0} | all-to-all | bytes 1703936 | tf_op jit(solution)/shard_map/all_to_all | solution.py:332
  80.1 2.0 %second.1 = (f32[256,256]{1,0:T(8,128)S(1)}, f32[4,16,256]{2,1,0:T(8,128)S(1)}, bf16[32,256]{1,0:T(8,128)(2,1)S(1)}, f32[8,256]{1,0:T(8,128)S(1)}) custom-call(s32[4]{0:T(128)S(1)} %pad_add_fusion.index_ref, bf16[16,104,256]{2,1,0:T(8,128)(2,1)S(1)} %all_to_all.30.got_ref, f32[256,256]{1,0:T(8,128)} %get-tuple-element.21.old_ref, f32[256,256]{1,0:T(8,128)S(1)} %bitcast.16), custom_call_target="tpu_custom_call" | custom-call | bytes 4194304 | tf_op jit(solution)/shard_map/second/pallas_call | solution.py:422
  82.1 22.4 %all_to_all.31.got_ref = f32[4,16,256]{2,1,0:T(8,128)S(1)} all-to-all(f32[4,16,256]{2,1,0:T(8,128)S(1)} %get-tuple-element.22), channel_id=1, replica_groups={{0,128,256,384},{16,144,272,400},{32,160,288,416},{48,176,304,432},{64,..., dimensions={0} | all-to-all | bytes 131072 | tf_op jit(solution)/shard_map/all_to_all | solution.py:332
  104.6 13.2 %all_to_all.32.got_ref = bf16[16,64,256]{2,1,0:T(8,128)(2,1)S(1)} all-to-all(bf16[16,64,256]{2,1,0:T(8,128)(2,1)S(1)} %repeat.1), channel_id=1, replica_groups=mesh['blk'=32,'bond'=16] {'bond'}, dimensions={0} | all-to-all | bytes 1048576 | tf_op jit(solution)/shard_map/all_to_all | solution.py:332
  117.8 0.0 copy-done.3
  117.8 7.4 %final.1 = (f32[256,256]{1,0:T(8,128)}, bf16[256,16,256]{2,1,0:T(8,128)(2,1)}) custom-call(bf16[16,64,256]{2,1,0:T(8,128)(2,1)S(1)} %all_to_all.32.got_ref, f32[8,256]{1,0:T(8,128)S(1)} %get-tuple-element.24.extra_ref, f32[256,256]{1,0:T(8,128)S(1)} %get-tuple-element.25.old_ref, f32[256,256]{1,0:T(8,128)S(1)} %bitcast.17, bf16[4096,256]{1,0:T(8,128)(2,1)S(1)} %copy-done.3, ...), custom_call_target="tpu_custom_call" | custom-call | flops 2684354560 | bytes 4194304 | tf_op jit(solution)/shard_map/final/pallas_call | solution.py:434
  (6 shorter events, 0.1 us)
Async XLA Ops:
  0.6 13.7 %copy-start.1 = (f32[1,256,256]{2,1,0:T(8,128)S(1)}, f32[1,256,256]{2,1,0:T(8,128)}, u32[]{:S(2)}) copy-start(f32[1,256,256]{2,1,0:T(8,128)} %param.7) | copy-start | bytes 786436
  0.6 22.8 %copy-start = (bf16[1,256,16,256]{3,2,1,0:T(8,128)(2,1)S(1)}, bf16[1,256,16,256]{3,2,1,0:T(8,128)(2,1)}, u32[]{:S(2)}) copy-start(bf16[1,256,16,256]{3,2,1,0:T(8,128)(2,1)} %param.4) | copy-start | bytes 6291460
  7.3 20.5 %all-to-all-start = ((f32[16,2,16,256]{3,2,1,0:T(8,128)}), f32[16,2,16,256]{3,2,1,0:T(8,128)S(1)}, u32[]{:S(2)}, u32[]{:S(2)}) async-start(f32[16,2,16,256]{3,2,1,0:T(8,128)} %ascend.1.after_ref), calls=%async_computation | async-start | bytes 1048576 | tf_op jit(solution)/shard_map/all_to_all | solution.py:332
  14.4 13.4 %collective-permute-start = (f32[16,256]{1,0:T(8,128)S(1)}, f32[16,256]{1,0:T(8,128)S(1)}, u32[]{:S(2)}, u32[]{:S(2)}) collective-permute-start(f32[16,256]{1,0:T(8,128)S(1)} %dynamic-slice_bitcast_fusion), channel_id=1, source_target_pairs={{0,128},{16,144},{32,160},{48,176},{64,192},{80,208},{96,224},{112... | collective-permute-start | bytes 49160 | tf_op jit(solution)/shard_map/ppermute | solution.py:336
  28.5 15.9 %all-to-all-start.1 = ((bf16[16,2,16,256]{3,2,1,0:T(8,128)(2,1)}), bf16[16,2,16,256]{3,2,1,0:T(8,128)(2,1)S(1)}, u32[]{:S(2)}, u32[]{:S(2)}) async-start(bf16[16,2,16,256]{3,2,1,0:T(8,128)(2,1)} %rounded.1), calls=%async_computation.1 | async-start | bytes 524288 | tf_op jit(solution)/shard_map/all_to_all | solution.py:332
  35.8 12.9 %collective-permute-start.2 = (f32[256,256]{1,0:T(8,128)S(1)}, f32[256,256]{1,0:T(8,128)S(1)}, u32[]{:S(2)}, u32[]{:S(2)}) collective-permute-start(f32[256,256]{1,0:T(8,128)S(1)} %bitcast.14), channel_id=1, source_target_pairs={{0,32},{16,48},{32,0},{48,16},{64,96},{80,112},{96,64},{112,80},{1... | collective-permute-start | bytes 786440 | tf_op jit(solution)/shard_map/ppermute | solution.py:336
  44.4 4.2 %collective-permute-start.1 = (bf16[16,2,16,256]{3,2,1,0:T(8,128)(2,1)S(1)}, bf16[16,2,16,256]{3,2,1,0:T(8,128)(2,1)S(1)}, u32[]{:S(2)}, u32[]{:S(2)}) collective-permute-start(bf16[16,2,16,256]{3,2,1,0:T(8,128)(2,1)S(1)} %all-to-all-done.1.own_ref), channel_id=1, source_target_pairs={{0,16},{16,0},{32,48},{48,32},{64,80},{80,64},{96,112},{112,96},{1... | collective-permute-start | bytes 786440 | tf_op jit(solution)/shard_map/ppermute | solution.py:336
  46.4 13.1 %collective-permute-start.3 = (bf16[16,2,16,256]{3,2,1,0:T(8,128)(2,1)S(1)}, bf16[16,2,16,256]{3,2,1,0:T(8,128)(2,1)S(1)}, u32[]{:S(2)}, u32[]{:S(2)}) collective-permute-start(bf16[16,2,16,256]{3,2,1,0:T(8,128)(2,1)S(1)} %all-to-all-done.1.own_ref), channel_id=1, source_target_pairs={{0,496},{16,32},{32,16},{48,64},{64,48},{80,96},{96,80},{112,128},... | collective-permute-start | bytes 786440 | tf_op jit(solution)/shard_map/ppermute | solution.py:336
  48.6 10.8 %copy-start.2 = (bf16[16,2,16,256]{3,2,1,0:T(8,128)(2,1)}, bf16[16,2,16,256]{3,2,1,0:T(8,128)(2,1)S(1)}, u32[]{:S(2)}) copy-start(bf16[16,2,16,256]{3,2,1,0:T(8,128)(2,1)S(1)} %collective-permute-done.1.near_ref) | copy-start | bytes 786436
  50.8 14.0 %all-to-all-start.2 = ((f32[4,16,256]{2,1,0:T(8,128)}), f32[4,16,256]{2,1,0:T(8,128)S(1)}, u32[]{:S(2)}, u32[]{:S(2)}) async-start(f32[4,16,256]{2,1,0:T(8,128)} %get-tuple-element.17.after_ref), calls=%async_computation.2 | async-start | bytes 131072 | tf_op jit(solution)/shard_map/all_to_all | solution.py:332
  64.9 52.9 %copy-start.3 = (bf16[4096,256]{1,0:T(8,128)(2,1)S(1)}, bf16[4096,256]{1,0:T(8,128)(2,1)}, u32[]{:S(2)}) copy-start(bf16[4096,256]{1,0:T(8,128)(2,1)} %get-tuple-element.26.hi_ref) | copy-start | bytes 6291460
  64.9 52.9 %copy-start.4 = (bf16[4096,256]{1,0:T(8,128)(2,1)S(1)}, bf16[4096,256]{1,0:T(8,128)(2,1)}, u32[]{:S(2)}) copy-start(bf16[4096,256]{1,0:T(8,128)(2,1)} %get-tuple-element.27.lo_ref) | copy-start | bytes 6291460

commit v6 on v5

--- a/solution.py
+++ b/solution.py
@@ -17,6 +17,9 @@
 CHUNKS = 4
 EXTRA = 8
 PARTS = 2
+TOGETHER = 8
+SENDS = 4
+NEAR = 0.01
 
 
 def split(x):
@@ -31,7 +34,8 @@
 def mm3(a, b, dims=NN):
     ah, al = split(a)
     bh, bl = split(b)
-    return mm(ah, bh, dims) + (mm(ah, bl, dims) + mm(al, bh, dims))
+    rows = jnp.concatenate([ah, ah, al], axis=1)
+    return mm(rows, jnp.concatenate([bh, bl, bh], axis=dims[1][0]), dims)
 
 
 def sandwich(c, e):
@@ -266,7 +270,7 @@
 
 def mm2(a, b, dims=NN):
     ah, al = split(a)
-    return mm(ah, b, dims) + mm(al, b, dims)
+    return mm(jnp.concatenate([ah, al], axis=1), jnp.concatenate([b, b], axis=0), dims)
 
 
 def polar_matrices(env, full_q, full_s, extra_ref):
@@ -280,52 +284,76 @@
     half = full_q + 0.5 * mm2(full_n, top)
     hh, hl = split(half)
     turned = top.T
-    side = mm(turned, hh) + mm(turned, hl)
+    side = mm(jnp.concatenate([turned, turned], axis=1), jnp.concatenate([hh, hl], axis=0))
     gram = full_r + side + side.T
     trace = jnp.sum(jnp.where(on, gram, 0.0), keepdims=True)
     factor = lax.rsqrt(trace + 1e-06)
     g = gram * (factor * factor)
     g2 = mm3(g, g)
     eye = jnp.where(on, 1.0, 0.0)
-    poly = 2.25 * eye - 2.4375 * g + mm3(g2, 1.6875 * eye - 0.5625 * g + 0.0625 * g2)
-    poly = poly * factor
-    ph, pl_ = split(poly)
-    return ph, pl_, mm(top, ph) + mm(top, pl_)
-
-
-def final_kernel(got_ref, extra_ref, old_ref, couple_ref, hi_ref, lo_ref, block_hbm, env_hbm, out_hbm, map_ref, env_ref, block_ref, wide_ref, out_ref, sems):
-    incoming = pltpu.make_async_copy(block_hbm, block_ref, sems.at[1 + PARTS])
+    rest = mm3(g2, 1.6875 * eye - 0.5625 * g + 0.0625 * g2) - 2.4375 * g
+    ph, pl_ = split(factor * (2.25 * eye + rest))
+    low = mm(jnp.concatenate([top, top], axis=1), jnp.concatenate([ph, pl_], axis=0))
+    near_one = jnp.sum(g * g) <= NEAR
+    return ph, pl_, low, 2.25 * factor, (factor * rest).astype(bf16), near_one
+
+
+def final_kernel(got_ref, extra_ref, old_ref, couple_ref, hi_ref, lo_ref, block_hbm, env_hbm, out_hbm, map_ref, env_ref, block_ref, scale_ref, wide_ref, out_ref, sems):
+    incoming = pltpu.make_async_copy(block_hbm, block_ref, sems.at[1])
     incoming.start()
     env = two_levels(old_ref, got_ref, couple_ref)
     env_ref[...] = env
-    outgoing = [pltpu.make_async_copy(env_ref, env_hbm, sems.at[0])]
-    outgoing[0].start()
+    outgoing = pltpu.make_async_copy(env_ref, env_hbm, sems.at[0])
+    outgoing.start()
     full_q = got_ref[:, 2 * ROWS : 3 * ROWS].astype(f32).reshape(SIZE, SIZE)
     full_s = got_ref[:, 3 * ROWS :].astype(f32).reshape(SIZE, SIZE)
-    ph, pl_, low = polar_matrices(env, full_q, full_s, extra_ref)
-    for k, part in enumerate((ph, ph, pl_, *split(low))):
+    ph, pl_, low, scale, rest, near_one = polar_matrices(env, full_q, full_s, extra_ref)
+    lh, ll = split(low)
+    for k, part in enumerate((ph, ph, pl_, lh, ll, rest)):
         map_ref[k * SIZE : (k + 1) * SIZE] = part
+    scale_ref[...] = jnp.broadcast_to(scale, scale_ref.shape)
     incoming.wait()
     step = SIZE // PARTS
-    for i in range(PARTS):
-        for b in range(ROWS):
-            here = pl.ds(b * SIZE + i * step, step)
-            hi = hi_ref[here]
-            flat = block_ref[here]
-            rows = jnp.concatenate([hi, lo_ref[here], hi, flat, flat], axis=1)
-            value = mm(rows, map_ref[...])
-            for h in range(2):
-                wide_ref[h, pl.ds(i * step * ROWS + b, step, stride=ROWS), :] = value[:, h * HALF : (h + 1) * HALF]
-        lines = pl.ds(i * step * ROWS, step * ROWS)
-        here = pl.ds(i * step, step)
-        for h in range(2):
-            part = wide_ref[h, lines].astype(bf16).reshape(step, ROWS, HALF)
-            out_ref[here, :, h * HALF : (h + 1) * HALF] = part
-        copy = pltpu.make_async_copy(out_ref.at[here], out_hbm.at[here], sems.at[1 + i])
-        copy.start()
-        outgoing.append(copy)
-    for copy in outgoing:
-        copy.wait()
+    few = step // SENDS
+
+    def taken(ref, i, first_of):
+        starts = [b * SIZE + i * step for b in range(first_of, first_of + TOGETHER)]
+        return jnp.concatenate([ref[pl.ds(start, step)] for start in starts], axis=0)
+
+    def whole(i, first_of):
+        hi, flat = taken(hi_ref, i, first_of), taken(block_ref, i, first_of)
+        rows = jnp.concatenate([hi, taken(lo_ref, i, first_of), hi, flat, flat], axis=1)
+        return mm(rows, map_ref[: 5 * SIZE])
+
+    def close(i, first_of):
+        hi, flat = taken(hi_ref, i, first_of), taken(block_ref, i, first_of)
+        value = mm(jnp.concatenate([flat, flat, hi], axis=1), map_ref[3 * SIZE :])
+        return value + scale_ref[...] * (hi.astype(f32) + taken(lo_ref, i, first_of).astype(f32))
+
+    def emit(product):
+        for i in range(PARTS):
+            for first_of in range(0, ROWS, TOGETHER):
+                value = product(i, first_of)
+                for k in range(TOGETHER):
+                    for h in range(2):
+                        lines = pl.ds(i * step * ROWS + first_of + k, step, stride=ROWS)
+                        wide_ref[h, lines, :] = value[k * step : (k + 1) * step, h * HALF : (h + 1) * HALF]
+            for k in range(i * SENDS, (i + 1) * SENDS):
+                here = pl.ds(k * few, few)
+                for h in range(2):
+                    part = wide_ref[h, pl.ds(k * few * ROWS, few * ROWS)].astype(bf16)
+                    out_ref[here, :, h * HALF : (h + 1) * HALF] = part.reshape(few, ROWS, HALF)
+                copy(k).start()
+
+    def copy(k):
+        here = pl.ds(k * few, few)
+        return pltpu.make_async_copy(out_ref.at[here], out_hbm.at[here], sems.at[2 + k])
+
+    pl.when(near_one)(lambda: emit(close))
+    pl.when(jnp.logical_not(near_one))(lambda: emit(whole))
+    for k in range(PARTS * SENDS):
+        copy(k).wait()
+    outgoing.wait()
 
 
 def exchange(x, axis, groups=None):
@@ -436,12 +464,13 @@
         "final",
         [pltpu.HBM((SIZE, SIZE), f32), pltpu.HBM((SIZE, ROWS, SIZE), bf16)],
         scratch=[
-            pltpu.VMEM((5 * SIZE, SIZE), bf16),
+            pltpu.VMEM((6 * SIZE, SIZE), bf16),
             pltpu.VMEM((SIZE, SIZE), f32),
             pltpu.VMEM((FLAT, SIZE), bf16),
+            pltpu.VMEM((1, SIZE), f32),
             pltpu.VMEM((2, FLAT, HALF), f32),
             pltpu.VMEM((SIZE, ROWS, SIZE), bf16),
-            pltpu.SemaphoreType.DMA((2 + PARTS,)),
+            pltpu.SemaphoreType.DMA((2 + PARTS * SENDS,)),
         ],
         in_specs=[vmem] * 6 + [any_place],
         out_specs=[any_place] * 2,

time: 126 us -> 126 us (level)
  the two profiles are of different devices: /device:TPU:64 before, /device:TPU:2 now
where the time goes in v6:
time: 126 us; the launch traced here: 124 us
  blocking collectives  51.2 us (41%)
  starting transfers between devices  40.7 us (32%)
  Pallas kernels  27.5 us (22%)
  waiting for transfers between devices  3.89 us (3%)
    all_to_all x3, blocking collectives, exchange(): return lax.all_to_all(x, axis, 0, 0, axis_index_groups=groups, tiled=True)  51.2 us
    ppermute x4, starting transfers between devices, permuted(): lax.ppermute(x, axis, [(i, route(i)) for i in range(lax.axis_size(axis))])  20.9 us
    all_to_all x3, starting transfers between devices, exchange(): return lax.all_to_all(x, axis, 0, 0, axis_index_groups=groups, tiled=True)  19.8 us
    pallas_call x1, Pallas kernels, ascend(): call(ascend_kernel, 'ascend', [((WIDTH, 2, ROWS, SIZE), f32)], scratch=[p...  6.61 us
    pallas_call x1, Pallas kernels, final(): call(final_kernel, 'final', [pltpu.HBM((SIZE, SIZE), f32), pltpu.HBM((SIZ...  6.35 us
    pallas_call x1, Pallas kernels, gradient(): call(gradient_kernel, 'gradient', [pltpu.HBM((FLAT, SIZE), bf16), pltpu.H...  5.31 us
    pallas_call x1, Pallas kernels, prepare(): call(prepare_kernel, 'prepare', [pltpu.HBM((FLAT, SIZE), bf16), pltpu.HBM...  4.29 us
    all_to_all x3, waiting for transfers between devices, exchange(): return lax.all_to_all(x, axis, 0, 0, axis_index_groups=groups, tiled=True)  3.88 us
  transfers between devices with their start and end apart: 7, of which 2 were waited for; matrix products, arithmetic and copies ran while one was open for 0% of the time, Pallas kernels for 9%

profile of v6, /device:TPU:2, one launch (start us, length us, event | category | flops | bytes accessed | tf_op | source)
XLA Modules:
  0.0 124.4 jit_solution(1067695785356109278)
XLA Ops:
  0.6 0.0 copy-start.1
  0.6 0.0 copy-start
  0.6 6.6 %ascend.1.after_ref = f32[16,2,16,256]{3,2,1,0:T(8,128)} custom-call(bf16[256,16,256]{2,1,0:T(8,128)(2,1)} %bitcast.12, bf16[256,256]{1,0:T(8,128)(2,1)} %bitcast.19, bf16[256,256]{1,0:T(8,128)(2,1)} %bitcast.18), custom_call_target="tpu_custom_call" | custom-call | flops 3221225472 | bytes 4194304 | tf_op jit(solution)/shard_map/ascend/pallas_call | solution.py:373
  7.3 9.3 %all-to-all-start = ((f32[16,2,16,256]{3,2,1,0:T(8,128)}), f32[16,2,16,256]{3,2,1,0:T(8,128)S(1)}, u32[]{:S(2)}, u32[]{:S(2)}) async-start(f32[16,2,16,256]{3,2,1,0:T(8,128)} %ascend.1.after_ref), calls=%async_computation | async-start | bytes 1048576 | tf_op jit(solution)/shard_map/all_to_all | solution.py:360
  16.6 0.0 copy-done.1
  16.6 7.3 %collective-permute-start = (f32[16,256]{1,0:T(8,128)S(1)}, f32[16,256]{1,0:T(8,128)S(1)}, u32[]{:S(2)}, u32[]{:S(2)}) collective-permute-start(f32[16,256]{1,0:T(8,128)S(1)} %dynamic-slice_bitcast_fusion), channel_id=1, source_target_pairs={{0,128},{16,144},{32,160},{48,176},{64,192},{80,208},{96,224},{112... | collective-permute-start | bytes 49160 | tf_op jit(solution)/shard_map/ppermute | solution.py:364
  23.9 0.0 copy-done
  23.9 4.3 %prepare.1 = (bf16[4096,256]{1,0:T(8,128)(2,1)}, bf16[256,4096]{1,0:T(8,128)(2,1)}, f32[256,256]{1,0:T(8,128)S(1)}) custom-call(bf16[256,16,256]{2,1,0:T(8,128)(2,1)S(1)} %bitcast.13, f32[16,2,16,256]{3,2,1,0:T(8,128)} %ascend.1.after_ref), custom_call_target="tpu_custom_call" | custom-call | flops 536870912 | bytes 4194304 | tf_op jit(solution)/shard_map/prepare/pallas_call | solution.py:393
  28.2 0.0 collective-permute-done.also_ref.foreign_ref
  28.2 0.0 all-to-all-done.got_ref
  28.2 0.8 rounded.1
  29.0 7.2 %all-to-all-start.1 = ((bf16[16,2,16,256]{3,2,1,0:T(8,128)(2,1)}), bf16[16,2,16,256]{3,2,1,0:T(8,128)(2,1)S(1)}, u32[]{:S(2)}, u32[]{:S(2)}) async-start(bf16[16,2,16,256]{3,2,1,0:T(8,128)(2,1)} %rounded.1), calls=%async_computation.1 | async-start | bytes 524288 | tf_op jit(solution)/shard_map/all_to_all | solution.py:360
  36.2 3.8 %collective-permute-start.2 = (f32[256,256]{1,0:T(8,128)S(1)}, f32[256,256]{1,0:T(8,128)S(1)}, u32[]{:S(2)}, u32[]{:S(2)}) collective-permute-start(f32[256,256]{1,0:T(8,128)S(1)} %bitcast.14), channel_id=1, source_target_pairs={{0,32},{16,48},{32,0},{48,16},{64,96},{80,112},{96,64},{112,80},{1... | collective-permute-start | bytes 786440 | tf_op jit(solution)/shard_map/ppermute | solution.py:364
  40.0 3.5 %all-to-all-done.1.own_ref = bf16[16,2,16,256]{3,2,1,0:T(8,128)(2,1)S(1)} async-done(((bf16[16,2,16,256]{3,2,1,0:T(8,128)(2,1)}), bf16[16,2,16,256]{3,2,1,0:T(8,128)(2,1)S(1)}, u32[]{:S(2)}, u32[]{:S(2)}) %all-to-all-start.1) | async-done | bytes 262176 | tf_op jit(solution)/shard_map/all_to_all | solution.py:360
  43.5 1.9 %collective-permute-start.1 = (bf16[16,2,16,256]{3,2,1,0:T(8,128)(2,1)S(1)}, bf16[16,2,16,256]{3,2,1,0:T(8,128)(2,1)S(1)}, u32[]{:S(2)}, u32[]{:S(2)}) collective-permute-start(bf16[16,2,16,256]{3,2,1,0:T(8,128)(2,1)S(1)} %all-to-all-done.1.own_ref), channel_id=1, source_target_pairs={{0,16},{16,0},{32,48},{48,32},{64,80},{80,64},{96,112},{112,96},{1... | collective-permute-start | bytes 786440 | tf_op jit(solution)/shard_map/ppermute | solution.py:364
  45.4 7.9 %collective-permute-start.3 = (bf16[16,2,16,256]{3,2,1,0:T(8,128)(2,1)S(1)}, bf16[16,2,16,256]{3,2,1,0:T(8,128)(2,1)S(1)}, u32[]{:S(2)}, u32[]{:S(2)}) collective-permute-start(bf16[16,2,16,256]{3,2,1,0:T(8,128)(2,1)S(1)} %all-to-all-done.1.own_ref), channel_id=1, source_target_pairs={{0,496},{16,32},{32,16},{48,64},{64,48},{80,96},{96,80},{112,128},... | collective-permute-start | bytes 786440 | tf_op jit(solution)/shard_map/ppermute | solution.py:364
  53.4 0.1 pad_add_fusion.index_ref
  53.4 0.0 collective-permute-done.2.foreign_ref
  53.4 0.0 collective-permute-done.1.near_ref
  53.4 2.2 %first.1 = (f32[256,256]{1,0:T(8,128)}, f32[4,16,256]{2,1,0:T(8,128)}) custom-call(s32[4]{0:T(128)S(1)} %pad_add_fusion.index_ref, bf16[16,2,16,256]{3,2,1,0:T(8,128)(2,1)S(1)} %all-to-all-done.1.own_ref, bf16[16,2,16,256]{3,2,1,0:T(8,128)(2,1)S(1)} %collective-permute-done.1.near_ref, f32[256,256]{1,0:T(8,128)S(1)} %bitcast.15, ...), custom_call_target="tpu_custom_call" | custom-call | bytes 4194304 | tf_op jit(solution)/shard_map/first/pallas_call | solution.py:414
  55.6 3.3 %all-to-all-start.2 = ((f32[4,16,256]{2,1,0:T(8,128)}), f32[4,16,256]{2,1,0:T(8,128)S(1)}, u32[]{:S(2)}, u32[]{:S(2)}) async-start(f32[4,16,256]{2,1,0:T(8,128)} %get-tuple-element.17.after_ref), calls=%async_computation.2 | async-start | bytes 131072 | tf_op jit(solution)/shard_map/all_to_all | solution.py:360
  58.9 0.0 collective-permute-done.3.far_ref
  58.9 0.0 copy-done.2
  58.9 5.3 %gradient.1 = (bf16[4096,256]{1,0:T(8,128)(2,1)}, bf16[4096,256]{1,0:T(8,128)(2,1)}, bf16[16,40,256]{2,1,0:T(8,128)(2,1)S(1)}) custom-call(s32[4]{0:T(128)S(1)} %pad_add_fusion.index_ref, bf16[256,256]{1,0:T(8,128)(2,1)} %bitcast.20, bf16[16,2,16,256]{3,2,1,0:T(8,128)(2,1)} %copy-done.2, bf16[16,2,16,256]{3,2,1,0:T(8,128)(2,1)S(1)} %collective-permute-done.3.far_ref, ...), custom_call_target="tpu_custom_call" | custom-call | flops 2147483648 | bytes 4194304 | tf_op jit(solution)/shard_map/gradient/pallas_call | solution.py:422
  64.2 0.4 all-to-all-done.2.got_ref
  64.6 0.1 pack.1
  64.7 0.0 copy-start.3
  64.7 15.2 %all_to_all.30.got_ref = bf16[16,104,256]{2,1,0:T(8,128)(2,1)S(1)} all-to-all(bf16[16,104,256]{2,1,0:T(8,128)(2,1)S(1)} %pack.1), channel_id=1, replica_groups=mesh['blk'=32,'bond'=16] {'bond'}, dimensions={0} | all-to-all | bytes 1703936 | tf_op jit(solution)/shard_map/all_to_all | solution.py:360
  79.9 2.0 %second.1 = (f32[256,256]{1,0:T(8,128)S(1)}, f32[4,16,256]{2,1,0:T(8,128)S(1)}, bf16[32,256]{1,0:T(8,128)(2,1)S(1)}, f32[8,256]{1,0:T(8,128)S(1)}) custom-call(s32[4]{0:T(128)S(1)} %pad_add_fusion.index_ref, bf16[16,104,256]{2,1,0:T(8,128)(2,1)S(1)} %all_to_all.30.got_ref, f32[256,256]{1,0:T(8,128)} %get-tuple-element.21.old_ref, f32[256,256]{1,0:T(8,128)S(1)} %bitcast.16), custom_call_target="tpu_custom_call" | custom-call | bytes 4194304 | tf_op jit(solution)/shard_map/second/pallas_call | solution.py:450
  81.8 22.2 %all_to_all.31.got_ref = f32[4,16,256]{2,1,0:T(8,128)S(1)} all-to-all(f32[4,16,256]{2,1,0:T(8,128)S(1)} %get-tuple-element.22), channel_id=1, replica_groups={{0,128,256,384},{16,144,272,400},{32,160,288,416},{48,176,304,432},{64,..., dimensions={0} | all-to-all | bytes 131072 | tf_op jit(solution)/shard_map/all_to_all | solution.py:360
  104.1 13.8 %all_to_all.32.got_ref = bf16[16,64,256]{2,1,0:T(8,128)(2,1)S(1)} all-to-all(bf16[16,64,256]{2,1,0:T(8,128)(2,1)S(1)} %repeat.1), channel_id=1, replica_groups=mesh['blk'=32,'bond'=16] {'bond'}, dimensions={0} | all-to-all | bytes 1048576 | tf_op jit(solution)/shard_map/all_to_all | solution.py:360
  117.9 6.3 %final.1 = (f32[256,256]{1,0:T(8,128)}, bf16[256,16,256]{2,1,0:T(8,128)(2,1)}) custom-call(bf16[16,64,256]{2,1,0:T(8,128)(2,1)S(1)} %all_to_all.32.got_ref, f32[8,256]{1,0:T(8,128)S(1)} %get-tuple-element.24.extra_ref, f32[256,256]{1,0:T(8,128)S(1)} %get-tuple-element.25.old_ref, f32[256,256]{1,0:T(8,128)S(1)} %bitcast.17, bf16[4096,256]{1,0:T(8,128)(2,1)S(1)} %copy-done.3, ...), custom_call_target="tpu_custom_call" | custom-call | flops 2684354560 | bytes 4194304 | tf_op jit(solution)/shard_map/final/pallas_call | solution.py:462
  (6 shorter events, 0.1 us)
Async XLA Ops:
  0.6 15.9 %copy-start.1 = (f32[1,256,256]{2,1,0:T(8,128)S(1)}, f32[1,256,256]{2,1,0:T(8,128)}, u32[]{:S(2)}) copy-start(f32[1,256,256]{2,1,0:T(8,128)} %param.7) | copy-start | bytes 786436
  0.6 23.2 %copy-start = (bf16[1,256,16,256]{3,2,1,0:T(8,128)(2,1)S(1)}, bf16[1,256,16,256]{3,2,1,0:T(8,128)(2,1)}, u32[]{:S(2)}) copy-start(bf16[1,256,16,256]{3,2,1,0:T(8,128)(2,1)} %param.4) | copy-start | bytes 6291460
  7.3 20.9 %all-to-all-start = ((f32[16,2,16,256]{3,2,1,0:T(8,128)}), f32[16,2,16,256]{3,2,1,0:T(8,128)S(1)}, u32[]{:S(2)}, u32[]{:S(2)}) async-start(f32[16,2,16,256]{3,2,1,0:T(8,128)} %ascend.1.after_ref), calls=%async_computation | async-start | bytes 1048576 | tf_op jit(solution)/shard_map/all_to_all | solution.py:360
  16.6 11.6 %collective-permute-start = (f32[16,256]{1,0:T(8,128)S(1)}, f32[16,256]{1,0:T(8,128)S(1)}, u32[]{:S(2)}, u32[]{:S(2)}) collective-permute-start(f32[16,256]{1,0:T(8,128)S(1)} %dynamic-slice_bitcast_fusion), channel_id=1, source_target_pairs={{0,128},{16,144},{32,160},{48,176},{64,192},{80,208},{96,224},{112... | collective-permute-start | bytes 49160 | tf_op jit(solution)/shard_map/ppermute | solution.py:364
  29.0 14.6 %all-to-all-start.1 = ((bf16[16,2,16,256]{3,2,1,0:T(8,128)(2,1)}), bf16[16,2,16,256]{3,2,1,0:T(8,128)(2,1)S(1)}, u32[]{:S(2)}, u32[]{:S(2)}) async-start(bf16[16,2,16,256]{3,2,1,0:T(8,128)(2,1)} %rounded.1), calls=%async_computation.1 | async-start | bytes 524288 | tf_op jit(solution)/shard_map/all_to_all | solution.py:360
  36.2 17.3 %collective-permute-start.2 = (f32[256,256]{1,0:T(8,128)S(1)}, f32[256,256]{1,0:T(8,128)S(1)}, u32[]{:S(2)}, u32[]{:S(2)}) collective-permute-start(f32[256,256]{1,0:T(8,128)S(1)} %bitcast.14), channel_id=1, source_target_pairs={{0,32},{16,48},{32,0},{48,16},{64,96},{80,112},{96,64},{112,80},{1... | collective-permute-start | bytes 786440 | tf_op jit(solution)/shard_map/ppermute | solution.py:364
  43.5 9.9 %collective-permute-start.1 = (bf16[16,2,16,256]{3,2,1,0:T(8,128)(2,1)S(1)}, bf16[16,2,16,256]{3,2,1,0:T(8,128)(2,1)S(1)}, u32[]{:S(2)}, u32[]{:S(2)}) collective-permute-start(bf16[16,2,16,256]{3,2,1,0:T(8,128)(2,1)S(1)} %all-to-all-done.1.own_ref), channel_id=1, source_target_pairs={{0,16},{16,0},{32,48},{48,32},{64,80},{80,64},{96,112},{112,96},{1... | collective-permute-start | bytes 786440 | tf_op jit(solution)/shard_map/ppermute | solution.py:364
  45.4 13.5 %collective-permute-start.3 = (bf16[16,2,16,256]{3,2,1,0:T(8,128)(2,1)S(1)}, bf16[16,2,16,256]{3,2,1,0:T(8,128)(2,1)S(1)}, u32[]{:S(2)}, u32[]{:S(2)}) collective-permute-start(bf16[16,2,16,256]{3,2,1,0:T(8,128)(2,1)S(1)} %all-to-all-done.1.own_ref), channel_id=1, source_target_pairs={{0,496},{16,32},{32,16},{48,64},{64,48},{80,96},{96,80},{112,128},... | collective-permute-start | bytes 786440 | tf_op jit(solution)/shard_map/ppermute | solution.py:364
  53.4 5.5 %copy-start.2 = (bf16[16,2,16,256]{3,2,1,0:T(8,128)(2,1)}, bf16[16,2,16,256]{3,2,1,0:T(8,128)(2,1)S(1)}, u32[]{:S(2)}) copy-start(bf16[16,2,16,256]{3,2,1,0:T(8,128)(2,1)S(1)} %collective-permute-done.1.near_ref) | copy-start | bytes 786436
  55.6 9.0 %all-to-all-start.2 = ((f32[4,16,256]{2,1,0:T(8,128)}), f32[4,16,256]{2,1,0:T(8,128)S(1)}, u32[]{:S(2)}, u32[]{:S(2)}) async-start(f32[4,16,256]{2,1,0:T(8,128)} %get-tuple-element.17.after_ref), calls=%async_computation.2 | async-start | bytes 131072 | tf_op jit(solution)/shard_map/all_to_all | solution.py:360
  64.7 53.2 %copy-start.3 = (bf16[4096,256]{1,0:T(8,128)(2,1)S(1)}, bf16[4096,256]{1,0:T(8,128)(2,1)}, u32[]{:S(2)}) copy-start(bf16[4096,256]{1,0:T(8,128)(2,1)} %get-tuple-element.26.hi_ref) | copy-start | bytes 6291460
  64.7 53.2 %copy-start.4 = (bf16[4096,256]{1,0:T(8,128)(2,1)S(1)}, bf16[4096,256]{1,0:T(8,128)(2,1)}, u32[]{:S(2)}) copy-start(bf16[4096,256]{1,0:T(8,128)(2,1)} %get-tuple-element.27.lo_ref) | copy-start | bytes 6291460

commit v7 on v6

--- a/solution.py
+++ b/solution.py
@@ -15,7 +15,7 @@
 FLAT = SIZE * ROWS
 HALF = 128
 CHUNKS = 4
-EXTRA = 8
+EXTRA = 16
 PARTS = 2
 TOGETHER = 8
 SENDS = 4

time: 126 us -> 126 us (level)
  the two profiles are of different devices: /device:TPU:2 before, /device:TPU:64 now
where the time goes in v7:
time: 126 us
  blocking collectives  51.8 us (41%)
  starting transfers between devices  39.9 us (32%)
  Pallas kernels  28.4 us (23%)
  waiting for transfers between devices  4.88 us (4%)
    all_to_all x3, blocking collectives, exchange(): return lax.all_to_all(x, axis, 0, 0, axis_index_groups=groups, tiled=True)  51.8 us
    all_to_all x3, starting transfers between devices, exchange(): return lax.all_to_all(x, axis, 0, 0, axis_index_groups=groups, tiled=True)  22.9 us
    ppermute x4, starting transfers between devices, permuted(): lax.ppermute(x, axis, [(i, route(i)) for i in range(lax.axis_size(axis))])  16.9 us
    pallas_call x1, Pallas kernels, final(): call(final_kernel, 'final', [pltpu.HBM((SIZE, SIZE), f32), pltpu.HBM((SIZ...  7.22 us
    pallas_call x1, Pallas kernels, ascend(): call(ascend_kernel, 'ascend', [((WIDTH, 2, ROWS, SIZE), f32)], scratch=[p...  6.61 us
    pallas_call x1, Pallas kernels, gradient(): call(gradient_kernel, 'gradient', [pltpu.HBM((FLAT, SIZE), bf16), pltpu.H...  5.31 us
    all_to_all x3, waiting for transfers between devices, exchange(): return lax.all_to_all(x, axis, 0, 0, axis_index_groups=groups, tiled=True)  4.87 us
    pallas_call x1, Pallas kernels, prepare(): call(prepare_kernel, 'prepare', [pltpu.HBM((FLAT, SIZE), bf16), pltpu.HBM...  4.29 us
  transfers between devices with their start and end apart: 7, of which 1 were waited for; matrix products, arithmetic and copies ran while one was open for 0% of the time, Pallas kernels for 9%

profile of v7, /device:TPU:64, one launch (start us, length us, event | category | flops | bytes accessed | tf_op | source)
XLA Modules:
  0.0 126.1 jit_solution(7478981289397739232)
XLA Ops:
  0.6 0.0 copy-start.1
  0.6 0.0 copy-start
  0.6 6.6 %ascend.1.after_ref = f32[16,2,16,256]{3,2,1,0:T(8,128)} custom-call(bf16[256,16,256]{2,1,0:T(8,128)(2,1)} %bitcast.12, bf16[256,256]{1,0:T(8,128)(2,1)} %bitcast.19, bf16[256,256]{1,0:T(8,128)(2,1)} %bitcast.18), custom_call_target="tpu_custom_call" | custom-call | flops 3221225472 | bytes 4194304 | tf_op jit(solution)/shard_map/ascend/pallas_call | solution.py:373
  7.3 7.1 %all-to-all-start = ((f32[16,2,16,256]{3,2,1,0:T(8,128)}), f32[16,2,16,256]{3,2,1,0:T(8,128)S(1)}, u32[]{:S(2)}, u32[]{:S(2)}) async-start(f32[16,2,16,256]{3,2,1,0:T(8,128)} %ascend.1.after_ref), calls=%async_computation | async-start | bytes 1048576 | tf_op jit(solution)/shard_map/all_to_all | solution.py:360
  14.3 0.0 copy-done.1
  14.4 9.1 %collective-permute-start = (f32[16,256]{1,0:T(8,128)S(1)}, f32[16,256]{1,0:T(8,128)S(1)}, u32[]{:S(2)}, u32[]{:S(2)}) collective-permute-start(f32[16,256]{1,0:T(8,128)S(1)} %dynamic-slice_bitcast_fusion), channel_id=1, source_target_pairs={{0,128},{16,144},{32,160},{48,176},{64,192},{80,208},{96,224},{112... | collective-permute-start | bytes 49160 | tf_op jit(solution)/shard_map/ppermute | solution.py:364
  23.5 0.0 copy-done
  23.5 4.3 %prepare.1 = (bf16[4096,256]{1,0:T(8,128)(2,1)}, bf16[256,4096]{1,0:T(8,128)(2,1)}, f32[256,256]{1,0:T(8,128)S(1)}) custom-call(bf16[256,16,256]{2,1,0:T(8,128)(2,1)S(1)} %bitcast.13, f32[16,2,16,256]{3,2,1,0:T(8,128)} %ascend.1.after_ref), custom_call_target="tpu_custom_call" | custom-call | flops 536870912 | bytes 4194304 | tf_op jit(solution)/shard_map/prepare/pallas_call | solution.py:393
  27.8 0.0 collective-permute-done.also_ref.foreign_ref
  27.8 0.0 all-to-all-done.got_ref
  27.8 0.8 rounded.1
  28.5 7.2 %all-to-all-start.1 = ((bf16[16,2,16,256]{3,2,1,0:T(8,128)(2,1)}), bf16[16,2,16,256]{3,2,1,0:T(8,128)(2,1)S(1)}, u32[]{:S(2)}, u32[]{:S(2)}) async-start(bf16[16,2,16,256]{3,2,1,0:T(8,128)(2,1)} %rounded.1), calls=%async_computation.1 | async-start | bytes 524288 | tf_op jit(solution)/shard_map/all_to_all | solution.py:360
  35.8 3.8 %collective-permute-start.2 = (f32[256,256]{1,0:T(8,128)S(1)}, f32[256,256]{1,0:T(8,128)S(1)}, u32[]{:S(2)}, u32[]{:S(2)}) collective-permute-start(f32[256,256]{1,0:T(8,128)S(1)} %bitcast.14), channel_id=1, source_target_pairs={{0,32},{16,48},{32,0},{48,16},{64,96},{80,112},{96,64},{112,80},{1... | collective-permute-start | bytes 786440 | tf_op jit(solution)/shard_map/ppermute | solution.py:364
  39.6 4.9 %all-to-all-done.1.own_ref = bf16[16,2,16,256]{3,2,1,0:T(8,128)(2,1)S(1)} async-done(((bf16[16,2,16,256]{3,2,1,0:T(8,128)(2,1)}), bf16[16,2,16,256]{3,2,1,0:T(8,128)(2,1)S(1)}, u32[]{:S(2)}, u32[]{:S(2)}) %all-to-all-start.1) | async-done | bytes 262176 | tf_op jit(solution)/shard_map/all_to_all | solution.py:360
  44.4 1.9 %collective-permute-start.1 = (bf16[16,2,16,256]{3,2,1,0:T(8,128)(2,1)S(1)}, bf16[16,2,16,256]{3,2,1,0:T(8,128)(2,1)S(1)}, u32[]{:S(2)}, u32[]{:S(2)}) collective-permute-start(bf16[16,2,16,256]{3,2,1,0:T(8,128)(2,1)S(1)} %all-to-all-done.1.own_ref), channel_id=1, source_target_pairs={{0,16},{16,0},{32,48},{48,32},{64,80},{80,64},{96,112},{112,96},{1... | collective-permute-start | bytes 786440 | tf_op jit(solution)/shard_map/ppermute | solution.py:364
  46.4 2.1 %collective-permute-start.3 = (bf16[16,2,16,256]{3,2,1,0:T(8,128)(2,1)S(1)}, bf16[16,2,16,256]{3,2,1,0:T(8,128)(2,1)S(1)}, u32[]{:S(2)}, u32[]{:S(2)}) collective-permute-start(bf16[16,2,16,256]{3,2,1,0:T(8,128)(2,1)S(1)} %all-to-all-done.1.own_ref), channel_id=1, source_target_pairs={{0,496},{16,32},{32,16},{48,64},{64,48},{80,96},{96,80},{112,128},... | collective-permute-start | bytes 786440 | tf_op jit(solution)/shard_map/ppermute | solution.py:364
  48.5 0.1 pad_add_fusion.index_ref
  48.6 0.0 collective-permute-done.2.foreign_ref
  48.6 0.0 collective-permute-done.1.near_ref
  48.6 2.2 %first.1 = (f32[256,256]{1,0:T(8,128)}, f32[4,16,256]{2,1,0:T(8,128)}) custom-call(s32[4]{0:T(128)S(1)} %pad_add_fusion.index_ref, bf16[16,2,16,256]{3,2,1,0:T(8,128)(2,1)S(1)} %all-to-all-done.1.own_ref, bf16[16,2,16,256]{3,2,1,0:T(8,128)(2,1)S(1)} %collective-permute-done.1.near_ref, f32[256,256]{1,0:T(8,128)S(1)} %bitcast.15, ...), custom_call_target="tpu_custom_call" | custom-call | bytes 4194304 | tf_op jit(solution)/shard_map/first/pallas_call | solution.py:414
  50.8 8.7 %all-to-all-start.2 = ((f32[4,16,256]{2,1,0:T(8,128)}), f32[4,16,256]{2,1,0:T(8,128)S(1)}, u32[]{:S(2)}, u32[]{:S(2)}) async-start(f32[4,16,256]{2,1,0:T(8,128)} %get-tuple-element.17.after_ref), calls=%async_computation.2 | async-start | bytes 131072 | tf_op jit(solution)/shard_map/all_to_all | solution.py:360
  59.5 0.0 collective-permute-done.3.far_ref
  59.5 0.0 copy-done.2
  59.5 5.3 %gradient.1 = (bf16[4096,256]{1,0:T(8,128)(2,1)}, bf16[4096,256]{1,0:T(8,128)(2,1)}, bf16[16,48,256]{2,1,0:T(8,128)(2,1)S(1)}) custom-call(s32[4]{0:T(128)S(1)} %pad_add_fusion.index_ref, bf16[256,256]{1,0:T(8,128)(2,1)} %bitcast.20, bf16[16,2,16,256]{3,2,1,0:T(8,128)(2,1)} %copy-done.2, bf16[16,2,16,256]{3,2,1,0:T(8,128)(2,1)S(1)} %collective-permute-done.3.far_ref, ...), custom_call_target="tpu_custom_call" | custom-call | flops 2147483648 | bytes 4194304 | tf_op jit(solution)/shard_map/gradient/pallas_call | solution.py:422
  64.8 0.0 all-to-all-done.2.got_ref
  64.8 0.1 pack.1
  64.9 16.0 %all_to_all.30.got_ref = bf16[16,112,256]{2,1,0:T(8,128)(2,1)S(1)} all-to-all(bf16[16,112,256]{2,1,0:T(8,128)(2,1)S(1)} %pack.1), channel_id=1, replica_groups=mesh['blk'=32,'bond'=16] {'bond'}, dimensions={0} | all-to-all | bytes 1835008 | tf_op jit(solution)/shard_map/all_to_all | solution.py:360
  80.8 2.0 %second.1 = (f32[256,256]{1,0:T(8,128)S(1)}, f32[4,16,256]{2,1,0:T(8,128)S(1)}, bf16[32,256]{1,0:T(8,128)(2,1)S(1)}, f32[16,256]{1,0:T(8,128)S(1)}) custom-call(s32[4]{0:T(128)S(1)} %pad_add_fusion.index_ref, bf16[16,112,256]{2,1,0:T(8,128)(2,1)S(1)} %all_to_all.30.got_ref, f32[256,256]{1,0:T(8,128)} %get-tuple-element.21.old_ref, f32[256,256]{1,0:T(8,128)S(1)} %bitcast.16), custom_call_target="tpu_custom_call" | custom-call | bytes 4194304 | tf_op jit(solution)/shard_map/second/pallas_call | solution.py:450
  82.8 22.4 %all_to_all.31.got_ref = f32[4,16,256]{2,1,0:T(8,128)S(1)} all-to-all(f32[4,16,256]{2,1,0:T(8,128)S(1)} %get-tuple-element.22), channel_id=1, replica_groups={{0,128,256,384},{16,144,272,400},{32,160,288,416},{48,176,304,432},{64,..., dimensions={0} | all-to-all | bytes 131072 | tf_op jit(solution)/shard_map/all_to_all | solution.py:360
  105.3 13.4 %all_to_all.32.got_ref = bf16[16,64,256]{2,1,0:T(8,128)(2,1)S(1)} all-to-all(bf16[16,64,256]{2,1,0:T(8,128)(2,1)S(1)} %repeat.1), channel_id=1, replica_groups=mesh['blk'=32,'bond'=16] {'bond'}, dimensions={0} | all-to-all | bytes 1048576 | tf_op jit(solution)/shard_map/all_to_all | solution.py:360
  118.7 0.0 copy-done.3
  118.7 7.2 %final.1 = (f32[256,256]{1,0:T(8,128)}, bf16[256,16,256]{2,1,0:T(8,128)(2,1)}) custom-call(bf16[16,64,256]{2,1,0:T(8,128)(2,1)S(1)} %all_to_all.32.got_ref, f32[16,256]{1,0:T(8,128)S(1)} %get-tuple-element.24.extra_ref, f32[256,256]{1,0:T(8,128)S(1)} %get-tuple-element.25.old_ref, f32[256,256]{1,0:T(8,128)S(1)} %bitcast.17, bf16[4096,256]{1,0:T(8,128)(2,1)S(1)} %copy-done.3, ...), custom_call_target="tpu_custom_call" | custom-call | flops 2684354560 | bytes 4194304 | tf_op jit(solution)/shard_map/final/pallas_call | solution.py:462
  (6 shorter events, 0.1 us)
Async XLA Ops:
  0.6 13.7 %copy-start.1 = (f32[1,256,256]{2,1,0:T(8,128)S(1)}, f32[1,256,256]{2,1,0:T(8,128)}, u32[]{:S(2)}) copy-start(f32[1,256,256]{2,1,0:T(8,128)} %param.7) | copy-start | bytes 786436
  0.6 22.8 %copy-start = (bf16[1,256,16,256]{3,2,1,0:T(8,128)(2,1)S(1)}, bf16[1,256,16,256]{3,2,1,0:T(8,128)(2,1)}, u32[]{:S(2)}) copy-start(bf16[1,256,16,256]{3,2,1,0:T(8,128)(2,1)} %param.4) | copy-start | bytes 6291460
  7.3 20.5 %all-to-all-start = ((f32[16,2,16,256]{3,2,1,0:T(8,128)}), f32[16,2,16,256]{3,2,1,0:T(8,128)S(1)}, u32[]{:S(2)}, u32[]{:S(2)}) async-start(f32[16,2,16,256]{3,2,1,0:T(8,128)} %ascend.1.after_ref), calls=%async_computation | async-start | bytes 1048576 | tf_op jit(solution)/shard_map/all_to_all | solution.py:360
  14.4 13.4 %collective-permute-start = (f32[16,256]{1,0:T(8,128)S(1)}, f32[16,256]{1,0:T(8,128)S(1)}, u32[]{:S(2)}, u32[]{:S(2)}) collective-permute-start(f32[16,256]{1,0:T(8,128)S(1)} %dynamic-slice_bitcast_fusion), channel_id=1, source_target_pairs={{0,128},{16,144},{32,160},{48,176},{64,192},{80,208},{96,224},{112... | collective-permute-start | bytes 49160 | tf_op jit(solution)/shard_map/ppermute | solution.py:364
  28.5 15.9 %all-to-all-start.1 = ((bf16[16,2,16,256]{3,2,1,0:T(8,128)(2,1)}), bf16[16,2,16,256]{3,2,1,0:T(8,128)(2,1)S(1)}, u32[]{:S(2)}, u32[]{:S(2)}) async-start(bf16[16,2,16,256]{3,2,1,0:T(8,128)(2,1)} %rounded.1), calls=%async_computation.1 | async-start | bytes 524288 | tf_op jit(solution)/shard_map/all_to_all | solution.py:360
  35.8 12.9 %collective-permute-start.2 = (f32[256,256]{1,0:T(8,128)S(1)}, f32[256,256]{1,0:T(8,128)S(1)}, u32[]{:S(2)}, u32[]{:S(2)}) collective-permute-start(f32[256,256]{1,0:T(8,128)S(1)} %bitcast.14), channel_id=1, source_target_pairs={{0,32},{16,48},{32,0},{48,16},{64,96},{80,112},{96,64},{112,80},{1... | collective-permute-start | bytes 786440 | tf_op jit(solution)/shard_map/ppermute | solution.py:364
  44.4 4.2 %collective-permute-start.1 = (bf16[16,2,16,256]{3,2,1,0:T(8,128)(2,1)S(1)}, bf16[16,2,16,256]{3,2,1,0:T(8,128)(2,1)S(1)}, u32[]{:S(2)}, u32[]{:S(2)}) collective-permute-start(bf16[16,2,16,256]{3,2,1,0:T(8,128)(2,1)S(1)} %all-to-all-done.1.own_ref), channel_id=1, source_target_pairs={{0,16},{16,0},{32,48},{48,32},{64,80},{80,64},{96,112},{112,96},{1... | collective-permute-start | bytes 786440 | tf_op jit(solution)/shard_map/ppermute | solution.py:364
  46.4 13.1 %collective-permute-start.3 = (bf16[16,2,16,256]{3,2,1,0:T(8,128)(2,1)S(1)}, bf16[16,2,16,256]{3,2,1,0:T(8,128)(2,1)S(1)}, u32[]{:S(2)}, u32[]{:S(2)}) collective-permute-start(bf16[16,2,16,256]{3,2,1,0:T(8,128)(2,1)S(1)} %all-to-all-done.1.own_ref), channel_id=1, source_target_pairs={{0,496},{16,32},{32,16},{48,64},{64,48},{80,96},{96,80},{112,128},... | collective-permute-start | bytes 786440 | tf_op jit(solution)/shard_map/ppermute | solution.py:364
  48.6 10.8 %copy-start.2 = (bf16[16,2,16,256]{3,2,1,0:T(8,128)(2,1)}, bf16[16,2,16,256]{3,2,1,0:T(8,128)(2,1)S(1)}, u32[]{:S(2)}) copy-start(bf16[16,2,16,256]{3,2,1,0:T(8,128)(2,1)S(1)} %collective-permute-done.1.near_ref) | copy-start | bytes 786436
  50.8 14.0 %all-to-all-start.2 = ((f32[4,16,256]{2,1,0:T(8,128)}), f32[4,16,256]{2,1,0:T(8,128)S(1)}, u32[]{:S(2)}, u32[]{:S(2)}) async-start(f32[4,16,256]{2,1,0:T(8,128)} %get-tuple-element.17.after_ref), calls=%async_computation.2 | async-start | bytes 131072 | tf_op jit(solution)/shard_map/all_to_all | solution.py:360
  64.9 53.8 %copy-start.3 = (bf16[4096,256]{1,0:T(8,128)(2,1)S(1)}, bf16[4096,256]{1,0:T(8,128)(2,1)}, u32[]{:S(2)}) copy-start(bf16[4096,256]{1,0:T(8,128)(2,1)} %get-tuple-element.26.hi_ref) | copy-start | bytes 6291460
  64.9 53.8 %copy-start.4 = (bf16[4096,256]{1,0:T(8,128)(2,1)S(1)}, bf16[4096,256]{1,0:T(8,128)(2,1)}, u32[]{:S(2)}) copy-start(bf16[4096,256]{1,0:T(8,128)(2,1)} %get-tuple-element.27.lo_ref) | copy-start | bytes 6291460
